TPU v7x, 32 devices: a whole 2x2x4 slice. The times are simulated.
32 devices in a mesh: batch: 8 (over z, core), seq: 4 (over y, x).
Axes of the slice: x: 2, y: 2, z: 4, core: 2. Of those that a mesh axis runs over, the one named last changes fastest.
Arguments:
- tokens: bfloat16 [8, 1024, 2048], P('batch', 'seq'), may hold values from -6 to 6
- segments: int32 [8, 1024], P('batch', 'seq'), may hold values from 0 to 5, as said below
- positions: int32 [8, 1024], P('batch', 'seq'), may hold values from 0 to 1023, as said below
- cotangent: bfloat16 [8, 1024, 2048], P('batch', 'seq'), may hold values from -6 to 6
- ln_gain: bfloat16 [2048], P(('batch', 'seq')), may hold values from 0.099609375 to 1.8984375
- ln_bias: bfloat16 [2048], P(('batch', 'seq')), may hold values from -3 to 3
- in_weight: bfloat16 [2048, 14336], P(('batch', 'seq')), may hold values from -0.125 to 0.125
- in_bias: bfloat16 [14336], P(('batch', 'seq')), may hold values from -3 to 3
- proj_weight: bfloat16 [2048, 2048], P(('batch', 'seq')), may hold values from -0.5 to 0.5
- down_weight: bfloat16 [8192, 2048], P(('batch', 'seq')), may hold values from -0.09375 to 0.09375
- out_bias: bfloat16 [2048], P(('batch', 'seq')), may hold values from -3 to 3
Outputs:
- out: bfloat16 [8, 1024, 2048], P('batch', 'seq')
- grad_tokens: bfloat16 [8, 1024, 2048], P('batch', 'seq')
- grad_ln_gain: float32 [2048], P(('batch', 'seq'))
- grad_ln_bias: float32 [2048], P(('batch', 'seq'))
- grad_in_weight: float32 [2048, 14336], P(('batch', 'seq'))
- grad_in_bias: float32 [14336], P(('batch', 'seq'))
- grad_proj_weight: float32 [2048, 2048], P(('batch', 'seq'))
- grad_down_weight: float32 [8192, 2048], P(('batch', 'seq'))
- grad_out_bias: float32 [2048], P(('batch', 'seq'))
Inputs may be any that keep to these rules, and one draw needn't show every extreme that they name: `segments`: within each sequence the document numbers start at 0 and rise by one at each document's first token; every document holds 200 to 2000 tokens except the last, which the sequence's end may cut. `positions`: 0 at a document's first token, rising by one along the document.
All inputs are finite; a program needn't handle non-finite values.
Results may differ from a plain program's by a relative error of at most 0.0095.
Values may be sent and summed in bfloat16 or wider, within the bound.
No kernel may reach another device: no remote copies, remote signals or barrier semaphores. Data moves between devices by JAX's collectives and lax.ppermute only.
A program may use at most 448 MiB of HBM per device.

v0:
```python
import math

import jax
import jax.numpy as jnp
from jax import lax
from jax.sharding import PartitionSpec as P

HD = 64
ROT = 32


NEG_LARGE = -1e30
NORM_EPS = 1e-05


def rotary_tables(place, rot_dims):
    freq = 10000.0 ** (-(2.0 * jnp.arange(rot_dims // 2).astype(jnp.float32)) / rot_dims)
    theta = place.astype(jnp.float32)[:, None] * freq[None, :]
    return (jnp.cos(theta), jnp.sin(theta))


def rotate(field, cosine, sine):
    half = cosine.shape[1]
    first = field[:, :, :half]
    second = field[:, :, half : 2 * half]
    remain = field[:, :, 2 * half :]
    cos_rows = cosine[:, None, :]
    sin_rows = sine[:, None, :]
    return jnp.concatenate(
        [first * cos_rows - second * sin_rows, second * cos_rows + first * sin_rows, remain], axis=2
    )


def inner_rows(left, right):
    return lax.dot_general(
        left, right, (((0,), (0,)), ((), ())), preferred_element_type=jnp.float32
    )


def times_trans(left, right):
    return lax.dot_general(
        left, right, (((1,), (1,)), ((), ())), preferred_element_type=jnp.float32
    )


def gelu_tanh(value):
    return jax.nn.gelu(value, approximate=True)


def key_blocks(piece):
    total = piece[0].shape[0]
    size = math.gcd(total, 512)
    count = total // size
    split = tuple((member.reshape((count, size) + member.shape[1:]) for member in piece))
    starts = size * jnp.arange(count, dtype=jnp.int32)
    return split + (starts,)


def allowed_pairs(query_seg, query_index, seg_part, first, size):
    key_index = first + jnp.arange(size, dtype=jnp.int32)
    return (query_seg[:, None] == seg_part[None, :]) & (key_index[None, :] <= query_index[:, None])


def forward_fold(query, query_seg, query_index):
    scale = HD ** (-0.5)

    def fold(carry, piece, piece_start):

        def step(inner, item):
            run_max, run_sum, run_acc = inner
            keys_part, values_part, seg_part, first = item
            size = keys_part.shape[0]
            key_heads = keys_part.reshape(size, -1, HD)
            value_heads = values_part.reshape(size, -1, HD)
            scores = (
                jnp.einsum("qhd,khd->hqk", query, key_heads, preferred_element_type=jnp.float32)
                * scale
            )
            allowed = allowed_pairs(query_seg, query_index, seg_part, first, size)
            masked = jnp.where(allowed[None], scores, NEG_LARGE)
            new_max = jnp.maximum(run_max, jnp.max(masked, axis=2))
            weights = jnp.where(allowed[None], jnp.exp(masked - new_max[:, :, None]), 0.0)
            factor = jnp.exp(run_max - new_max)
            run_sum = run_sum * factor + jnp.sum(weights, axis=2)
            update = jnp.einsum(
                "hqk,khd->hqd",
                weights.astype(jnp.bfloat16),
                value_heads,
                preferred_element_type=jnp.float32,
            )
            run_acc = run_acc * factor[:, :, None] + update
            return ((new_max, run_sum, run_acc), None)

        carry, _ = lax.scan(step, carry, key_blocks(piece))
        return carry

    return fold


def backward_fold(query, query_seg, query_index, grad_heads, log_total, delta):
    scale = HD ** (-0.5)

    def fold(carry, piece, piece_start):

        def step(inner, item):
            grad_query, key_sums, value_sums = inner
            keys_part, values_part, seg_part, first = item
            size = keys_part.shape[0]
            key_heads = keys_part.reshape(size, -1, HD)
            value_heads = values_part.reshape(size, -1, HD)
            scores = (
                jnp.einsum("qhd,khd->hqk", query, key_heads, preferred_element_type=jnp.float32)
                * scale
            )
            allowed = allowed_pairs(query_seg, query_index, seg_part, first, size)
            probs = jnp.where(allowed[None], jnp.exp(scores - log_total[:, :, None]), 0.0)
            grad_probs = jnp.einsum(
                "qhd,khd->hqk", grad_heads, value_heads, preferred_element_type=jnp.float32
            )
            grad_scores = (probs * (grad_probs - delta[:, :, None])).astype(jnp.bfloat16)
            grad_query = (
                grad_query
                + jnp.einsum(
                    "hqk,khd->qhd", grad_scores, key_heads, preferred_element_type=jnp.float32
                )
                * scale
            )
            key_term = (
                jnp.einsum(
                    "hqk,qhd->khd", grad_scores, query, preferred_element_type=jnp.float32
                ).reshape(size, -1)
                * scale
            )
            value_term = jnp.einsum(
                "hqk,qhd->khd",
                probs.astype(jnp.bfloat16),
                grad_heads,
                preferred_element_type=jnp.float32,
            ).reshape(size, -1)
            key_sums = lax.dynamic_update_slice_in_dim(
                key_sums, lax.dynamic_slice_in_dim(key_sums, first, size, 0) + key_term, first, 0
            )
            value_sums = lax.dynamic_update_slice_in_dim(
                value_sums,
                lax.dynamic_slice_in_dim(value_sums, first, size, 0) + value_term,
                first,
                0,
            )
            return ((grad_query, key_sums, value_sums), None)

        carry, _ = lax.scan(step, carry, key_blocks(piece))
        return carry

    return fold


def shards(
    tokens,
    segments,
    positions,
    cotangent,
    ln_gain,
    ln_bias,
    in_weight,
    in_bias,
    proj_weight,
    down_weight,
    out_bias,
):
    rows = tokens.shape[1]
    width = tokens.shape[2]
    heads = width // HD
    inputs = tokens[0].astype(jnp.float32)
    seg_local = segments[0]
    pos_local = positions[0]
    grad_output = cotangent[0]
    query_index = lax.axis_index("seq") * rows + jnp.arange(rows, dtype=jnp.int32)
    gain_all, bias_all, in_all, in_bias_all, proj_all, down_all, out_bias_all = (
        lax.all_gather(ln_gain, ("batch", "seq"), axis=0, tiled=True),
        lax.all_gather(ln_bias, ("batch", "seq"), axis=0, tiled=True),
        lax.all_gather(in_weight, ("batch", "seq"), axis=0, tiled=True),
        lax.all_gather(in_bias, ("batch", "seq"), axis=0, tiled=True),
        lax.all_gather(proj_weight, ("batch", "seq"), axis=0, tiled=True),
        lax.all_gather(down_weight, ("batch", "seq"), axis=0, tiled=True),
        lax.all_gather(out_bias, ("batch", "seq"), axis=0, tiled=True),
    )
    centre = jnp.mean(inputs, axis=1, keepdims=True)
    centred = inputs - centre
    inv_std = lax.rsqrt(jnp.mean(centred * centred, axis=1, keepdims=True) + NORM_EPS)
    normal = centred * inv_std
    normed = (normal * gain_all.astype(jnp.float32) + bias_all.astype(jnp.float32)).astype(
        jnp.bfloat16
    )
    mixed = jnp.dot(normed, in_all, preferred_element_type=jnp.float32) + in_bias_all.astype(
        jnp.float32
    )
    cosine, sine = rotary_tables(pos_local, ROT)
    query = rotate(mixed[:, :width].reshape(rows, heads, HD), cosine, sine).astype(jnp.bfloat16)
    keys = (
        rotate(mixed[:, width : 2 * width].reshape(rows, heads, HD), cosine, sine)
        .astype(jnp.bfloat16)
        .reshape(rows, width)
    )
    values = mixed[:, 2 * width : 3 * width].astype(jnp.bfloat16)
    pre_act = mixed[:, 3 * width :]
    start_state = (
        jnp.full((heads, rows), NEG_LARGE, jnp.float32),
        jnp.zeros((heads, rows), jnp.float32),
        jnp.zeros((heads, rows, HD), jnp.float32),
    )
    folder = forward_fold(query, seg_local, query_index)
    run_max, run_sum, run_acc = folder(
        start_state,
        (
            lax.all_gather(keys, "seq", axis=0, tiled=True),
            lax.all_gather(values, "seq", axis=0, tiled=True),
            lax.all_gather(seg_local, "seq", axis=0, tiled=True),
        ),
        jnp.int32(0),
    )
    attended = jnp.transpose(run_acc / run_sum[:, :, None], (1, 0, 2))
    log_total = run_max + jnp.log(run_sum)
    attended_low = attended.reshape(rows, width).astype(jnp.bfloat16)
    activated = gelu_tanh(pre_act).astype(jnp.bfloat16)
    result = (
        inputs
        + jnp.dot(attended_low, proj_all, preferred_element_type=jnp.float32)
        + jnp.dot(activated, down_all, preferred_element_type=jnp.float32)
        + out_bias_all.astype(jnp.float32)
    )
    gain_back, in_back, proj_back, down_back = (
        lax.all_gather(ln_gain, ("batch", "seq"), axis=0, tiled=True),
        lax.all_gather(in_weight, ("batch", "seq"), axis=0, tiled=True),
        lax.all_gather(proj_weight, ("batch", "seq"), axis=0, tiled=True),
        lax.all_gather(down_weight, ("batch", "seq"), axis=0, tiled=True),
    )
    grad_float = grad_output.astype(jnp.float32)
    grad_out_bias = jnp.sum(grad_float, axis=0)
    grad_proj = inner_rows(attended_low, grad_output)
    grad_down = inner_rows(activated, grad_output)
    grad_proj, grad_down, grad_out_bias = (
        lax.psum_scatter(grad_proj, ("batch", "seq"), scatter_dimension=0, tiled=True),
        lax.psum_scatter(grad_down, ("batch", "seq"), scatter_dimension=0, tiled=True),
        lax.psum_scatter(grad_out_bias, ("batch", "seq"), scatter_dimension=0, tiled=True),
    )
    grad_attended = times_trans(grad_output, proj_back).astype(jnp.bfloat16)
    grad_act = times_trans(grad_output, down_back)
    gelu_value, gelu_pull = jax.vjp(gelu_tanh, pre_act)
    grad_pre = gelu_pull(grad_act)[0]
    grad_heads = grad_attended.reshape(rows, heads, HD)
    delta = jnp.einsum("qhd,qhd->hq", grad_heads.astype(jnp.float32), attended)
    back = backward_fold(query, seg_local, query_index, grad_heads, log_total, delta)
    length = rows * lax.axis_size("seq")
    back_state = (
        jnp.zeros((rows, heads, HD), jnp.float32),
        jnp.zeros((length, width), jnp.float32),
        jnp.zeros((length, width), jnp.float32),
    )
    grad_query, key_sums, value_sums = back(
        back_state,
        (
            lax.all_gather(keys, "seq", axis=0, tiled=True),
            lax.all_gather(values, "seq", axis=0, tiled=True),
            lax.all_gather(seg_local, "seq", axis=0, tiled=True),
        ),
        jnp.int32(0),
    )
    grad_keys, grad_values = (
        lax.psum_scatter(
            key_sums.astype(jnp.bfloat16), "seq", scatter_dimension=0, tiled=True
        ).astype(jnp.float32),
        lax.psum_scatter(
            value_sums.astype(jnp.bfloat16), "seq", scatter_dimension=0, tiled=True
        ).astype(jnp.float32),
    )
    grad_q = rotate(grad_query, cosine, -sine).reshape(rows, width)
    grad_k = rotate(grad_keys.reshape(rows, heads, HD), cosine, -sine).reshape(rows, width)
    grad_mixed = jnp.concatenate([grad_q, grad_k, grad_values, grad_pre], axis=1).astype(
        jnp.bfloat16
    )
    grad_in_bias = jnp.sum(grad_mixed.astype(jnp.float32), axis=0)
    grad_in = inner_rows(normed, grad_mixed)
    grad_normed = times_trans(grad_mixed, in_back)
    grad_gain = jnp.sum(grad_normed * normal, axis=0)
    grad_bias = jnp.sum(grad_normed, axis=0)
    scaled = grad_normed * gain_back.astype(jnp.float32)
    grad_inputs = grad_float + inv_std * (
        scaled
        - jnp.mean(scaled, axis=1, keepdims=True)
        - normal * jnp.mean(scaled * normal, axis=1, keepdims=True)
    )
    grad_gain, grad_bias, grad_in, grad_in_bias = (
        lax.psum_scatter(grad_gain, ("batch", "seq"), scatter_dimension=0, tiled=True),
        lax.psum_scatter(grad_bias, ("batch", "seq"), scatter_dimension=0, tiled=True),
        lax.psum_scatter(grad_in, ("batch", "seq"), scatter_dimension=0, tiled=True),
        lax.psum_scatter(grad_in_bias, ("batch", "seq"), scatter_dimension=0, tiled=True),
    )
    return (
        result.astype(jnp.bfloat16)[None],
        grad_inputs.astype(jnp.bfloat16)[None],
        grad_gain,
        grad_bias,
        grad_in,
        grad_in_bias,
        grad_proj,
        grad_down,
        grad_out_bias,
    )


def solution(mesh):
    placed = (
        P("batch", "seq", None),
        P("batch", "seq"),
        P("batch", "seq"),
        P("batch", "seq", None),
        P(("batch", "seq")),
        P(("batch", "seq")),
        P(("batch", "seq"), None),
        P(("batch", "seq")),
        P(("batch", "seq"), None),
        P(("batch", "seq"), None),
        P(("batch", "seq")),
    )
    return jax.shard_map(
        shards,
        mesh=mesh,
        in_specs=placed,
        out_specs=(
            P("batch", "seq", None),
            P("batch", "seq", None),
            P(("batch", "seq")),
            P(("batch", "seq")),
            P(("batch", "seq"), None),
            P(("batch", "seq")),
            P(("batch", "seq"), None),
            P(("batch", "seq"), None),
            P(("batch", "seq")),
        ),
        check_vma=False,
    )
```

profile of v0, /device:TPU:0, one launch (start us, length us, event | category | flops | bytes accessed | tf_op | source)
XLA Modules:
  0.0 5319.7 jit_solution(18244504491066278113)
XLA Ops:
  12.2 45.2 all-reduce.10
  61.9 268.7 %all-gather.7.cloned.1.call-done = bf16[2048,14336]{1,0:T(8,128)(2,1)} async-done(((bf16[64,14336]{1,0:T(8,128)(2,1)}), bf16[2048,14336]{1,0:T(8,128)(2,1)}) %all-gather.7.cloned.1.call-update) | async-done | bytes 58720272 | tf_op jit(solution)/shard_map/all_gather | solution.py:181
  330.6 30.5 convolution_add_fusion
  380.1 8.3 all-gather
  389.6 19.7 all-gather.13.cloned.1.call-done
  418.9 43.9 all-gather.9.cloned.1.call-done
  462.8 6.5 copy.57
  469.4 6.4 copy.59
  475.8 42.1 all-gather.11.cloned.1.call-done
  517.9 6.3 copy.60
  524.1 58.2 %while.30 = (s32[]{:T(128)}, f32[32,256]{1,0:T(8,128)S(1)}, f32[32,256]{1,0:T(8,128)S(1)}, f32[32,256,64]{1,2,0:T(8,128)}, s32[1,256]{1,0:T(1,128)S(1)}, /*index...) while((s32[]{:T(128)}, f32[32,256]{1,0:T(8,128)S(1)}, ...), condition=%wide.region_5.6_spmd.clone, body=%wide.region_2.5_spmd.clone.sunk | while | flops 1130275584 | bytes 136328400 | solution.py:94
  528.1 7.2 fusion.119
  535.4 8.4 fusion.120
  546.2 6.2 fusion.122
  556.4 7.7 fusion.119
  564.1 8.4 fusion.120
  574.9 7.4 fusion.122
  594.3 220.1 %while.31 = (s32[]{:T(128)}, f32[256,32,64]{0,2,1:T(8,128)}, f32[1024,2048]{0,1:T(8,128)}, f32[1024,2048]{1,0:T(8,128)}, bf16[2,512,2048]{1,2,0:T(8,128)(2,1)}, ...) while((s32[]{:T(128)}, f32[256,32,64]{0,2,1:T(8,128)}, ...), condition=%wide.region_7.8_spmd.clone, body=%wide.region_6.7_spmd.clone.sunk | while | flops 2731410176 | bytes 216511824 | solution.py:151
  597.3 8.1 fusion.133
  606.9 11.4 fusion.134
  618.3 8.7 bitcast_add_fusion.6
  634.0 7.1 bitcast_add_fusion.7
  641.1 20.7 dynamic_update_slice.10
  672.2 10.9 fusion.135
  683.1 6.5 bitcast_add_fusion.8
  695.0 11.9 dynamic_update_slice.11
  709.4 8.4 fusion.133
  719.3 10.6 fusion.134
  729.9 6.9 bitcast_add_fusion.6
  743.4 6.6 bitcast_add_fusion.7
  750.0 19.7 dynamic_update_slice.10
  780.1 10.9 fusion.135
  791.1 6.5 bitcast_add_fusion.8
  802.9 11.3 dynamic_update_slice.11
  820.5 6.1 convert_element_type.108
  826.7 21.7 fusion.33
  849.4 24.8 reduce-scatter.9.cloned.1.call-done
  881.3 48.8 reduce-scatter.11.cloned.1.call-done
  930.1 28.2 fusion.50
  967.0 8.2 fusion.57
  975.2 27.5 fusion.55
  1004.0 42.5 fusion.65
  1047.1 7.1 fusion.34
  1054.3 19.8 fusion.44
  1074.1 14.1 all-reduce.13.cloned.1.call-done
  1093.3 357.0 %reduce-scatter.13.cloned.1.call-done = f32[64,2048]{1,0:T(8,128)} async-done(((f32[2048,2048]{1,0:T(8,128)}), f32[64,2048]{1,0:T(8,128)}) %reduce-scatter.13.cloned.1.call-update) | async-done | bytes 524304 | tf_op jit(solution)/shard_map/reduce_scatter | solution.py:242
  1450.3 1408.5 %reduce-scatter.15.cloned.1.call-done = f32[256,2048]{1,0:T(8,128)} async-done(((f32[8192,2048]{1,0:T(8,128)}), f32[256,2048]{1,0:T(8,128)}) %reduce-scatter.15.cloned.1.call-update) | async-done | bytes 2097168 | tf_op jit(solution)/shard_map/reduce_scatter | solution.py:243
  2858.9 2454.0 %reduce-scatter.17.cloned.1.call-done = f32[64,14336]{1,0:T(8,128)} async-done(((f32[2048,14336]{1,0:T(8,128)}), f32[64,14336]{1,0:T(8,128)}) %reduce-scatter.17.cloned.1.call-update) | async-done | bytes 3670032
  (181 shorter events, 143.0 us)
Async XLA Ops:
  7.2 323.4 %all-gather.7.cloned.1.call-start = ((), (), s32[]{:S(2)}) async-start(), calls=%async_computation.5 | async-start | bytes 60555264 | tf_op jit(solution)/shard_map/all_gather | solution.py:181
  7.9 401.3 %all-gather.13.cloned.1.call-start = ((), (), s32[]{:S(2)}) async-start(), calls=%async_computation.8 | async-start | bytes 8650752 | tf_op jit(solution)/shard_map/all_gather | solution.py:183
  8.7 454.2 %all-gather.9.cloned.1.call-start = ((), (), s32[]{:S(2)}) async-start(), calls=%async_computation.6 | async-start | bytes 5242880 | tf_op jit(solution)/shard_map/all_gather | solution.py:215
  57.3 303.7 %copy-start.16 = (f32[2048]{0:T(1024)}, f32[2048]{0:T(1024)S(1)}, u32[]{:S(2)}) copy-start(f32[2048]{0:T(1024)S(1)} %convert_element_type.93) | copy-start | bytes 24580
  57.3 303.7 %copy-start.14 = (f32[2048]{0:T(1024)}, f32[2048]{0:T(1024)S(1)}, u32[]{:S(2)}) copy-start(f32[2048]{0:T(1024)S(1)} %convert_element_type.92) | copy-start | bytes 24580
  59.5 301.5 %copy-start.18 = (f32[256]{0:T(256)}, f32[256]{0:T(256)S(1)}, u32[]{:S(2)}) copy-start(f32[256]{0:T(256)S(1)} %broadcast_multiply_fusion.2) | copy-start | bytes 3076
  61.2 299.9 %copy-start.20 = (f32[256]{0:T(256)}, f32[256]{0:T(256)S(1)}, u32[]{:S(2)}) copy-start(f32[256]{0:T(256)S(1)} %add_rsqrt_fusion) | copy-start | bytes 3076
  61.9 309.9 %copy-start.22 = (f32[256,16]{0,1:T(8,128)}, f32[256,16]{0,1:T(8,128)S(1)}, u32[]{:S(2)}) copy-start(f32[256,16]{0,1:T(8,128)S(1)} %get-tuple-element.400) | copy-start | bytes 49156
  370.0 10.1 copy-start.24
  370.0 39.3 copy-start.6
  376.6 141.2 %all-gather.11.cloned.1.call-start = ((), (), s32[]{:S(2)}) async-start(), calls=%async_computation.7 | async-start | bytes 5242880 | tf_op jit(solution)/shard_map/all_gather | solution.py:216
  379.4 447.3 %all-gather.15.cloned.1.call-start = ((), (), s32[]{:S(2)}) async-start(), calls=%async_computation.9 | async-start | bytes 34603008 | tf_op jit(solution)/shard_map/all_gather | solution.py:184
  380.0 494.1 %reduce-scatter.9.cloned.1.call-start = ((), (), s32[]{:S(2)}) async-start(), calls=%async_computation.10 | async-start | bytes 5242880 | tf_op jit(solution)/shard_map/reduce_scatter | solution.py:269
  535.4 10.8 copy-start.1
  564.1 10.8 copy-start.1
  597.3 9.6 copy-start.11
  618.3 9.1 copy-start
  661.8 10.4 copy-start.12
  709.4 9.9 copy-start.11
  729.9 6.9 copy-start
  769.7 10.4 copy-start.12
  820.4 109.7 %reduce-scatter.11.cloned.1.call-start = ((), (), s32[]{:S(2)}) async-start(), calls=%async_computation.11 | async-start | bytes 5242880 | tf_op jit(solution)/shard_map/reduce_scatter | solution.py:272
  820.5 6.3 copy-start.7
  826.6 21.9 copy-start.2
  826.6 50.2 copy-start.23
  826.7 50.2 copy-start.25
  826.7 261.5 %all-reduce.13.cloned.1.call-start = ((), (), s32[]{:S(2)}) async-start(), calls=%async_computation.15 | async-start | bytes 163840
  874.1 3.1 copy-start.13
  874.1 56.0 %copy-start.3 = (bf16[1,256,2048]{2,1,0:T(8,128)(2,1)S(1)}, bf16[1,256,2048]{2,1,0:T(8,128)(2,1)}, u32[]{:S(2)}) copy-start(bf16[1,256,2048]{2,1,0:T(8,128)(2,1)} %param.15) | copy-start | bytes 3145732
  874.1 56.0 %copy-start.15 = (f32[2048]{0:T(1024)S(1)}, f32[2048]{0:T(1024)}, u32[]{:S(2)}) copy-start(f32[2048]{0:T(1024)} %copy-done.14) | copy-start | bytes 24580
  874.1 56.0 %copy-start.19 = (f32[256]{0:T(256)S(1)}, f32[256]{0:T(256)}, u32[]{:S(2)}) copy-start(f32[256]{0:T(256)} %copy-done.18) | copy-start | bytes 3076
  874.1 56.0 %copy-start.21 = (f32[256]{0:T(256)S(1)}, f32[256]{0:T(256)}, u32[]{:S(2)}) copy-start(f32[256]{0:T(256)} %copy-done.20) | copy-start | bytes 3076
  879.9 50.2 copy-start.9
  881.3 77.0 %copy-start.8 = (bf16[1,256,2048]{2,1,0:T(8,128)(2,1)S(1)}, bf16[1,256,2048]{2,1,0:T(8,128)(2,1)}, u32[]{:S(2)}) copy-start(bf16[1,256,2048]{2,1,0:T(8,128)(2,1)} %param.18) | copy-start | bytes 3145732
  958.3 4.5 copy-start.4
  958.3 8.7 copy-start.5
  966.7 483.6 %reduce-scatter.13.cloned.1.call-start = ((), (), s32[]{:S(2)}) async-start(), calls=%async_computation.12 | async-start | bytes 17301504 | tf_op jit(solution)/shard_map/reduce_scatter | solution.py:242
  975.2 1883.7 %reduce-scatter.15.cloned.1.call-start = ((), (), s32[]{:S(2)}) async-start(), calls=%async_computation.13 | async-start | bytes 69206016 | tf_op jit(solution)/shard_map/reduce_scatter | solution.py:243
  1002.8 1.2 copy-start.10
  1002.8 1.2 copy-start.17
  1002.8 4310.0 %reduce-scatter.17.cloned.1.call-start = ((), (), s32[]{:S(2)}) async-start(), calls=%async_computation.14 | async-start | bytes 121110528
  1046.5 0.7 copy-start.26
Sparse Core Ops, SparseCore 0:
  10.9 319.6 all-gather.6
  333.4 75.7 all-gather.12
  411.7 51.1 all-gather.8
  465.1 52.6 all-gather.10
  520.6 194.7 all-gather.14
  820.5 53.5 reduce-scatter.8
  877.4 52.6 reduce-scatter.10
  966.9 121.2 all-reduce.12
  1091.0 359.2 reduce-scatter.12
  1453.1 1405.7 reduce-scatter.14
  2861.8 2450.9 reduce-scatter.16
where the time goes:
time: 5330 us; the launch traced here: 5320 us
  waiting for transfers between devices  4680 us (88%)
  matrix products  305 us (6%)
  local copies, waits for them, and re-layouts  173 us (3%)
  other arithmetic  84.9 us (2%)
  blocking collectives  53.4 us (1%)
    unnamed x13, waiting for transfers between devices  2470 us
    reduce_scatter x1, waiting for transfers between devices, shards(): lax.psum_scatter(grad_down, ('batch', 'seq'), scatter_dimension=0, tiled=...  1410 us
    reduce_scatter x1, waiting for transfers between devices, shards(): lax.psum_scatter(grad_proj, ('batch', 'seq'), scatter_dimension=0, tiled=...  357 us
    all_gather x1, waiting for transfers between devices, shards(): lax.all_gather(in_weight, ('batch', 'seq'), axis=0, tiled=True)  269 us
  transfers between devices with their start and end apart: 11, of which 10 were waited for; matrix products, arithmetic and copies ran while one was open for 10% of the time, Pallas kernels for 0%

commit v1 on v0

v1 whole, which is shorter than its diff:
```python
import functools

import jax
import jax.numpy as jnp
from jax import lax
from jax.experimental import pallas as pl
from jax.experimental.pallas import tpu as pltpu
from jax.sharding import PartitionSpec as P

HD = 64
ROT = 32
NEG_LARGE = -1e30
NORM_EPS = 1e-05
CORES = 2
f32 = jnp.float32
bf16 = jnp.bfloat16
BOTH = ("batch", "seq")
NN = ((1,), (0,))
NT = ((1,), (1,))
TN = ((0,), (0,))


def dot(left, right, dims):
    return lax.dot_general(left, right, (dims, ((), ())), preferred_element_type=f32)


def swap_halves(x):
    width = x.shape[1]
    lane = lax.broadcasted_iota(jnp.int32, x.shape, 1) % HD
    return jnp.where(
        lane < ROT // 2, pltpu.roll(x, width - ROT // 2, 1), pltpu.roll(x, ROT // 2, 1)
    )


def attention_kernel(
    block, mixed_ref, grad_ref, cos_ref, sin_ref, start_ref, out_ref, dmixed_ref, q_s, k_s, v_s, o_s, dq_s, dk_s, dv_s
):
    head = pl.program_id(1)
    length, width = grad_ref.shape
    scale = HD**-0.5

    def wide(ref):
        table = ref[...]
        return jnp.concatenate([table] * (width // table.shape[1]), axis=1)

    @pl.when(head == 0)
    def _():
        cosine, sine = wide(cos_ref), wide(sin_ref)
        q = mixed_ref[:, 0:width]
        q_s[...] = ((q * cosine + swap_halves(q) * sine).astype(bf16) * scale).astype(bf16)
        k = mixed_ref[:, width : 2 * width]
        k_s[...] = (k * cosine + swap_halves(k) * sine).astype(bf16)
        v_s[...] = mixed_ref[:, 2 * width : 3 * width].astype(bf16)
        o_s[...] = jnp.zeros_like(o_s)
        dq_s[...] = jnp.zeros_like(dq_s)
        dk_s[...] = jnp.zeros_like(dk_s)
        dv_s[...] = jnp.zeros_like(dv_s)

    mine = lax.broadcasted_iota(jnp.int32, (1, width), 1) // HD == head
    zero = jnp.zeros((), bf16)
    for i in range(length // block):
        rows = pl.ds(i * block, block)
        reach = (i + 1) * block
        q = jnp.where(mine, q_s[rows, :], zero)
        grad = jnp.where(mine, grad_ref[rows, :], zero)
        k = k_s[0:reach, :]
        v = v_s[0:reach, :]
        scores = dot(q, k, NT)
        key_at = lax.broadcasted_iota(jnp.int32, (block, reach), 1)
        query_at = i * block + lax.broadcasted_iota(jnp.int32, (block, reach), 0)
        allowed = (key_at <= query_at) & (key_at >= start_ref[rows, :])
        scores = jnp.where(allowed, scores, NEG_LARGE)
        probs = jnp.exp(scores - jnp.max(scores, axis=1, keepdims=True))
        probs = probs * (1.0 / jnp.sum(probs, axis=1, keepdims=True))
        low = probs.astype(bf16)
        o_s[rows, :] = jnp.where(mine, dot(low, v, NN), o_s[rows, :])
        dprobs = dot(grad, v, NT)
        delta = jnp.sum(probs * dprobs, axis=1, keepdims=True)
        dscores = (probs * (dprobs - delta)).astype(bf16)
        dq_s[rows, :] = jnp.where(mine, dot(dscores, k, NN), dq_s[rows, :])
        dk_s[0:reach, :] += dot(dscores, q, TN)
        dv_s[0:reach, :] += dot(low, grad, TN)

    @pl.when(head == pl.num_programs(1) - 1)
    def _():
        cosine, sine = wide(cos_ref), wide(sin_ref)
        out_ref[...] = o_s[...].astype(bf16)
        dq = dq_s[...] * scale
        dmixed_ref[:, 0:width] = (dq * cosine - swap_halves(dq) * sine).astype(bf16)
        dk = dk_s[...]
        dmixed_ref[:, width : 2 * width] = (dk * cosine - swap_halves(dk) * sine).astype(bf16)
        dmixed_ref[:, 2 * width : 3 * width] = dv_s[...].astype(bf16)


def attention(mixed, grad, cosine, sine, start, length):
    tokens, width = grad.shape

    def rows(columns):
        return pl.BlockSpec((length, columns), lambda s, h: (s, 0))

    return pl.pallas_call(
        functools.partial(attention_kernel, min(256, length)),
        grid=(tokens // length, width // HD),
        in_specs=[rows(3 * width), rows(width), rows(cosine.shape[1]), rows(cosine.shape[1]), rows(1)],
        out_specs=[rows(width), rows(3 * width)],
        out_shape=[
            jax.ShapeDtypeStruct((tokens, width), bf16),
            jax.ShapeDtypeStruct((tokens, 3 * width), bf16),
        ],
        scratch_shapes=[pltpu.VMEM((length, width), bf16)] * 3 + [pltpu.VMEM((length, width), f32)] * 4,
        compiler_params=pltpu.CompilerParams(vmem_limit_bytes=48 * 1024 * 1024),
        cost_estimate=pl.CostEstimate(
            flops=40 * tokens * length * width, bytes_accessed=16 * tokens * width, transcendentals=0
        ),
    )(mixed, grad, cosine, sine, start)


def rotary_wide(place, width=128):
    lane = jnp.arange(width) % HD
    freq = 10000.0 ** (-(2.0 * (lane % (ROT // 2)).astype(f32)) / ROT)
    theta = place.astype(f32)[:, None] * freq[None, :]
    cosine = jnp.where(lane < ROT, jnp.cos(theta), 1.0)
    sine = jnp.sin(theta)
    sine = jnp.where(lane < ROT // 2, -sine, jnp.where(lane < ROT, sine, 0.0))
    return cosine, sine


def gelu_parts(u):
    a = (2.0 / jnp.pi) ** 0.5
    t = jnp.tanh(a * (u + 0.044715 * u * u * u))
    value = 0.5 * u * (1.0 + t)
    slope = 0.5 * (1.0 + t) + 0.5 * u * (1.0 - t * t) * a * (1.0 + 3 * 0.044715 * u * u)
    return value, slope


def build(n_batch, n_seq):
    ranks = CORES * n_seq
    planes = n_batch // CORES
    n_dev = n_batch * n_seq
    plane_groups = [[z * ranks + r for r in range(ranks)] for z in range(planes)]
    line_groups = [[z * CORES + c for z in range(planes)] for c in range(CORES)]

    def gather_plane(x):
        return lax.all_gather(x, BOTH, axis_index_groups=plane_groups, axis=0, tiled=True)

    def scatter_plane(x):
        return lax.psum_scatter(
            x, BOTH, axis_index_groups=plane_groups, scatter_dimension=0, tiled=True
        )

    def swap_plane(x):
        return lax.all_to_all(x, BOTH, 0, 0, axis_index_groups=plane_groups, tiled=True)

    def gather_line(x):
        return lax.all_gather(x, "batch", axis_index_groups=line_groups, axis=0, tiled=True)

    def scatter_line(x):
        return lax.psum_scatter(
            x, "batch", axis_index_groups=line_groups, scatter_dimension=0, tiled=True
        )

    def shards(
        tokens, segments, positions, cotangent, ln_gain, ln_bias, in_weight, in_bias, proj_weight, down_weight, out_bias
    ):
        rows, width = tokens.shape[1:]
        length = rows * n_seq
        in_rows, total = in_weight.shape
        proj_rows, down_rows = proj_weight.shape[0], down_weight.shape[0]
        hidden = total - 3 * width
        chunks = 2
        part = down_rows // chunks
        whole_heads = proj_rows % HD == 0
        head_groups = planes if whole_heads else 1
        head_cols = width // (head_groups * ranks)
        mine_cols = width // ranks
        index = lax.axis_index("batch") * n_seq + lax.axis_index("seq")
        rank = index % ranks

        small = jnp.concatenate([in_bias, ln_gain, ln_bias, out_bias])
        small_all = lax.all_to_all(
            jnp.broadcast_to(small[None], (n_dev, small.shape[0])), BOTH, 0, 0, tiled=True
        ).astype(f32)
        n_bias = in_bias.shape[0]
        n_width = ln_gain.shape[0]
        bias_all = small_all[:, :n_bias].reshape(-1)
        gain_all = small_all[:, n_bias : n_bias + n_width].reshape(-1)
        shift_all = small_all[:, n_bias + n_width : n_bias + 2 * n_width].reshape(-1)
        out_bias_all = small_all[:, n_bias + 2 * n_width :].reshape(-1)
        place = lax.all_to_all(
            jnp.broadcast_to(positions, (ranks, rows)), BOTH, 0, 0, axis_index_groups=plane_groups, tiled=True
        ).reshape(-1)

        def split_heads(x):
            lead = x.shape[0]
            x = x.reshape(lead, 3, head_groups, ranks, head_cols)
            return jnp.transpose(x, (3, 0, 1, 2, 4)).reshape(ranks, lead, 3 * mine_cols)

        def split_hidden(x, c):
            lead = x.shape[0]
            x = x.reshape(lead, planes, ranks, chunks, part)[:, :, :, c]
            return jnp.transpose(x, (2, 0, 1, 3)).reshape(ranks, lead, planes * part)

        def join_heads(x):
            lead = x.shape[1]
            x = x.reshape(ranks, lead, 3, head_groups, head_cols)
            return jnp.transpose(x, (1, 2, 3, 0, 4)).reshape(lead, 3 * width)

        def join_hidden(xs):
            lead = xs[0].shape[1]
            x = jnp.stack([x.reshape(ranks, lead, planes, part) for x in xs])
            return jnp.transpose(x, (2, 3, 1, 0, 4)).reshape(lead, hidden)

        bias_heads = lax.dynamic_index_in_dim(
            split_heads(bias_all[None, : 3 * width]), rank, 0, keepdims=False
        )
        bias_hidden = [
            lax.dynamic_index_in_dim(split_hidden(bias_all[None, 3 * width :], c), rank, 0, keepdims=False)
            for c in range(chunks)
        ]

        def in_columns(x):
            return gather_line(swap_plane(x).reshape(ranks * in_rows, x.shape[2]))

        down = [gather_line(down_weight[c * part : (c + 1) * part]) for c in range(chunks)]
        w_hidden = [in_columns(split_hidden(in_weight[:, 3 * width :], c)) for c in range(chunks)]
        w_heads = in_columns(split_heads(in_weight[:, : 3 * width]))
        if whole_heads:
            proj = gather_line(proj_weight)
        else:
            proj = lax.dynamic_slice_in_dim(
                lax.all_gather(proj_weight, BOTH, axis=0, tiled=True), rank * mine_cols, mine_cols, 0
            )

        token_all = gather_plane(tokens[0])
        grad_all = gather_plane(cotangent[0])

        wide = token_all.astype(f32)
        centred = wide - jnp.mean(wide, axis=1, keepdims=True)
        inv_std = lax.rsqrt(jnp.mean(centred * centred, axis=1, keepdims=True) + NORM_EPS)
        normed = (centred * inv_std * gain_all + shift_all).astype(bf16)

        activated, grad_u, grad_down, grad_hidden = [], [], [], []
        for c in range(chunks):
            u = dot(normed, w_hidden[c], NN) + bias_hidden[c]
            value, slope = gelu_parts(u)
            act = value.astype(bf16)
            du = (dot(grad_all, down[c], NT) * slope).astype(bf16)
            activated.append(act)
            grad_u.append(du)
            grad_down.append(scatter_line(dot(act, grad_all, TN).astype(bf16)))
            grad_hidden.append(scatter_line(dot(normed, du, TN).astype(bf16)))

        mixed = dot(normed, w_heads, NN) + bias_heads
        grad_attended = dot(grad_all, proj, NT).astype(bf16)
        cosine, sine = rotary_wide(place)
        start = (jnp.arange(place.shape[0], dtype=jnp.int32) % length - place)[:, None]
        attended, grad_mixed = attention(mixed, grad_attended, cosine, sine, start, length)
        grad_proj = dot(attended, grad_all, TN).astype(bf16)
        if whole_heads:
            grad_proj = scatter_line(grad_proj).astype(f32)
        else:
            grad_proj = lax.psum_scatter(
                lax.dynamic_update_slice_in_dim(
                    jnp.zeros((width, width), f32), grad_proj.astype(f32), rank * mine_cols, 0
                ),
                BOTH, scatter_dimension=0, tiled=True,
            )
        grad_heads = scatter_line(dot(normed, grad_mixed, TN).astype(bf16))

        out = dot(attended, proj, NN)
        for c in range(chunks):
            out = out + dot(activated[c], down[c], NN)
        grad_normed = dot(grad_mixed, w_heads, NT)
        for c in range(chunks):
            grad_normed = grad_normed + dot(grad_u[c], w_hidden[c], NT)
        out = scatter_plane(out.astype(bf16)).astype(f32)
        grad_normed = scatter_plane(grad_normed.astype(bf16)).astype(f32)

        own = tokens[0].astype(f32)
        own_grad = cotangent[0].astype(f32)
        result = own + out + out_bias_all
        centred = own - jnp.mean(own, axis=1, keepdims=True)
        inv_std = lax.rsqrt(jnp.mean(centred * centred, axis=1, keepdims=True) + NORM_EPS)
        normal = centred * inv_std
        scaled = grad_normed * gain_all
        grad_tokens = own_grad + inv_std * (
            scaled
            - jnp.mean(scaled, axis=1, keepdims=True)
            - normal * jnp.mean(scaled * normal, axis=1, keepdims=True)
        )

        def full_columns(heads_part, hidden_parts):
            at = (jnp.arange(ranks) == rank)[:, None, None]
            heads_all = join_heads(jnp.where(at, heads_part[None, None], 0.0))
            hidden_all = join_hidden([jnp.where(at, x[None, None], 0.0) for x in hidden_parts])
            return jnp.concatenate([heads_all, hidden_all], axis=1)

        bias_sum = full_columns(
            jnp.sum(grad_mixed.astype(f32), axis=0), [jnp.sum(x.astype(f32), axis=0) for x in grad_u]
        )
        sums = jnp.concatenate(
            [
                bias_sum.reshape(n_dev, n_bias),
                jnp.sum(grad_normed * normal, axis=0).reshape(n_dev, n_width),
                jnp.sum(grad_normed, axis=0).reshape(n_dev, n_width),
                jnp.sum(own_grad, axis=0).reshape(n_dev, n_width),
            ],
            axis=1,
        )
        sums = jnp.sum(lax.all_to_all(sums, BOTH, 0, 0, tiled=True), axis=0)

        def own_columns(x):
            return swap_plane(x.reshape(ranks, in_rows, x.shape[1]))

        grad_in = jnp.concatenate(
            [join_heads(own_columns(grad_heads)), join_hidden([own_columns(x) for x in grad_hidden])], axis=1
        ).astype(f32)
        return (
            result.astype(bf16)[None],
            grad_tokens.astype(bf16)[None],
            sums[n_bias : n_bias + n_width],
            sums[n_bias + n_width : n_bias + 2 * n_width],
            grad_in,
            sums[:n_bias],
            grad_proj,
            jnp.concatenate(grad_down, axis=0).astype(f32),
            sums[n_bias + 2 * n_width :],
        )

    return shards


def solution(mesh):
    placed = (
        P("batch", "seq", None),
        P("batch", "seq"),
        P("batch", "seq"),
        P("batch", "seq", None),
        P(("batch", "seq")),
        P(("batch", "seq")),
        P(("batch", "seq"), None),
        P(("batch", "seq")),
        P(("batch", "seq"), None),
        P(("batch", "seq"), None),
        P(("batch", "seq")),
    )
    return jax.shard_map(
        build(mesh.shape["batch"], mesh.shape["seq"]),
        mesh=mesh,
        in_specs=placed,
        out_specs=(
            P("batch", "seq", None),
            P("batch", "seq", None),
            P(("batch", "seq")),
            P(("batch", "seq")),
            P(("batch", "seq"), None),
            P(("batch", "seq")),
            P(("batch", "seq"), None),
            P(("batch", "seq"), None),
            P(("batch", "seq")),
        ),
        check_vma=False,
    )
```

time: 5330 us -> 855 us (0.16)
  waiting for transfers between devices: 4680 us -> 434 us
  local copies, waits for them, and re-layouts: 173 us -> 42.6 us
  matrix products: 305 us -> 194 us
    unnamed x13 -> x16, waiting for transfers between devices: 2470 us -> 2.62 us
    reduce_scatter x4 -> x8, waiting for transfers between devices: 1840 us -> 186 us  [the longest x2 111 us: scatter_plane(): lax.psum_scatter(x, BOTH, axis_index_groups=plane_groups, scatter_dimensi...]
    all_gather x5 -> x8, waiting for transfers between devices: 374 us -> 227 us  [the longest x6 172 us: gather_line(): lax.all_gather(x, 'batch', axis_index_groups=line_groups, axis=0, tiled=T...]
    dot_general x23 -> x18, matrix products: 305 us -> 194 us  [dot(): lax.dot_general(left, right, (dims, ((), ())), preferred_element_type=f32)]
    dynamic_update_slice x6 -> x0, local copies, waits for them, and re-layouts: 74.5 us -> none  [the longest x2 40.4 us: step(): lax.dynamic_update_slice_in_dim(key_sums, lax.dynamic_slice_in_dim(key_su...]
    all_to_all x0 -> x3, blocking collectives: none -> 54.2 us  [swap_plane(): lax.all_to_all(x, BOTH, 0, 0, axis_index_groups=plane_groups, tiled=True)]
  transfers between devices with their start and end apart: 11 -> 22, of which waited for: 10 -> 15; matrix products, arithmetic and copies ran while one was open for 10% -> 32% of each run, Pallas kernels for 0% -> 5%
where the time goes in v1:
time: 855 us; the launch traced here: 849 us
  waiting for transfers between devices  434 us (51%)
  matrix products  194 us (23%)
  blocking collectives  54.2 us (6%)
  Pallas kernels  43.6 us (5%)
  local copies, waits for them, and re-layouts  42.6 us (5%)
  other arithmetic  39.8 us (5%)
  starting transfers between devices  25.9 us (3%)
  between operations  14.8 us (2%)
    dot_general x18, matrix products, dot(): lax.dot_general(left, right, (dims, ((), ())), preferred_element_type=f32)  194 us
    all_gather x6, waiting for transfers between devices, gather_line(): lax.all_gather(x, 'batch', axis_index_groups=line_groups, axis=0, tiled=T...  172 us
    reduce_scatter x2, waiting for transfers between devices, scatter_plane(): lax.psum_scatter(x, BOTH, axis_index_groups=plane_groups, scatter_dimensi...  111 us
    reduce_scatter x6, waiting for transfers between devices, scatter_line(): lax.psum_scatter(x, 'batch', axis_index_groups=line_groups, scatter_dimen...  74.3 us
    all_gather x2, waiting for transfers between devices, gather_plane(): lax.all_gather(x, BOTH, axis_index_groups=plane_groups, axis=0, tiled=True)  54.9 us
    all_to_all x3, blocking collectives, swap_plane(): lax.all_to_all(x, BOTH, 0, 0, axis_index_groups=plane_groups, tiled=True)  54.2 us
    pallas_call x1, Pallas kernels, attention(): pl.pallas_call(functools.partial(attention_kernel, min(256, length)), gri...  43.6 us
  transfers between devices with their start and end apart: 22, of which 15 were waited for; matrix products, arithmetic and copies ran while one was open for 32% of the time, Pallas kernels for 5%

profile of v1, /device:TPU:0, one launch (start us, length us, event | category | flops | bytes accessed | tf_op | source)
XLA Modules:
  0.0 848.7 jit_solution(16842229547444994757)
XLA Ops:
  13.1 17.9 %all_to_all.51 = bf16[8,64,512]{2,1,0:T(8,128)(2,1)} all-to-all(bf16[8,64,512]{2,1,0:T(8,128)(2,1)S(1)} %reshape.298), channel_id=1, replica_groups={{0,1,2,3,4,5,6,7},{8,9,10,11,12,13,14,15},{16,17,18,19,20,21,22,23},{24..., dimensions={0} | all-to-all | bytes 1048576 | tf_op jit(solution)/shard_map/all_to_all | solution.py:152
  33.1 12.5 %all_to_all.52 = bf16[8,64,512]{2,1,0:T(8,128)(2,1)} all-to-all(bf16[8,64,512]{2,1,0:T(8,128)(2,1)S(1)} %reshape.301), channel_id=1, replica_groups={{0,1,2,3,4,5,6,7},{8,9,10,11,12,13,14,15},{16,17,18,19,20,21,22,23},{24..., dimensions={0} | all-to-all | bytes 1048576 | tf_op jit(solution)/shard_map/all_to_all | solution.py:152
  49.6 23.9 %all_to_all.53 = bf16[8,64,768]{2,1,0:T(8,128)(2,1)} all-to-all(bf16[8,64,768]{2,1,0:T(8,128)(2,1)S(1)} %reshape.292), channel_id=1, replica_groups={{0,1,2,3,4,5,6,7},{8,9,10,11,12,13,14,15},{16,17,18,19,20,21,22,23},{24..., dimensions={0} | all-to-all | bytes 1572864 | tf_op jit(solution)/shard_map/all_to_all | solution.py:152
  74.1 3.3 all-to-all-start.2
  82.0 5.0 all-to-all-start
  87.7 3.8 fusion.68
  95.9 4.7 convert_reduce_fusion
  104.1 5.8 fusion.6
  109.9 16.9 %all-gather.15.cloned.1.call-done = bf16[2048,512]{1,0:T(8,128)(2,1)} async-done(((bf16[512,512]{1,0:T(8,128)(2,1)}), bf16[2048,512]{1,0:T(8,128)(2,1)}) %all-gather.15.cloned.1.call-update) | async-done | bytes 2097168 | tf_op jit(solution)/shard_map/all_gather | solution.py:155
  126.8 10.4 %fusion.89 = f32[2048,512]{1,0:T(8,128)} fusion(bf16[2048,2048]{1,0:T(8,128)(2,1)} %fusion.6, bf16[2048,512]{1,0:T(8,128)(2,1)} %all-gather.15.cloned.1.call-done), kind=kOutput, calls=%fused_computation.136 | convolution fusion | flops 4294967296 | bytes 14680064 | tf_op jit(solution)/shard_map/dot_general | solution.py:24
  137.2 36.1 %all-gather.17.cloned.1.call-done = bf16[512,2048]{1,0:T(8,128)(2,1)} async-done(((bf16[128,2048]{1,0:T(8,128)(2,1)}), bf16[512,2048]{1,0:T(8,128)(2,1)}) %all-gather.17.cloned.1.call-update) | async-done | bytes 2097168 | tf_op jit(solution)/shard_map/all_gather | solution.py:155
  173.4 54.9 %all-gather.25.cloned.1.call-done = bf16[1,2048,2048]{2,1,0:T(8,128)(2,1)} async-done(((bf16[1,256,2048]{2,1,0:T(8,128)(2,1)}), bf16[1,2048,2048]{2,1,0:T(8,128)(2,1)}) %all-gather.25.cloned.1.call-update) | async-done | bytes 8388624 | tf_op jit(solution)/shard_map/all_gather | solution.py:144
  228.3 13.1 %convert_reduce_fusion.3 = (f32[512]{0:T(512)}, bf16[2048,512]{1,0:T(8,128)(2,1)S(1)}) fusion(f32[2048,512]{1,0:T(8,128)} %fusion.89, f32[512]{0:T(512)S(1)} %bitcast.195, bf16[512,2048]{1,0:T(8,128)(2,1)} %all-gather.17.cloned.1.call-done, bf16[1,2048,2048]{2,1,0:T(8,128)(2,1)} %all-gather.25.cloned.1.call-done), kind=kOutput, calls=%fused_computation.43 | convolution fusion | flops 4318035456 | bytes 16781312 | tf_op jit(solution)/shard_map/dot_general | solution.py:24
  242.7 5.9 convolution_convert_fusion.2
  248.6 27.0 %all-gather.19.cloned.1.call-done = bf16[2048,512]{1,0:T(8,128)(2,1)} async-done(((bf16[512,512]{1,0:T(8,128)(2,1)}), bf16[2048,512]{1,0:T(8,128)(2,1)}) %all-gather.19.cloned.1.call-update) | async-done | bytes 2097168 | tf_op jit(solution)/shard_map/all_gather | solution.py:155
  275.6 10.5 %fusion.90 = f32[2048,512]{1,0:T(8,128)} fusion(bf16[2048,2048]{1,0:T(8,128)(2,1)} %fusion.6, bf16[2048,512]{1,0:T(8,128)(2,1)} %all-gather.19.cloned.1.call-done), kind=kOutput, calls=%fused_computation.137 | convolution fusion | flops 4294967296 | bytes 14680064 | tf_op jit(solution)/shard_map/dot_general | solution.py:24
  286.1 36.2 %all-gather.21.cloned.1.call-done = bf16[512,2048]{1,0:T(8,128)(2,1)} async-done(((bf16[128,2048]{1,0:T(8,128)(2,1)}), bf16[512,2048]{1,0:T(8,128)(2,1)}) %all-gather.21.cloned.1.call-update) | async-done | bytes 2097168 | tf_op jit(solution)/shard_map/all_gather | solution.py:155
  322.3 13.0 %convert_reduce_fusion.2 = (f32[512]{0:T(512)}, bf16[2048,512]{1,0:T(8,128)(2,1)S(1)}) fusion(f32[2048,512]{1,0:T(8,128)} %fusion.90, f32[512]{0:T(512)S(1)} %bitcast.198, bf16[512,2048]{1,0:T(8,128)(2,1)} %all-gather.21.cloned.1.call-done, bf16[1,2048,2048]{2,1,0:T(8,128)(2,1)} %all-gather.25.cloned.1.call-done), kind=kOutput, calls=%fused_computation.42 | convolution fusion | flops 4318035456 | bytes 16781312 | tf_op jit(solution)/shard_map/dot_general | solution.py:24
  336.6 9.8 %convolution_convert_fusion.1 = bf16[2048,512]{1,0:T(8,128)(2,1)} fusion(bf16[2048,2048]{1,0:T(8,128)(2,1)} %fusion.6, bf16[2048,512]{1,0:T(8,128)(2,1)S(1)} %get-tuple-element.38), kind=kOutput, calls=%fused_computation.53 | convolution fusion | flops 4296015872 | bytes 12582912 | tf_op jit(solution)/shard_map/dot_general | solution.py:24
  346.5 39.7 %all-gather.11.cloned.1.call-done = bf16[2048,768]{1,0:T(8,128)(2,1)} async-done(((bf16[512,768]{1,0:T(8,128)(2,1)}), bf16[2048,768]{1,0:T(8,128)(2,1)}) %all-gather.11.cloned.1.call-update) | async-done | bytes 3145744 | tf_op jit(solution)/shard_map/all_gather | solution.py:155
  386.1 11.7 %broadcast_add_fusion.mixed_ref = f32[2048,768]{1,0:T(8,128)} fusion(f32[768]{0:T(1024)S(1)} %dynamic-slice_reduce_fusion, bf16[2048,2048]{1,0:T(8,128)(2,1)} %fusion.6, bf16[2048,768]{1,0:T(8,128)(2,1)} %all-gather.11.cloned.1.call-done), kind=kOutput, calls=%fused_computation.50 | convolution fusion | flops 6444023808 | bytes 17828864 | tf_op jit(solution)/shard_map/dot_general | solution.py:24
  397.8 16.5 %all-gather.13.cloned.1.call-done = bf16[256,2048]{1,0:T(8,128)(2,1)} async-done(((bf16[64,2048]{1,0:T(8,128)(2,1)}), bf16[256,2048]{1,0:T(8,128)(2,1)}) %all-gather.13.cloned.1.call-update) | async-done | bytes 1048592 | tf_op jit(solution)/shard_map/all_gather | solution.py:155
  414.3 6.1 fusion.48.grad_ref
  420.5 43.6 %shard_map.172 = (bf16[2048,256]{1,0:T(8,128)(2,1)S(1)}, bf16[2048,768]{1,0:T(8,128)(2,1)}) custom-call(f32[2048,768]{1,0:T(8,128)} %broadcast_add_fusion.mixed_ref, bf16[2048,256]{1,0:T(8,128)(2,1)S(1)} %fusion.48.grad_ref, f32[2048,128]{1,0:T(8,128)S(1)} %get-tuple-element.29.cos_ref, f32[2048,128]{1,0:T(8,128)S(1)} %get-tuple-element.28.sin_ref, ...), custom_call_target="tpu_custom_call" | custom-call | flops 21474836480 | bytes 8388608 | tf_op jit(solution)/shard_map/pallas_call | solution.py:101
  464.1 10.3 %convolution_convert_fusion = bf16[2048,768]{1,0:T(8,128)(2,1)} fusion(bf16[2048,2048]{1,0:T(8,128)(2,1)S(1)} %bitcast.175, bf16[2048,768]{1,0:T(8,128)(2,1)} %get-tuple-element.12), kind=kOutput, calls=%fused_computation.46 | convolution fusion | flops 6444023808 | bytes 14680064 | tf_op jit(solution)/shard_map/dot_general | solution.py:24
  474.5 6.7 fusion.51
  481.3 11.2 %fusion.37 = bf16[512,2048]{1,0:T(8,128)(2,1)} fusion(bf16[1,2048,2048]{2,1,0:T(8,128)(2,1)} %all-gather.25.cloned.1.call-done, f32[2048,512]{1,0:T(8,128)} %fusion.89, f32[512]{0:T(512)S(1)} %bitcast.196), kind=kOutput, calls=%fused_computation.51 | convolution fusion | flops 4306501632 | bytes 14682112 | tf_op jit(solution)/shard_map/dot_general | solution.py:24
  492.8 11.3 %fusion.40 = bf16[512,2048]{1,0:T(8,128)(2,1)} fusion(bf16[1,2048,2048]{2,1,0:T(8,128)(2,1)} %all-gather.25.cloned.1.call-done, f32[2048,512]{1,0:T(8,128)} %fusion.90, f32[512]{0:T(512)S(1)} %bitcast.199), kind=kOutput, calls=%fused_computation.52 | convolution fusion | flops 4306501632 | bytes 14682112 | tf_op jit(solution)/shard_map/dot_general | solution.py:24
  504.2 12.8 %fusion.91 = f32[2048,2048]{1,0:T(8,128)} fusion(bf16[2048,768]{1,0:T(8,128)(2,1)} %get-tuple-element.12, bf16[2048,768]{1,0:T(8,128)(2,1)} %all-gather.11.cloned.1.call-done), kind=kOutput, calls=%fused_computation.138 | convolution fusion | flops 6442450944 | bytes 23068672 | tf_op jit(solution)/shard_map/dot_general | solution.py:24
  517.0 8.4 fusion.92
  525.4 17.1 %add_convert_fusion = bf16[2048,2048]{1,0:T(8,128)(2,1)} fusion(f32[2048,2048]{1,0:T(8,128)} %fusion.91, f32[2048,2048]{1,0:T(8,128)} %fusion.92, bf16[2048,512]{1,0:T(8,128)(2,1)S(1)} %copy-done.6, bf16[2048,512]{1,0:T(8,128)(2,1)} %all-gather.19.cloned.1.call-done), kind=kOutput, calls=%fused_computation.9 | convolution fusion | flops 4307550208 | bytes 46137344 | tf_op jit(solution)/shard_map/dot_general | solution.py:24
  544.2 11.4 %fusion.83 = f32[2048,2048]{1,0:T(8,128)} fusion(bf16[512,2048]{1,0:T(8,128)(2,1)S(1)} %copy-done.22, f32[2048,512]{1,0:T(8,128)} %fusion.90, f32[512]{0:T(512)S(1)} %bitcast.200), kind=kOutput, calls=%fused_computation.130 | convolution fusion | flops 4305453056 | bytes 23070720 | tf_op jit(solution)/shard_map/dot_general | solution.py:24
  555.6 8.5 fusion.82
  564.1 15.4 %add_convert_fusion.1 = bf16[2048,2048]{1,0:T(8,128)(2,1)} fusion(f32[2048,2048]{1,0:T(8,128)} %fusion.83, f32[2048,2048]{1,0:T(8,128)} %fusion.82, bf16[2048,256]{1,0:T(8,128)(2,1)S(1)} %get-tuple-element.11, bf16[256,2048]{1,0:T(8,128)(2,1)S(1)} %copy-done.8), kind=kOutput, calls=%fused_computation.10 | convolution fusion | flops 2160066560 | bytes 44040192 | tf_op jit(solution)/shard_map/dot_general | solution.py:24
  581.3 3.5 all-to-all-start.7
  585.4 8.6 %all-to-all-done.7 = bf16[8,64,512]{2,1,0:T(8,128)(2,1)S(1)} async-done(((bf16[8,64,512]{2,1,0:T(8,128)(2,1)}), bf16[8,64,512]{2,1,0:T(8,128)(2,1)S(1)}, u32[]{:S(2)}, u32[]{:S(2)}) %all-to-all-start.7) | async-done | bytes 524320 | tf_op jit(solution)/shard_map/all_to_all | solution.py:152
  594.0 3.5 all-to-all-start.8
  600.1 6.6 all-to-all-done.8
  606.7 4.4 all-to-all-start.6
  613.4 28.9 %reduce-scatter.21.cloned.1.call-done = bf16[128,2048]{1,0:T(8,128)(2,1)} async-done(((bf16[512,2048]{1,0:T(8,128)(2,1)}), bf16[128,2048]{1,0:T(8,128)(2,1)}) %reduce-scatter.21.cloned.1.call-update) | async-done | bytes 524304 | tf_op jit(solution)/shard_map/reduce_scatter | solution.py:158
  642.3 45.4 %reduce-scatter.23.cloned.1.call-done = bf16[128,2048]{1,0:T(8,128)(2,1)} async-done(((bf16[512,2048]{1,0:T(8,128)(2,1)}), bf16[128,2048]{1,0:T(8,128)(2,1)}) %reduce-scatter.23.cloned.1.call-update) | async-done | bytes 524304 | tf_op jit(solution)/shard_map/reduce_scatter | solution.py:158
  697.8 3.2 maximum_bitcast_fusion
  703.0 3.6 reshape.311
  706.7 4.5 copy.53
  717.5 44.4 %reduce-scatter.11.cloned.1.call-done = bf16[256,2048]{1,0:T(8,128)(2,1)} async-done(((bf16[2048,2048]{1,0:T(8,128)(2,1)}), bf16[256,2048]{1,0:T(8,128)(2,1)}) %reduce-scatter.11.cloned.1.call-update) | async-done | bytes 1048592 | tf_op jit(solution)/shard_map/reduce_scatter | solution.py:147
  765.2 4.6 all-to-all-start.5
  769.8 66.8 %reduce-scatter.9.cloned.1.call-done = bf16[256,2048]{1,0:T(8,128)(2,1)} async-done(((bf16[2048,2048]{1,0:T(8,128)(2,1)}), bf16[256,2048]{1,0:T(8,128)(2,1)}) %reduce-scatter.9.cloned.1.call-update) | async-done | bytes 1048592 | tf_op jit(solution)/shard_map/reduce_scatter | solution.py:147
  836.6 4.1 fusion.72
  (177 shorter events, 60.1 us)
Async XLA Ops:
  7.2 88.7 %all-gather.23.cloned.1.call-start = ((), (), s32[]{:S(2)}) async-start(), calls=%async_computation.31 | async-start | bytes 9437184 | tf_op jit(solution)/shard_map/all_gather | solution.py:144
  7.9 118.9 %all-gather.15.cloned.1.call-start = ((), (), s32[]{:S(2)}) async-start(), calls=%async_computation.19 | async-start | bytes 2621440 | tf_op jit(solution)/shard_map/all_gather | solution.py:155
  12.4 18.6 %copy-start.9 = (bf16[256,2048]{1,0:T(8,128)(2,1)S(1)}, bf16[256,2048]{1,0:T(8,128)(2,1)}, u32[]{:S(2)}) copy-start(bf16[256,2048]{1,0:T(8,128)(2,1)} %param.19) | copy-start | bytes 3145732
  31.0 142.4 %all-gather.17.cloned.1.call-start = ((), (), s32[]{:S(2)}) async-start(), calls=%async_computation.20 | async-start | bytes 2621440 | tf_op jit(solution)/shard_map/all_gather | solution.py:155
  32.1 14.2 %slice-start.2 = ((bf16[64,14336]{1,0:T(8,128)(2,1)}), bf16[64,6144]{1,0:T(8,128)(2,1)S(1)}, s32[]{:S(2)}) async-start(bf16[64,14336]{1,0:T(8,128)(2,1)} %param.16), calls=%async_computation.35 | async-start | bytes 1572864 | tf_op jit(solution)/shard_map/slice | solution.py:226
  32.1 196.2 %all-gather.25.cloned.1.call-start = ((), (), s32[]{:S(2)}) async-start(), calls=%async_computation.32 | async-start | bytes 9437184 | tf_op jit(solution)/shard_map/all_gather | solution.py:144
  32.7 243.0 %all-gather.19.cloned.1.call-start = ((), (), s32[]{:S(2)}) async-start(), calls=%async_computation.21 | async-start | bytes 2621440 | tf_op jit(solution)/shard_map/all_gather | solution.py:155
  45.6 276.7 %all-gather.21.cloned.1.call-start = ((), (), s32[]{:S(2)}) async-start(), calls=%async_computation.22 | async-start | bytes 2621440 | tf_op jit(solution)/shard_map/all_gather | solution.py:155
  46.2 339.9 %all-gather.11.cloned.1.call-start = ((), (), s32[]{:S(2)}) async-start(), calls=%async_computation.17 | async-start | bytes 3932160 | tf_op jit(solution)/shard_map/all_gather | solution.py:155
  47.9 25.5 %copy-start.15 = (s32[1,256]{1,0:T(1,128)S(1)}, s32[1,256]{1,0:T(1,128)}, u32[]{:S(2)}) copy-start(s32[1,256]{1,0:T(1,128)} %param.12) | copy-start | bytes 3076
  47.9 30.2 %copy-start.16 = (bf16[448]{0:T(512)(128)(2,1)S(1)}, bf16[448]{0:T(512)(128)(2,1)}, u32[]{:S(2)}) copy-start(bf16[448]{0:T(512)(128)(2,1)} %param.17) | copy-start | bytes 2692
  48.0 30.2 %copy-start.17 = (bf16[64]{0:T(256)(128)(2,1)S(1)}, bf16[64]{0:T(256)(128)(2,1)}, u32[]{:S(2)}) copy-start(bf16[64]{0:T(256)(128)(2,1)} %param.20) | copy-start | bytes 388
  48.0 30.2 %copy-start.18 = (bf16[64]{0:T(256)(128)(2,1)S(1)}, bf16[64]{0:T(256)(128)(2,1)}, u32[]{:S(2)}) copy-start(bf16[64]{0:T(256)(128)(2,1)} %param.15) | copy-start | bytes 388
  48.0 30.2 %copy-start.19 = (bf16[64]{0:T(256)(128)(2,1)S(1)}, bf16[64]{0:T(256)(128)(2,1)}, u32[]{:S(2)}) copy-start(bf16[64]{0:T(256)(128)(2,1)} %param.14) | copy-start | bytes 388
  74.1 7.9 all-to-all-start.2
  77.4 336.9 %all-gather.13.cloned.1.call-start = ((), (), s32[]{:S(2)}) async-start(), calls=%async_computation.18 | async-start | bytes 1310720 | tf_op jit(solution)/shard_map/all_gather | solution.py:155
  82.0 12.5 %all-to-all-start = ((bf16[32,2,320]{2,1,0:T(2,128)(2,1)}), bf16[32,2,320]{2,1,0:T(2,128)(2,1)S(1)}, u32[]{:S(2)}, u32[]{:S(2)}) async-start(bf16[32,2,320]{2,1,0:T(2,128)(2,1)} %reshape.330), calls=%async_computation | async-start | bytes 98304 | tf_op jit(solution)/shard_map/all_to_all | solution.py:180
  87.1 494.2 %reduce-scatter.15.cloned.1.call-start = ((), (), s32[]{:S(2)}) async-start(), calls=%async_computation.26 | async-start | bytes 2621440 | tf_op jit(solution)/shard_map/reduce_scatter | solution.py:158
  95.5 8.6 %copy-start.10 = (f32[2048]{0:T(1024)}, f32[2048]{0:T(1024)S(1)}, u32[]{:S(2)}) copy-start(f32[2048]{0:T(1024)S(1)} %mul.175) | copy-start | bytes 24580
  95.9 5.9 copy-start.1
  228.3 14.4 %copy-start.4 = (bf16[2048,2048]{1,0:T(8,128)(2,1)S(1)}, bf16[2048,2048]{1,0:T(8,128)(2,1)}, u32[]{:S(2)}) copy-start(bf16[2048,2048]{1,0:T(8,128)(2,1)} %fusion.6) | copy-start | bytes 25165828
  248.6 336.8 %reduce-scatter.17.cloned.1.call-start = ((), (), s32[]{:S(2)}) async-start(), calls=%async_computation.27 | async-start | bytes 2621440 | tf_op jit(solution)/shard_map/reduce_scatter | solution.py:158
  346.4 260.3 %reduce-scatter.13.cloned.1.call-start = ((), (), s32[]{:S(2)}) async-start(), calls=%async_computation.25 | async-start | bytes 3932160 | tf_op jit(solution)/shard_map/reduce_scatter | solution.py:158
  414.3 6.2 copy-start
  414.3 49.8 %slice-start = ((s8[8388608]{0:T(1024)(128)(4,1)}), s8[4194304]{0:T(1024)(128)(4,1)S(1)}, s32[]{:S(2)}) async-start(s8[8388608]{0:T(1024)(128)(4,1)} %bitcast.174), calls=%async_computation.33 | async-start | bytes 8388608
  420.5 43.7 %slice-start.1 = ((s8[8388608]{0:T(1024)(128)(4,1)}), s8[4194304]{0:T(1024)(128)(4,1)S(1)}, s32[]{:S(2)}) async-start(s8[8388608]{0:T(1024)(128)(4,1)} %bitcast.174), calls=%async_computation.34 | async-start | bytes 8388608
  474.4 137.2 %reduce-scatter.19.cloned.1.call-start = ((), (), s32[]{:S(2)}) async-start(), calls=%async_computation.28 | async-start | bytes 1310720 | tf_op jit(solution)/shard_map/reduce_scatter | solution.py:158
  481.2 161.0 %reduce-scatter.21.cloned.1.call-start = ((), (), s32[]{:S(2)}) async-start(), calls=%async_computation.29 | async-start | bytes 2621440 | tf_op jit(solution)/shard_map/reduce_scatter | solution.py:158
  492.6 195.1 %reduce-scatter.23.cloned.1.call-start = ((), (), s32[]{:S(2)}) async-start(), calls=%async_computation.30 | async-start | bytes 2621440 | tf_op jit(solution)/shard_map/reduce_scatter | solution.py:158
  504.1 257.9 %reduce-scatter.11.cloned.1.call-start = ((), (), s32[]{:S(2)}) async-start(), calls=%async_computation.24 | async-start | bytes 9437184 | tf_op jit(solution)/shard_map/reduce_scatter | solution.py:147
  504.2 12.9 %copy-start.21 = (bf16[2048,512]{1,0:T(8,128)(2,1)S(1)}, bf16[2048,512]{1,0:T(8,128)(2,1)}, u32[]{:S(2)}) copy-start(bf16[2048,512]{1,0:T(8,128)(2,1)} %all-gather.15.cloned.1.call-done) | copy-start | bytes 6291460
  504.2 12.9 %copy-start.24 = (bf16[2048,512]{1,0:T(8,128)(2,1)S(1)}, bf16[2048,512]{1,0:T(8,128)(2,1)}, u32[]{:S(2)}) copy-start(bf16[2048,512]{1,0:T(8,128)(2,1)} %copy-done.23) | copy-start | bytes 6291460
  517.0 8.4 copy-start.6
  542.6 1.6 copy-start.22
  542.6 294.0 %reduce-scatter.9.cloned.1.call-start = ((), (), s32[]{:S(2)}) async-start(), calls=%async_computation.23 | async-start | bytes 9437184 | tf_op jit(solution)/shard_map/reduce_scatter | solution.py:147
  544.2 11.4 %copy-start.20 = (bf16[512,2048]{1,0:T(8,128)(2,1)S(1)}, bf16[512,2048]{1,0:T(8,128)(2,1)}, u32[]{:S(2)}) copy-start(bf16[512,2048]{1,0:T(8,128)(2,1)} %all-gather.17.cloned.1.call-done) | copy-start | bytes 6291460
  544.2 11.4 %copy-start.25 = (f32[2048,512]{1,0:T(8,128)S(1)}, f32[2048,512]{1,0:T(8,128)}, u32[]{:S(2)}) copy-start(f32[2048,512]{1,0:T(8,128)} %fusion.89) | copy-start | bytes 12582916
  555.6 8.5 %copy-start.8 = (bf16[256,2048]{1,0:T(8,128)(2,1)S(1)}, bf16[256,2048]{1,0:T(8,128)(2,1)}, u32[]{:S(2)}) copy-start(bf16[256,2048]{1,0:T(8,128)(2,1)} %all-gather.13.cloned.1.call-done) | copy-start | bytes 3145732
  579.5 1.5 copy-start.3
  580.7 4.6 copy-start.12
  581.2 29.9 %copy-start.13 = (f32[512]{0:T(512)S(1)}, f32[512]{0:T(512)}, u32[]{:S(2)}) copy-start(f32[512]{0:T(512)} %get-tuple-element.35) | copy-start | bytes 6148
  581.2 29.9 %copy-start.14 = (f32[512]{0:T(512)S(1)}, f32[512]{0:T(512)}, u32[]{:S(2)}) copy-start(f32[512]{0:T(512)} %get-tuple-element.37) | copy-start | bytes 6148
  581.3 12.7 %all-to-all-start.7 = ((bf16[8,64,512]{2,1,0:T(8,128)(2,1)}), bf16[8,64,512]{2,1,0:T(8,128)(2,1)S(1)}, u32[]{:S(2)}, u32[]{:S(2)}) async-start(bf16[8,64,512]{2,1,0:T(8,128)(2,1)} %bitcast.182), calls=%async_computation.11 | async-start | bytes 1048576 | tf_op jit(solution)/shard_map/all_to_all | solution.py:152
  594.0 12.7 %all-to-all-start.8 = ((bf16[8,64,512]{2,1,0:T(8,128)(2,1)}), bf16[8,64,512]{2,1,0:T(8,128)(2,1)S(1)}, u32[]{:S(2)}, u32[]{:S(2)}) async-start(bf16[8,64,512]{2,1,0:T(8,128)(2,1)} %bitcast.183), calls=%async_computation.13 | async-start | bytes 1048576 | tf_op jit(solution)/shard_map/all_to_all | solution.py:152
  606.7 83.7 %copy-start.7 = (bf16[8,64,512]{2,1,0:T(8,128)(2,1)}, bf16[8,64,512]{2,1,0:T(8,128)(2,1)S(1)}, u32[]{:S(2)}) copy-start(bf16[8,64,512]{2,1,0:T(8,128)(2,1)S(1)} %all-to-all-done.8) | copy-start | bytes 1572868
  606.7 96.3 %all-to-all-start.6 = ((bf16[8,64,768]{2,1,0:T(8,128)(2,1)}), bf16[8,64,768]{2,1,0:T(8,128)(2,1)}, u32[]{:S(2)}, u32[]{:S(2)}) async-start(bf16[8,64,768]{2,1,0:T(8,128)(2,1)} %bitcast.181), calls=%async_computation.9 | async-start | bytes 1572864 | tf_op jit(solution)/shard_map/all_to_all | solution.py:152
  711.2 50.8 %copy-start.11 = (f32[2048]{0:T(1024)S(1)}, f32[2048]{0:T(1024)}, u32[]{:S(2)}) copy-start(f32[2048]{0:T(1024)} %copy-done.10) | copy-start | bytes 24580
  765.2 75.5 %all-to-all-start.5 = ((f32[32,1,640]{2,1,0:T(1,128)}), f32[32,1,640]{2,1,0:T(1,128)S(1)}, u32[]{:S(2)}, u32[]{:S(2)}) async-start(f32[32,1,640]{2,1,0:T(1,128)} %all_to_all.37), calls=%async_computation.7 | async-start | bytes 163840 | tf_op jit(solution)/shard_map/all_to_all | solution.py:310
  (3 other events, 3.8 us)
Sparse Core Ops, SparseCore 0:
  9.9 69.0 all-gather.22
  80.5 46.2 all-gather.14
  128.9 44.3 all-gather.16
  175.1 53.0 all-gather.24
  229.7 45.9 all-gather.18
  277.6 44.6 all-gather.20
  323.9 62.2 all-gather.10
  387.7 26.5 all-gather.12
  416.6 43.3 reduce-scatter.14
  462.2 43.1 reduce-scatter.16
  507.8 59.5 reduce-scatter.12
  570.1 27.1 reduce-scatter.18
  599.7 42.5 reduce-scatter.20
  644.4 43.1 reduce-scatter.22
  691.3 70.6 reduce-scatter.10
  765.3 71.2 reduce-scatter.8

commit v2 on v1

--- a/solution.py
+++ b/solution.py
@@ -133,6 +133,165 @@
     return value, slope
 
 
+def params():
+    return pltpu.CompilerParams(vmem_limit_bytes=48 * 1024 * 1024)
+
+
+def norm_kernel(steps, own_ref, other_ref, gain_ref, shift_ref, out_ref):
+    def write(x):
+        x = x.astype(f32)
+        centred = x - jnp.mean(x, axis=1, keepdims=True)
+        inv_std = lax.rsqrt(jnp.mean(centred * centred, axis=1, keepdims=True) + NORM_EPS)
+        out_ref[...] = (centred * inv_std * gain_ref[...] + shift_ref[...]).astype(bf16)
+
+    @pl.when(pl.program_id(0) < steps)
+    def _():
+        write(own_ref[...])
+
+    @pl.when(pl.program_id(0) >= steps)
+    def _():
+        write(other_ref[...])
+
+
+def join_kernel(steps, own_ref, other_ref, out_ref):
+    @pl.when(pl.program_id(0) < steps)
+    def _():
+        out_ref[...] = own_ref[...]
+
+    @pl.when(pl.program_id(0) >= steps)
+    def _():
+        out_ref[...] = other_ref[...]
+
+
+def over_both(kernel, own, other, *rest):
+    tokens, width = own.shape
+    block = min(256, tokens)
+    steps = tokens // block
+    whole = pl.BlockSpec((1, width), lambda i: (0, 0))
+    return pl.pallas_call(
+        functools.partial(kernel, steps),
+        grid=(2 * steps,),
+        in_specs=[
+            pl.BlockSpec((block, width), lambda i: (jnp.minimum(i, steps - 1), 0)),
+            pl.BlockSpec((block, width), lambda i: (jnp.maximum(i - steps, 0), 0)),
+        ]
+        + [whole] * len(rest),
+        out_specs=pl.BlockSpec((block, width), lambda i: (i, 0)),
+        out_shape=jax.ShapeDtypeStruct((2 * tokens, width), bf16),
+        compiler_params=params(),
+        cost_estimate=pl.CostEstimate(flops=16 * tokens * width, bytes_accessed=8 * tokens * width, transcendentals=0),
+    )(own, other, *[x[None] for x in rest])
+
+
+def hidden_kernel(normed_ref, grad_ref, up_ref, down_ref, bias_ref, act_ref, du_ref, sum_ref):
+    u = dot(normed_ref[...], up_ref[...], NN) + bias_ref[...]
+    grad = dot(grad_ref[...], down_ref[...], NT)
+    value, slope = gelu_parts(u)
+    act_ref[...] = value.astype(bf16)
+    du = (grad * slope).astype(bf16)
+    du_ref[...] = du
+
+    @pl.when(pl.program_id(0) == 0)
+    def _():
+        sum_ref[...] = jnp.zeros_like(sum_ref)
+
+    sum_ref[...] += jnp.sum(du.astype(f32), axis=0, keepdims=True)
+
+
+def hidden_layer(normed, grad, up, down, bias):
+    tokens, width = normed.shape
+    units = up.shape[1]
+    block = min(256, tokens)
+    rows = pl.BlockSpec((block, width), lambda i: (i, 0))
+    part = pl.BlockSpec((block, units), lambda i: (i, 0))
+
+    def whole(shape):
+        return pl.BlockSpec(shape, lambda i: (0, 0))
+
+    return pl.pallas_call(
+        hidden_kernel,
+        grid=(tokens // block,),
+        in_specs=[rows, rows, whole((width, units)), whole((units, width)), whole((1, units))],
+        out_specs=[part, part, whole((1, units))],
+        out_shape=[
+            jax.ShapeDtypeStruct((tokens, units), bf16),
+            jax.ShapeDtypeStruct((tokens, units), bf16),
+            jax.ShapeDtypeStruct((1, units), f32),
+        ],
+        compiler_params=params(),
+        cost_estimate=pl.CostEstimate(
+            flops=4 * tokens * width * units, bytes_accessed=4 * tokens * width, transcendentals=0
+        ),
+    )(normed, grad, up, down, bias[None])
+
+
+def heads_kernel(normed_ref, grad_ref, in_ref, proj_ref, bias_ref, mixed_ref, dout_ref):
+    mixed_ref[...] = dot(normed_ref[...], in_ref[...], NN) + bias_ref[...]
+    dout_ref[...] = dot(grad_ref[...], proj_ref[...], NT).astype(bf16)
+
+
+def heads_layer(normed, grad, weight, proj, bias):
+    tokens, width = normed.shape
+    columns, inner = weight.shape[1], proj.shape[0]
+    block = min(256, tokens)
+    rows = pl.BlockSpec((block, width), lambda i: (i, 0))
+
+    def whole(shape):
+        return pl.BlockSpec(shape, lambda i: (0, 0))
+
+    return pl.pallas_call(
+        heads_kernel,
+        grid=(tokens // block,),
+        in_specs=[rows, rows, whole((width, columns)), whole((inner, width)), whole((1, columns))],
+        out_specs=[pl.BlockSpec((block, columns), lambda i: (i, 0)), pl.BlockSpec((block, inner), lambda i: (i, 0))],
+        out_shape=[
+            jax.ShapeDtypeStruct((tokens, columns), f32),
+            jax.ShapeDtypeStruct((tokens, inner), bf16),
+        ],
+        compiler_params=params(),
+        cost_estimate=pl.CostEstimate(
+            flops=2 * tokens * width * (columns + inner), bytes_accessed=4 * tokens * width, transcendentals=0
+        ),
+    )(normed, grad, weight, proj, bias[None])
+
+
+def joined_kernel(count, dims, first_ref, *refs):
+    total = dot(refs[0][...], refs[count][...], dims)
+    for i in range(1, count):
+        total += dot(refs[i][...], refs[count + i][...], dims)
+    refs[2 * count][...] = total.astype(bf16)
+
+
+def joined_product(lefts, rights, dims, first, tokens):
+    count = len(lefts)
+    columns = rights[0].shape[1 if dims is NN else 0]
+    block = min(256, tokens)
+    steps = tokens // block
+    rights_specs = [pl.BlockSpec(x.shape, lambda i, first: (0, 0)) for x in rights]
+    return pl.pallas_call(
+        functools.partial(joined_kernel, count, dims),
+        grid_spec=pltpu.PrefetchScalarGridSpec(
+            num_scalar_prefetch=1,
+            grid=(steps,),
+            in_specs=[pl.BlockSpec((block, x.shape[1]), lambda i, first: (first[0] * steps + i, 0)) for x in lefts]
+            + rights_specs,
+            out_specs=pl.BlockSpec((block, columns), lambda i, first: (i, 0)),
+        ),
+        out_shape=jax.ShapeDtypeStruct((tokens, columns), bf16),
+        compiler_params=params(),
+        cost_estimate=pl.CostEstimate(
+            flops=2 * tokens * columns * sum(x.shape[1] for x in lefts), bytes_accessed=4 * tokens * columns,
+            transcendentals=0,
+        ),
+    )(first[None], *lefts, *rights)
+
+
+def after(x, *others):
+    if not others:
+        return x
+    return lax.optimization_barrier((x,) + others)[0]
+
+
 def build(n_batch, n_seq):
     ranks = CORES * n_seq
     planes = n_batch // CORES
@@ -140,13 +299,56 @@
     plane_groups = [[z * ranks + r for r in range(ranks)] for z in range(planes)]
     line_groups = [[z * CORES + c for z in range(planes)] for c in range(CORES)]
 
-    def gather_plane(x):
-        return lax.all_gather(x, BOTH, axis_index_groups=plane_groups, axis=0, tiled=True)
-
-    def scatter_plane(x):
-        return lax.psum_scatter(
-            x, BOTH, axis_index_groups=plane_groups, scatter_dimension=0, tiled=True
-        )
+    def seq_permute(x, bit):
+        return lax.ppermute(x, "seq", [(s, s ^ bit) for s in range(n_seq)])
+
+    def core_permute(x):
+        return lax.ppermute(x, "batch", [(b, b ^ 1) for b in range(n_batch)])
+
+    def take(x, i):
+        return lax.dynamic_index_in_dim(x, i, 0, keepdims=False)
+
+    def two(flag, mine, theirs, axis):
+        return jnp.where(flag == 0, jnp.stack([mine, theirs], axis), jnp.stack([theirs, mine], axis))
+
+    def gather_plane(x, core, seq):
+        if n_seq != 4:
+            whole = lax.all_gather(x, BOTH, axis_index_groups=plane_groups, axis=0, tiled=True)
+            whole = whole.reshape((CORES, n_seq * x.shape[0]) + x.shape[1:])
+            return take(whole, core), take(whole, 1 - core), whole
+        bit_x, bit_y = seq % 2, seq // 2
+        half = x.shape[1] // 2
+        left, right = x[:, :half], x[:, half:]
+        left = two(bit_y, left, seq_permute(left, 2), 0)
+        right = two(bit_x, right, seq_permute(right, 1), 0)
+        early = left
+        left = two(bit_x, left, seq_permute(left, 1), 1)
+        right = two(bit_y, right, seq_permute(right, 2), 0)
+        own = jnp.concatenate([left, right], axis=3).reshape(4 * x.shape[0], x.shape[1])
+        return own, core_permute(own), early
+
+    def scatter_plane(product, tokens, core, seq):
+        if n_seq != 4:
+            both = [product(core ^ i) for i in range(CORES)]
+            return lax.psum_scatter(
+                jnp.concatenate(both), BOTH, axis_index_groups=plane_groups, scatter_dimension=0, tiled=True
+            ).astype(f32)
+        other = core_permute(product(jnp.int32(1)))
+        x = product(jnp.int32(0)).astype(f32) + other.astype(f32)
+        x = x.astype(bf16).reshape(2, 2, tokens // n_seq, x.shape[1])
+        bit_x, bit_y = seq % 2, seq // 2
+        half = x.shape[3] // 2
+        left, right = x[..., :half], x[..., half:]
+        by_x = jnp.swapaxes(left, 0, 1)
+        from_x = seq_permute(take(by_x, 1 - bit_x), 1)
+        from_y = seq_permute(take(right, 1 - bit_y), 2)
+        left = (take(by_x, bit_x).astype(f32) + from_x.astype(f32)).astype(bf16)
+        right = (take(right, bit_y).astype(f32) + from_y.astype(f32)).astype(bf16)
+        from_y = seq_permute(take(left, 1 - bit_y), 2)
+        from_x = seq_permute(take(right, 1 - bit_x), 1)
+        left = take(left, bit_y).astype(f32) + from_y.astype(f32)
+        right = take(right, bit_x).astype(f32) + from_x.astype(f32)
+        return jnp.concatenate([left, right], axis=1)
 
     def swap_plane(x):
         return lax.all_to_all(x, BOTH, 0, 0, axis_index_groups=plane_groups, tiled=True)
@@ -158,6 +360,29 @@
         return lax.psum_scatter(
             x, "batch", axis_index_groups=line_groups, scatter_dimension=0, tiled=True
         )
+
+    class Chain:
+        def __init__(self, x, plane):
+            self.x, self.plane, self.step = x, plane, 0
+            self.up = self.down = None
+
+        def hop(self, *others):
+            self.step += 1
+            left = planes - self.step
+            up = take(self.x, jnp.minimum(left + self.plane, planes - 1))
+            down = take(self.x, jnp.maximum(self.plane - left, 0))
+            if self.step > 1:
+                up = (up.astype(f32) + self.up.astype(f32)).astype(bf16)
+                down = (down.astype(f32) + self.down.astype(f32)).astype(bf16)
+            up, down = after(up, *others), after(down, *others)
+            self.up = lax.ppermute(up, "batch", [(b, b + CORES) for b in range(CORES * self.step)])
+            self.down = lax.ppermute(down, "batch", [(b, b - CORES) for b in range(CORES * left, n_batch)])
+            return self.up, self.down
+
+        def result(self):
+            while self.step < planes - 1:
+                self.hop()
+            return take(self.x, self.plane).astype(f32) + self.up.astype(f32) + self.down.astype(f32)
 
     def shards(
         tokens, segments, positions, cotangent, ln_gain, ln_bias, in_weight, in_bias, proj_weight, down_weight, out_bias
@@ -175,40 +400,55 @@
         mine_cols = width // ranks
         index = lax.axis_index("batch") * n_seq + lax.axis_index("seq")
         rank = index % ranks
-
-        small = jnp.concatenate([in_bias, ln_gain, ln_bias, out_bias])
+        plane = index // ranks
+        core, seq = rank // n_seq, rank % n_seq
+
+        def split_heads(x):
+            lead = x.shape[0]
+            x = x.reshape(lead, 3, head_groups, ranks, head_cols)
+            return jnp.transpose(x, (3, 0, 1, 2, 4)).reshape(ranks, lead, 3 * mine_cols)
+
+        def split_hidden(x, c):
+            lead = x.shape[0]
+            x = x.reshape(lead, planes, ranks, chunks, part)[:, :, :, c]
+            return jnp.transpose(x, (2, 0, 1, 3)).reshape(ranks, lead, planes * part)
+
+        def join_heads(x):
+            lead = x.shape[1]
+            x = x.reshape(ranks, lead, 3, head_groups, head_cols)
+            return jnp.transpose(x, (1, 2, 3, 0, 4)).reshape(lead, 3 * width)
+
+        def join_hidden(xs):
+            lead = xs[0].shape[1]
+            x = jnp.stack([x.reshape(ranks, lead, planes, part) for x in xs])
+            return jnp.transpose(x, (2, 3, 1, 0, 4)).reshape(lead, hidden)
+
+        def swap_columns(x):
+            return swap_plane(x).reshape(ranks * in_rows, x.shape[2])
+
+        hidden_send = [swap_columns(split_hidden(in_weight[:, 3 * width :], 0))]
+        later = [split_heads(in_weight[:, : 3 * width])]
+        later += [split_hidden(in_weight[:, 3 * width :], c) for c in range(1, chunks)]
+        later = swap_columns(after(jnp.concatenate(later, axis=2), hidden_send[0]))
+        heads_send = later[:, : 3 * mine_cols]
+        for c in range(1, chunks):
+            at = 3 * mine_cols + (c - 1) * planes * part
+            hidden_send.append(later[:, at : at + planes * part])
+        token_halves = gather_plane(tokens[0], core, seq)
+        grad_halves = gather_plane(after(cotangent[0], token_halves[2]), core, seq)
+        small = jnp.concatenate([x.astype(f32) for x in (in_bias, ln_gain, ln_bias, out_bias, positions[0])])
         small_all = lax.all_to_all(
-            jnp.broadcast_to(small[None], (n_dev, small.shape[0])), BOTH, 0, 0, tiled=True
-        ).astype(f32)
+            jnp.broadcast_to(after(small, token_halves[2])[None], (n_dev, small.shape[0])), BOTH, 0, 0, tiled=True
+        )
         n_bias = in_bias.shape[0]
         n_width = ln_gain.shape[0]
         bias_all = small_all[:, :n_bias].reshape(-1)
         gain_all = small_all[:, n_bias : n_bias + n_width].reshape(-1)
         shift_all = small_all[:, n_bias + n_width : n_bias + 2 * n_width].reshape(-1)
-        out_bias_all = small_all[:, n_bias + 2 * n_width :].reshape(-1)
-        place = lax.all_to_all(
-            jnp.broadcast_to(positions, (ranks, rows)), BOTH, 0, 0, axis_index_groups=plane_groups, tiled=True
-        ).reshape(-1)
-
-        def split_heads(x):
-            lead = x.shape[0]
-            x = x.reshape(lead, 3, head_groups, ranks, head_cols)
-            return jnp.transpose(x, (3, 0, 1, 2, 4)).reshape(ranks, lead, 3 * mine_cols)
-
-        def split_hidden(x, c):
-            lead = x.shape[0]
-            x = x.reshape(lead, planes, ranks, chunks, part)[:, :, :, c]
-            return jnp.transpose(x, (2, 0, 1, 3)).reshape(ranks, lead, planes * part)
-
-        def join_heads(x):
-            lead = x.shape[1]
-            x = x.reshape(ranks, lead, 3, head_groups, head_cols)
-            return jnp.transpose(x, (1, 2, 3, 0, 4)).reshape(lead, 3 * width)
-
-        def join_hidden(xs):
-            lead = xs[0].shape[1]
-            x = jnp.stack([x.reshape(ranks, lead, planes, part) for x in xs])
-            return jnp.transpose(x, (2, 3, 1, 0, 4)).reshape(lead, hidden)
+        out_bias_all = small_all[:, n_bias + 2 * n_width : n_bias + 3 * n_width].reshape(-1)
+        place = small_all[:, n_bias + 3 * n_width :].reshape(planes, CORES, length)
+        place = lax.dynamic_index_in_dim(place, plane, 0, keepdims=False).astype(jnp.int32)
+        place = jnp.concatenate([take(place, core), take(place, 1 - core)])
 
         bias_heads = lax.dynamic_index_in_dim(
             split_heads(bias_all[None, : 3 * width]), rank, 0, keepdims=False
@@ -218,64 +458,104 @@
             for c in range(chunks)
         ]
 
-        def in_columns(x):
-            return gather_line(swap_plane(x).reshape(ranks * in_rows, x.shape[2]))
-
-        down = [gather_line(down_weight[c * part : (c + 1) * part]) for c in range(chunks)]
-        w_hidden = [in_columns(split_hidden(in_weight[:, 3 * width :], c)) for c in range(chunks)]
-        w_heads = in_columns(split_heads(in_weight[:, : 3 * width]))
+        def own_columns(x):
+            return swap_plane(x.reshape(ranks, in_rows, x.shape[1]))
+
+        own_parts = []
+        def pack(main, extra):
+            lead, few = extra.shape[:2]
+            columns = few * width // main.shape[1]
+            extra = extra.reshape(lead, few, width // columns, columns)
+            return jnp.concatenate([main, jnp.swapaxes(extra, 1, 2).reshape(lead, -1, columns)], axis=2)
+
+        def unpack(x, few):
+            lead, packed, total = x.shape
+            columns = few * width // packed
+            extra = x[:, :, total - columns :].reshape(lead, width // columns, few, columns)
+            return x[:, :, : total - columns], jnp.swapaxes(extra, 1, 2).reshape(lead, few, width)
+
+        down, w_hidden = [None] * chunks, [None] * chunks
+        activated, grad_u, sum_u, grad_down, grad_hidden = [], [], [], [], []
+
+        def hidden_part(c, *others):
+            act, du, total = hidden_layer(normed, after(grad_all, *others), w_hidden[c], down[c], bias_hidden[c][0])
+            activated.append(act)
+            grad_u.append(du)
+            sum_u.append(total)
+            return dot(normed, du, TN).astype(bf16), dot(act, grad_all, TN).astype(bf16)
+
+        normed = over_both(norm_kernel, *token_halves[:2], gain_all, shift_all)
+        grad_all = over_both(join_kernel, *grad_halves[:2])
+        def gather_hidden(c, *others):
+            x = pack(hidden_send[c][None], down_weight[None, c * part : (c + 1) * part])[0]
+            x = gather_line(after(x, *others)).reshape(planes, ranks * in_rows, -1)
+            x, y = unpack(x, part)
+            w_hidden[c], down[c] = x.reshape(width, -1), y.reshape(-1, width)
+            return w_hidden[c]
+
         if whole_heads:
             proj = gather_line(proj_weight)
         else:
             proj = lax.dynamic_slice_in_dim(
                 lax.all_gather(proj_weight, BOTH, axis=0, tiled=True), rank * mine_cols, mine_cols, 0
             )
-
-        token_all = gather_plane(tokens[0])
-        grad_all = gather_plane(cotangent[0])
-
-        wide = token_all.astype(f32)
-        centred = wide - jnp.mean(wide, axis=1, keepdims=True)
-        inv_std = lax.rsqrt(jnp.mean(centred * centred, axis=1, keepdims=True) + NORM_EPS)
-        normed = (centred * inv_std * gain_all + shift_all).astype(bf16)
-
-        activated, grad_u, grad_down, grad_hidden = [], [], [], []
-        for c in range(chunks):
-            u = dot(normed, w_hidden[c], NN) + bias_hidden[c]
-            value, slope = gelu_parts(u)
-            act = value.astype(bf16)
-            du = (dot(grad_all, down[c], NT) * slope).astype(bf16)
-            activated.append(act)
-            grad_u.append(du)
-            grad_down.append(scatter_line(dot(act, grad_all, TN).astype(bf16)))
-            grad_hidden.append(scatter_line(dot(normed, du, TN).astype(bf16)))
-
-        mixed = dot(normed, w_heads, NN) + bias_heads
-        grad_attended = dot(grad_all, proj, NT).astype(bf16)
+        gather_hidden(0, proj)
+        w_heads = gather_line(after(heads_send, proj))
+        by_plane = (planes, width // planes, -1)
+
+        def scatter_packed(main, extra, few):
+            x = pack(main.reshape(by_plane), extra.reshape(planes, few, width))
+            x, y = unpack(scatter_line(x.reshape(width, -1))[None], few)
+            return x[0], y[0].astype(f32)
+
+        to_hidden, to_down = hidden_part(0)
+        for c in range(1, chunks):
+            gather_hidden(c, w_hidden[0], activated[0])
+        first, second = scatter_packed(to_hidden, to_down, part)
+        grad_hidden.append(first)
+        grad_down.append(second)
+        hop = ()
+        mixed, grad_attended = heads_layer(normed, after(grad_all, to_hidden, to_down, *hidden_send), w_heads, proj, bias_heads[0])
         cosine, sine = rotary_wide(place)
         start = (jnp.arange(place.shape[0], dtype=jnp.int32) % length - place)[:, None]
-        attended, grad_mixed = attention(mixed, grad_attended, cosine, sine, start, length)
-        grad_proj = dot(attended, grad_all, TN).astype(bf16)
+        attended, grad_mixed = [], []
+        for i in range(CORES):
+            rows_of = slice(i * length, (i + 1) * length)
+            a, m = attention(
+                mixed[rows_of], after(grad_attended[rows_of], *hop), cosine[rows_of], sine[rows_of], start[rows_of], length
+            )
+            attended.append(a)
+            grad_mixed.append(m)
+        attended, grad_mixed = jnp.concatenate(attended), jnp.concatenate(grad_mixed)
+        to_proj = dot(attended, after(grad_all, *hop), TN).astype(bf16)
+        to_heads = dot(normed, grad_mixed, TN).astype(bf16)
         if whole_heads:
-            grad_proj = scatter_line(grad_proj).astype(f32)
+            grad_heads, grad_proj = scatter_packed(to_heads, to_proj, proj_rows)
         else:
+            grad_heads = scatter_line(to_heads)
             grad_proj = lax.psum_scatter(
                 lax.dynamic_update_slice_in_dim(
-                    jnp.zeros((width, width), f32), grad_proj.astype(f32), rank * mine_cols, 0
+                    jnp.zeros((width, width), f32), to_proj.astype(f32), rank * mine_cols, 0
                 ),
                 BOTH, scatter_dimension=0, tiled=True,
             )
-        grad_heads = scatter_line(dot(normed, grad_mixed, TN).astype(bf16))
-
-        out = dot(attended, proj, NN)
-        for c in range(chunks):
-            out = out + dot(activated[c], down[c], NN)
-        grad_normed = dot(grad_mixed, w_heads, NT)
-        for c in range(chunks):
-            grad_normed = grad_normed + dot(grad_u[c], w_hidden[c], NT)
-        out = scatter_plane(out.astype(bf16)).astype(f32)
-        grad_normed = scatter_plane(grad_normed.astype(bf16)).astype(f32)
-
+
+        last = []
+        for c in range(1, chunks):
+            to_hidden, to_down = hidden_part(c, to_heads, to_proj)
+            last += [to_hidden, to_down]
+            grad_hidden.append(scatter_line(to_hidden))
+            grad_down.append(scatter_line(to_down).astype(f32))
+        bias_heads_sum = jnp.sum(grad_mixed.astype(f32), axis=0)
+        attended, grad_mixed = after(attended, *last), after(grad_mixed, *last)
+        out = scatter_plane(
+            lambda i: joined_product([attended] + activated, [proj] + down, NN, i, length), length, core, seq
+        )
+        grad_normed = scatter_plane(
+            lambda i: joined_product([grad_mixed] + grad_u, [w_heads] + w_hidden, NT, i, length), length, core, seq
+        )
+
+        grad_normed = after(grad_normed, grad_proj, grad_heads)
         own = tokens[0].astype(f32)
         own_grad = cotangent[0].astype(f32)
         result = own + out + out_bias_all
@@ -289,6 +569,10 @@
             - normal * jnp.mean(scaled * normal, axis=1, keepdims=True)
         )
 
+        last = [result, grad_tokens]
+        grad_hidden[1:] = [after(x, *last) for x in grad_hidden[1:]]
+        grad_down[1:] = [after(x, *last) for x in grad_down[1:]]
+
         def full_columns(heads_part, hidden_parts):
             at = (jnp.arange(ranks) == rank)[:, None, None]
             heads_all = join_heads(jnp.where(at, heads_part[None, None], 0.0))
@@ -296,7 +580,7 @@
             return jnp.concatenate([heads_all, hidden_all], axis=1)
 
         bias_sum = full_columns(
-            jnp.sum(grad_mixed.astype(f32), axis=0), [jnp.sum(x.astype(f32), axis=0) for x in grad_u]
+            bias_heads_sum, [x[0] for x in sum_u]
         )
         sums = jnp.concatenate(
             [
@@ -308,9 +592,6 @@
             axis=1,
         )
         sums = jnp.sum(lax.all_to_all(sums, BOTH, 0, 0, tiled=True), axis=0)
-
-        def own_columns(x):
-            return swap_plane(x.reshape(ranks, in_rows, x.shape[1]))
 
         grad_in = jnp.concatenate(
             [join_heads(own_columns(grad_heads)), join_hidden([own_columns(x) for x in grad_hidden])], axis=1

time: 855 us -> 587 us (0.69)
  waiting for transfers between devices: 434 us -> 119 us
  matrix products: 194 us -> 45.3 us
  Pallas kernels: 43.6 us -> 154 us
  local copies, waits for them, and re-layouts: 42.6 us -> 117 us
  blocking collectives: 54.2 us -> 0 us
  other arithmetic: 39.8 us -> 70.1 us
  starting transfers between devices: 25.9 us -> 55.4 us
    all_gather x6 -> x4, waiting for transfers between devices: 172 us -> 11 us  [gather_line(): lax.all_gather(x, 'batch', axis_index_groups=line_groups, axis=0, tiled=T...]
    dot_general x18 -> x6, matrix products: 194 us -> 45.3 us  [dot(): lax.dot_general(left, right, (dims, ((), ())), preferred_element_type=f32)]
    reduce_scatter x2 -> x0, waiting for transfers between devices: 111 us -> none  [scatter_plane(): lax.psum_scatter(x, BOTH, axis_index_groups=plane_groups, scatter_dimensi...]
    pallas_call x0 -> x9, Pallas kernels: none -> 109 us  [the longest x4 44.8 us: joined_product(): pl.pallas_call(functools.partial(joined_kernel, count, dims), grid_spec=p...]
    ppermute x0 -> x20, waiting for transfers between devices: none -> 74.8 us  [the longest x16 74.8 us: seq_permute(): return lax.ppermute(x, 'seq', [(s, s ^ bit) for s in range(n_seq)])]
    reduce_scatter x6 -> x4, waiting for transfers between devices: 74.3 us -> 10.9 us  [scatter_line(): lax.psum_scatter(x, 'batch', axis_index_groups=line_groups, scatter_dimen...]
    all_gather x2 -> x0, waiting for transfers between devices: 54.9 us -> none  [gather_plane(): lax.all_gather(x, BOTH, axis_index_groups=plane_groups, axis=0, tiled=True)]
    all_to_all x3 -> x0, blocking collectives: 54.2 us -> none  [swap_plane(): lax.all_to_all(x, BOTH, 0, 0, axis_index_groups=plane_groups, tiled=True)]
  transfers between devices with their start and end apart: 22 -> 35, of which waited for: 15 -> 12; matrix products, arithmetic and copies ran while one was open for 32% -> 37% of each run, Pallas kernels for 5% -> 27%
where the time goes in v2:
time: 587 us; the launch traced here: 576 us
  Pallas kernels  154 us (26%)
  waiting for transfers between devices  119 us (20%)
  local copies, waits for them, and re-layouts  117 us (20%)
  other arithmetic  70.1 us (12%)
  starting transfers between devices  55.4 us (9%)
  matrix products  45.3 us (8%)
  between operations  15.9 us (3%)
    ppermute x16, waiting for transfers between devices, seq_permute(): return lax.ppermute(x, 'seq', [(s, s ^ bit) for s in range(n_seq)])  74.8 us
    dot_general x6, matrix products, dot(): lax.dot_general(left, right, (dims, ((), ())), preferred_element_type=f32)  45.3 us
    pallas_call x4, Pallas kernels, joined_product(): pl.pallas_call(functools.partial(joined_kernel, count, dims), grid_spec=p...  44.8 us
    pallas_call x2, Pallas kernels, attention(): pl.pallas_call(functools.partial(attention_kernel, min(256, length)), gri...  44.7 us
    pallas_call x2, Pallas kernels, hidden_layer(): pl.pallas_call(hidden_kernel, grid=(tokens // block,), in_specs=[rows, ro...  28.8 us
    ppermute x16, starting transfers between devices, seq_permute(): return lax.ppermute(x, 'seq', [(s, s ^ bit) for s in range(n_seq)])  25.6 us
    unnamed x137, local copies, waits for them, and re-layouts  23.2 us
    pallas_call x2, Pallas kernels, over_both(): pl.pallas_call(functools.partial(kernel, steps), grid=(2 * steps,), in_sp...  20.9 us
  transfers between devices with their start and end apart: 35, of which 12 were waited for; matrix products, arithmetic and copies ran while one was open for 37% of the time, Pallas kernels for 27%

profile of v2, /device:TPU:0, one launch (start us, length us, event | category | flops | bytes accessed | tf_op | source)
XLA Modules:
  0.0 576.4 jit_solution(12281744202010228976)
XLA Ops:
  13.8 5.2 all-to-all-start.1
  20.4 7.8 %all-to-all-done.1 = bf16[8,64,512]{2,1,0:T(8,128)(2,1)S(1)} async-done(((bf16[8,64,512]{2,1,0:T(8,128)(2,1)}), bf16[8,64,512]{2,1,0:T(8,128)(2,1)S(1)}, u32[]{:S(2)}, u32[]{:S(2)}) %all-to-all-start.1) | async-done | bytes 524320 | tf_op jit(solution)/shard_map/all_to_all | solution.py:354
  29.3 10.9 %all-gather.5.cloned.1.call-done.proj_ref.refs_3_ = bf16[256,2048]{1,0:T(8,128)(2,1)} async-done(((bf16[64,2048]{1,0:T(8,128)(2,1)}), bf16[256,2048]{1,0:T(8,128)(2,1)}) %all-gather.5.cloned.1.call-update) | async-done | bytes 1048592 | tf_op jit(solution)/shard_map/all_gather | solution.py:357
  48.9 7.1 %collective-permute-done = bf16[256,1024]{1,0:T(8,128)(2,1)} collective-permute-done((bf16[256,1024]{1,0:T(8,128)(2,1)}, bf16[256,1024]{1,0:T(8,128)(2,1)}, u32[]{:S(2)}, u32[]{:S(2)}) %collective-permute-start) | collective-permute-done | bytes 524320 | tf_op jit(solution)/shard_map/ppermute | solution.py:303
  67.9 3.8 all-to-all-start.2
  74.6 25.5 %collective-permute-done.5 = bf16[256,1024]{1,0:T(8,128)(2,1)S(1)} collective-permute-done((bf16[256,1024]{1,0:T(8,128)(2,1)}, bf16[256,1024]{1,0:T(8,128)(2,1)S(1)}, u32[]{:S(2)}, u32[]{:S(2)}) %collective-permute-start.5) | collective-permute-done | bytes 524320 | tf_op jit(solution)/shard_map/ppermute | solution.py:303
  100.3 7.3 %collective-permute-start.6 = (bf16[2,256,1024]{2,1,0:T(8,128)(2,1)S(1)}, bf16[2,256,1024]{2,1,0:T(8,128)(2,1)S(1)}, u32[]{:S(2)}, u32[]{:S(2)}) collective-permute-start(bf16[2,256,1024]{2,1,0:T(8,128)(2,1)S(1)} %maximum_select_fusion.8), channel_id=1, source_target_pairs={{0,1},{1,0},{2,3},{3,2},{4,5},{5,4},{6,7},{7,6},{8,9},{9,8},{10,11... | collective-permute-start | bytes 3145736 | tf_op jit(solution)/shard_map/ppermute | solution.py:303
  116.2 14.1 %collective-permute-done.6 = bf16[2,256,1024]{2,1,0:T(8,128)(2,1)S(1)} collective-permute-done((bf16[2,256,1024]{2,1,0:T(8,128)(2,1)S(1)}, bf16[2,256,1024]{2,1,0:T(8,128)(2,1)S(1)}, u32[]{:S(2)}, u32[]{:S(2)}) %collective-permute-start.6) | collective-permute-done | bytes 1048608 | tf_op jit(solution)/shard_map/ppermute | solution.py:303
  130.8 3.0 collective-permute-done.8
  138.5 3.9 all-to-all-start
  143.5 7.2 %all-to-all-done = f32[32,1,896]{2,1,0:T(1,128)S(1)} async-done(((f32[32,1,896]{2,1,0:T(1,128)}), f32[32,1,896]{2,1,0:T(1,128)S(1)}, u32[]{:S(2)}, u32[]{:S(2)}) %all-to-all-start) | async-done | bytes 114720 | tf_op jit(solution)/shard_map/all_to_all | solution.py:440
  153.2 11.3 %shard_map.169.normed_ref = bf16[2048,2048]{1,0:T(8,128)(2,1)} custom-call(bf16[1024,2048]{1,0:T(8,128)(2,1)} %pad_maximum_fusion.own_ref, bf16[1024,2048]{1,0:T(8,128)(2,1)} %collective-permute-done.4.other_ref, f32[1,2048]{1,0:T(1,128)S(1)} %broadcast_in_dim_reshape.11.gain_ref, f32[1,2048]{1,0:T(1,128)S(1)} %broadcast_in_dim_reshape.12.shift_ref), custom_call_target="tpu_custom_call" | custom-call | flops 33554432 | bytes 16777216 | tf_op jit(solution)/shard_map/pallas_call | solution.py:171
  164.5 9.6 %shard_map.170.grad_ref = bf16[2048,2048]{1,0:T(8,128)(2,1)} custom-call(bf16[1024,2048]{1,0:T(8,128)(2,1)} %pad_maximum_fusion.1.own_ref, bf16[1024,2048]{1,0:T(8,128)(2,1)} %collective-permute-done.9.other_ref), custom_call_target="tpu_custom_call" | custom-call | flops 33554432 | bytes 16777216 | tf_op jit(solution)/shard_map/pallas_call | solution.py:171
  174.1 3.8 fusion.40
  181.6 14.3 %shard_map.171 = (bf16[2048,512]{1,0:T(8,128)(2,1)S(1)}, bf16[2048,512]{1,0:T(8,128)(2,1)S(1)}, f32[1,512]{1,0:T(1,128)S(1)}) custom-call(bf16[2048,2048]{1,0:T(8,128)(2,1)} %shard_map.169.normed_ref, bf16[2048,2048]{1,0:T(8,128)(2,1)} %shard_map.170.grad_ref, bf16[2048,512]{1,0:T(8,128)(2,1)} %bitcast.270, bf16[512,2048]{1,0:T(8,128)(2,1)} %bitcast.259, ...), custom_call_target="tpu_custom_call" | custom-call | flops 8589934592 | bytes 16777216 | tf_op jit(solution)/shard_map/pallas_call | solution.py:211
  197.6 9.4 %convolution_convert_fusion.3 = bf16[512,2048]{1,0:T(8,128)(2,1)} fusion(bf16[2048,512]{1,0:T(8,128)(2,1)S(1)} %get-tuple-element.38.refs_1_, bf16[2048,2048]{1,0:T(8,128)(2,1)} %shard_map.170.grad_ref), kind=kOutput, calls=%fused_computation.13 | convolution fusion | flops 4296015872 | bytes 12582912 | tf_op jit(solution)/shard_map/dot_general | solution.py:24
  207.0 4.5 reshape_reshape.15
  211.6 6.4 %copy.105 = bf16[4,128,4,512]{1,2,0,3:T(4,128)(2,1)} copy(bf16[4,128,4,512]{3,2,1,0:T(4,128)(2,1)} %reshape_reshape.15) | data formatting | bytes 4194304 | tf_op jit(solution)/shard_map/reshape;reshape | solution.py:468
  218.0 4.6 concatenate.149
  222.6 8.3 %convolution_convert_fusion.4 = bf16[2048,512]{0,1:T(8,128)(2,1)S(1)} fusion(bf16[2048,2048]{1,0:T(8,128)(2,1)} %shard_map.169.normed_ref, bf16[2048,512]{1,0:T(8,128)(2,1)S(1)} %copy-done.13), kind=kOutput, calls=%fused_computation.14 | convolution fusion | flops 4296015872 | bytes 12582912 | tf_op jit(solution)/shard_map/dot_general | solution.py:24
  234.3 3.8 fusion.19
  241.9 14.6 %shard_map.172 = (f32[2048,768]{1,0:T(8,128)}, bf16[2048,256]{1,0:T(8,128)(2,1)S(1)}) custom-call(bf16[2048,2048]{1,0:T(8,128)(2,1)} %shard_map.169.normed_ref, bf16[2048,2048]{1,0:T(8,128)(2,1)} %shard_map.170.grad_ref, bf16[2048,768]{1,0:T(8,128)(2,1)S(1)} %copy-done.5, bf16[256,2048]{1,0:T(8,128)(2,1)S(1)} %copy-done.6, f32[1,768]{1,0:T(1,128)S(1)} %fusion.27.bias_ref), custom_call_target="tpu_custom_call" | custom-call | flops 8589934592 | bytes 16777216 | tf_op jit(solution)/shard_map/pallas_call | solution.py:242
  256.7 6.0 %fusion.36 = (f32[1024,768]{1,0:T(8,128)}, f32[1024,768]{1,0:T(8,128)}) fusion(f32[2048,768]{1,0:T(8,128)} %get-tuple-element.42), kind=kLoop, calls=%fused_computation.139 | loop fusion | bytes 12582912 | tf_op jit(solution)/shard_map/slice | solution.py:525
  262.7 22.3 %shard_map.173 = (bf16[1024,256]{1,0:T(8,128)(2,1)S(1)}, bf16[1024,768]{1,0:T(8,128)(2,1)S(1)}) custom-call(f32[1024,768]{1,0:T(8,128)} %get-tuple-element.64.mixed_ref, bf16[1024,256]{1,0:T(8,128)(2,1)S(1)} %get-tuple-element.84.grad_ref, f32[1024,128]{1,0:T(8,128)S(1)} %copy-done.4, f32[1024,128]{1,0:T(8,128)S(1)} %get-tuple-element.80.sin_ref, ...), custom_call_target="tpu_custom_call" | custom-call | flops 10737418240 | bytes 4194304 | tf_op jit(solution)/shard_map/pallas_call | solution.py:101
  285.1 22.4 %shard_map.174 = (bf16[1024,256]{1,0:T(8,128)(2,1)S(1)}, bf16[1024,768]{1,0:T(8,128)(2,1)S(1)}) custom-call(f32[1024,768]{1,0:T(8,128)} %get-tuple-element.63.mixed_ref, bf16[1024,256]{1,0:T(8,128)(2,1)S(1)} %get-tuple-element.83.grad_ref, f32[1024,128]{1,0:T(8,128)S(1)} %copy-done.3, f32[1024,128]{1,0:T(8,128)S(1)} %copy-done.2, s32[1024,1]{1,0:T(8,128)S(1)} %copy.95.start_ref), custom_call_target="tpu_custom_call" | custom-call | flops 10737418240 | bytes 4194304 | tf_op jit(solution)/shard_map/pallas_call | solution.py:101
  316.9 9.8 %convolution_convert_fusion = bf16[2048,768]{0,1:T(8,128)(2,1)S(1)} fusion(bf16[2048,2048]{1,0:T(8,128)(2,1)} %shard_map.169.normed_ref, bf16[2048,768]{1,0:T(8,128)(2,1)S(1)} %constant_dynamic-update-slice_fusion.2.refs_0_), kind=kOutput, calls=%fused_computation.7 | convolution fusion | flops 6444023808 | bytes 14680064 | tf_op jit(solution)/shard_map/dot_general | solution.py:24
  329.1 3.8 fusion.39
  336.6 14.5 %shard_map.175 = (bf16[2048,512]{1,0:T(8,128)(2,1)S(1)}, bf16[2048,512]{1,0:T(8,128)(2,1)S(1)}, f32[1,512]{1,0:T(1,128)S(1)}) custom-call(bf16[2048,2048]{1,0:T(8,128)(2,1)} %shard_map.169.normed_ref, bf16[2048,2048]{1,0:T(8,128)(2,1)} %shard_map.170.grad_ref, bf16[2048,512]{1,0:T(8,128)(2,1)} %bitcast.273, bf16[512,2048]{1,0:T(8,128)(2,1)} %bitcast.262, ...), custom_call_target="tpu_custom_call" | custom-call | flops 8589934592 | bytes 16777216 | tf_op jit(solution)/shard_map/pallas_call | solution.py:211
  352.4 5.8 convolution_convert_fusion.1
  358.2 9.7 %convolution_convert_fusion.2 = bf16[2048,512]{1,0:T(8,128)(2,1)} fusion(bf16[2048,2048]{1,0:T(8,128)(2,1)} %shard_map.169.normed_ref, bf16[2048,512]{1,0:T(8,128)(2,1)S(1)} %get-tuple-element.50.refs_2_), kind=kOutput, calls=%fused_computation.12 | convolution fusion | flops 4296015872 | bytes 12582912 | tf_op jit(solution)/shard_map/dot_general | solution.py:24
  370.0 12.9 %shard_map.179 = bf16[1024,2048]{1,0:T(8,128)(2,1)} custom-call(s32[1]{0:T(128)} %constant.211.clone.1.first_ref, bf16[2048,768]{1,0:T(8,128)(2,1)} %copy-done.30, bf16[2048,512]{1,0:T(8,128)(2,1)S(1)} %copy-done.14, bf16[2048,512]{1,0:T(8,128)(2,1)S(1)} %get-tuple-element.50.refs_2_, bf16[2048,768]{1,0:T(8,128)(2,1)} %all-gather.9.cloned.1.call-done.in_ref.refs_3_, ...), custom_call_target="tpu_custom_call" | custom-call | flops 7516192768 | bytes 8388608 | tf_op jit(solution)/shard_map/pallas_call | solution.py:271
  384.1 9.6 %shard_map.177 = bf16[1024,2048]{1,0:T(8,128)(2,1)} custom-call(s32[1]{0:T(128)} %constant.211.clone.1.first_ref, bf16[2048,256]{1,0:T(8,128)(2,1)S(1)} %constant_dynamic-update-slice_fusion.refs_0_, bf16[2048,512]{1,0:T(8,128)(2,1)S(1)} %copy-done.9, bf16[2048,512]{1,0:T(8,128)(2,1)} %copy-done.11, bf16[256,2048]{1,0:T(8,128)(2,1)S(1)} %copy-done.7, ...), custom_call_target="tpu_custom_call" | custom-call | flops 5368709120 | bytes 8388608 | tf_op jit(solution)/shard_map/pallas_call | solution.py:271
  399.1 9.6 %shard_map.176 = bf16[1024,2048]{1,0:T(8,128)(2,1)} custom-call(s32[1]{0:T(128)} %constant.187.clone.1.first_ref, bf16[2048,256]{1,0:T(8,128)(2,1)S(1)} %constant_dynamic-update-slice_fusion.refs_0_, bf16[2048,512]{1,0:T(8,128)(2,1)S(1)} %copy-done.10, bf16[2048,512]{1,0:T(8,128)(2,1)} %copy-done.11, bf16[256,2048]{1,0:T(8,128)(2,1)S(1)} %copy-done.7, ...), custom_call_target="tpu_custom_call" | custom-call | flops 5368709120 | bytes 8388608 | tf_op jit(solution)/shard_map/pallas_call | solution.py:271
  408.7 12.8 %shard_map.178 = bf16[1024,2048]{1,0:T(8,128)(2,1)} custom-call(s32[1]{0:T(128)} %constant.187.clone.1.first_ref, bf16[2048,768]{1,0:T(8,128)(2,1)} %copy-done.30, bf16[2048,512]{1,0:T(8,128)(2,1)S(1)} %copy-done.15, bf16[2048,512]{1,0:T(8,128)(2,1)S(1)} %copy-done.17, bf16[2048,768]{1,0:T(8,128)(2,1)} %all-gather.9.cloned.1.call-done.in_ref.refs_3_, ...), custom_call_target="tpu_custom_call" | custom-call | flops 7516192768 | bytes 8388608 | tf_op jit(solution)/shard_map/pallas_call | solution.py:271
  424.8 3.5 all-to-all-start.5
  428.3 10.8 %reduce-scatter.5.cloned.1.call-done = bf16[512,1024]{0,1:T(8,128)(2,1)} async-done(((bf16[2048,1024]{0,1:T(8,128)(2,1)}), bf16[512,1024]{0,1:T(8,128)(2,1)}) %reduce-scatter.5.cloned.1.call-update) | async-done | bytes 1048592 | tf_op jit(solution)/shard_map/reduce_scatter | solution.py:360
  441.5 5.4 add_convert_fusion
  452.6 6.1 %add_convert_fusion.1 = bf16[1024,2048]{1,0:T(8,128)(2,1)} fusion(bf16[1024,2048]{1,0:T(8,128)(2,1)} %collective-permute-done.10, bf16[1024,2048]{1,0:T(8,128)(2,1)S(1)} %copy-done.31), kind=kLoop, calls=%fused_computation.1 | loop fusion | flops 8388608 | bytes 12582912 | tf_op jit(solution)/shard_map/convert_element_type | solution.py:338
  458.8 4.4 all-to-all-start.4
  485.3 3.5 reshape.615
  488.8 4.4 copy.104
  493.2 3.3 reshape.616
  510.2 13.6 %collective-permute-done.11 = bf16[2,256,1024]{2,1,0:T(8,128)(2,1)} collective-permute-done((bf16[2,256,1024]{2,1,0:T(8,128)(2,1)}, bf16[2,256,1024]{2,1,0:T(8,128)(2,1)}, u32[]{:S(2)}, u32[]{:S(2)}) %collective-permute-start.11) | collective-permute-done | bytes 1048608 | tf_op jit(solution)/shard_map/ppermute | solution.py:303
  527.2 7.8 %collective-permute-done.19 = bf16[256,1024]{1,0:T(8,128)(2,1)S(1)} collective-permute-done((bf16[256,1024]{1,0:T(8,128)(2,1)S(1)}, bf16[256,1024]{1,0:T(8,128)(2,1)S(1)}, u32[]{:S(2)}, u32[]{:S(2)}) %collective-permute-start.19) | collective-permute-done | bytes 524320 | tf_op jit(solution)/shard_map/ppermute | solution.py:303
  537.5 4.3 all-to-all-start.3
  541.8 3.6 collective-permute-done.14
  551.3 3.7 all-to-all-start.6
  557.8 6.4 %all-to-all-done.6 = bf16[8,64,512]{2,1,0:T(8,128)(2,1)S(1)} async-done(((bf16[8,64,512]{2,1,0:T(8,128)(2,1)}), bf16[8,64,512]{2,1,0:T(8,128)(2,1)S(1)}, u32[]{:S(2)}, u32[]{:S(2)}) %all-to-all-start.6) | async-done | bytes 524320 | tf_op jit(solution)/shard_map/all_to_all | solution.py:354
  (341 shorter events, 154.0 us)
Async XLA Ops:
  7.2 33.1 %all-gather.5.cloned.1.call-start = ((), (), s32[]{:S(2)}) async-start(), calls=%async_computation.11 | async-start | bytes 1310720 | tf_op jit(solution)/shard_map/all_gather | solution.py:357
  13.8 14.4 %all-to-all-start.1 = ((bf16[8,64,512]{2,1,0:T(8,128)(2,1)}), bf16[8,64,512]{2,1,0:T(8,128)(2,1)S(1)}, u32[]{:S(2)}, u32[]{:S(2)}) async-start(bf16[8,64,512]{2,1,0:T(8,128)(2,1)} %reshape.588), calls=%async_computation.1 | async-start | bytes 1048576 | tf_op jit(solution)/shard_map/all_to_all | solution.py:354
  18.9 155.2 %all-gather.7.cloned.1.call-start = ((), (), s32[]{:S(2)}) async-start(), calls=%async_computation.12 | async-start | bytes 5242880 | tf_op jit(solution)/shard_map/all_gather | solution.py:357
  20.1 20.1 %copy-start.18 = (bf16[1,256,2048]{2,1,0:T(8,128)(2,1)S(1)}, bf16[1,256,2048]{2,1,0:T(8,128)(2,1)}, u32[]{:S(2)}) copy-start(bf16[1,256,2048]{2,1,0:T(8,128)(2,1)} %param.11) | copy-start | bytes 3145732
  42.2 13.8 %collective-permute-start = (bf16[256,1024]{1,0:T(8,128)(2,1)}, bf16[256,1024]{1,0:T(8,128)(2,1)}, u32[]{:S(2)}, u32[]{:S(2)}) collective-permute-start(bf16[256,1024]{1,0:T(8,128)(2,1)} %get-tuple-element.98), channel_id=1, source_target_pairs={{0,2},{1,3},{2,0},{3,1},{4,6},{5,7},{6,4},{7,5},{8,10},{9,11},{10,... | collective-permute-start | bytes 1572872 | tf_op jit(solution)/shard_map/ppermute | solution.py:303
  43.7 16.3 %collective-permute-start.2 = (bf16[256,1024]{1,0:T(8,128)(2,1)}, bf16[256,1024]{1,0:T(8,128)(2,1)}, u32[]{:S(2)}, u32[]{:S(2)}) collective-permute-start(bf16[256,1024]{1,0:T(8,128)(2,1)} %get-tuple-element.97), channel_id=1, source_target_pairs={{0,1},{1,0},{2,3},{3,2},{4,5},{5,4},{6,7},{7,6},{8,9},{9,8},{10,11... | collective-permute-start | bytes 1572872 | tf_op jit(solution)/shard_map/ppermute | solution.py:303
  58.4 51.3 %collective-permute-start.1 = (bf16[2,256,1024]{2,1,0:T(8,128)(2,1)}, bf16[2,256,1024]{2,1,0:T(8,128)(2,1)}, u32[]{:S(2)}, u32[]{:S(2)}) collective-permute-start(bf16[2,256,1024]{2,1,0:T(8,128)(2,1)} %maximum_select_fusion.4), channel_id=1, source_target_pairs={{0,1},{1,0},{2,3},{3,2},{4,5},{5,4},{6,7},{7,6},{8,9},{9,8},{10,11... | collective-permute-start | bytes 3145736 | tf_op jit(solution)/shard_map/ppermute | solution.py:303
  62.3 49.5 %collective-permute-start.3 = (bf16[2,256,1024]{2,1,0:T(8,128)(2,1)}, bf16[2,256,1024]{2,1,0:T(8,128)(2,1)}, u32[]{:S(2)}, u32[]{:S(2)}) collective-permute-start(bf16[2,256,1024]{2,1,0:T(8,128)(2,1)} %maximum_select_fusion.6), channel_id=1, source_target_pairs={{0,2},{1,3},{2,0},{3,1},{4,6},{5,7},{6,4},{7,5},{8,10},{9,11},{10,... | collective-permute-start | bytes 3145736 | tf_op jit(solution)/shard_map/ppermute | solution.py:303
  65.6 42.0 %collective-permute-start.7 = (bf16[256,1024]{1,0:T(8,128)(2,1)}, bf16[256,1024]{1,0:T(8,128)(2,1)S(1)}, u32[]{:S(2)}, u32[]{:S(2)}) collective-permute-start(bf16[256,1024]{1,0:T(8,128)(2,1)} %get-tuple-element.91), channel_id=1, source_target_pairs={{0,1},{1,0},{2,3},{3,2},{4,5},{5,4},{6,7},{7,6},{8,9},{9,8},{10,11... | collective-permute-start | bytes 1572872 | tf_op jit(solution)/shard_map/ppermute | solution.py:303
  66.2 33.9 %collective-permute-start.5 = (bf16[256,1024]{1,0:T(8,128)(2,1)}, bf16[256,1024]{1,0:T(8,128)(2,1)S(1)}, u32[]{:S(2)}, u32[]{:S(2)}) collective-permute-start(bf16[256,1024]{1,0:T(8,128)(2,1)} %get-tuple-element.92), channel_id=1, source_target_pairs={{0,2},{1,3},{2,0},{3,1},{4,6},{5,7},{6,4},{7,5},{8,10},{9,11},{10,... | collective-permute-start | bytes 1572872 | tf_op jit(solution)/shard_map/ppermute | solution.py:303
  67.9 68.9 %all-to-all-start.2 = ((bf16[8,64,1280]{2,1,0:T(8,128)(2,1)}), bf16[8,64,1280]{2,1,0:T(8,128)(2,1)S(1)}, u32[]{:S(2)}, u32[]{:S(2)}) async-start(bf16[8,64,1280]{2,1,0:T(8,128)(2,1)} %pad_maximum_fusion.6), calls=%async_computation.2 | async-start | bytes 2621440 | tf_op jit(solution)/shard_map/all_to_all | solution.py:354
  71.7 168.4 %all-gather.9.cloned.1.call-start = ((), (), s32[]{:S(2)}) async-start(), calls=%async_computation.13 | async-start | bytes 3932160 | tf_op jit(solution)/shard_map/all_gather | solution.py:357
  71.7 28.4 %copy-start.50 = (bf16[1,256,1024]{2,1,0:T(8,128)(2,1)S(1)}, bf16[1,256,1024]{2,1,0:T(8,128)(2,1)}, u32[]{:S(2)}) copy-start(bf16[1,256,1024]{2,1,0:T(8,128)(2,1)} %get-tuple-element.88) | copy-start | bytes 1572868
  73.2 34.5 %copy-start.49 = (bf16[1,256,1024]{2,1,0:T(8,128)(2,1)S(1)}, bf16[1,256,1024]{2,1,0:T(8,128)(2,1)}, u32[]{:S(2)}) copy-start(bf16[1,256,1024]{2,1,0:T(8,128)(2,1)} %get-tuple-element.90) | copy-start | bytes 1572868
  100.3 30.0 %collective-permute-start.6 = (bf16[2,256,1024]{2,1,0:T(8,128)(2,1)S(1)}, bf16[2,256,1024]{2,1,0:T(8,128)(2,1)S(1)}, u32[]{:S(2)}, u32[]{:S(2)}) collective-permute-start(bf16[2,256,1024]{2,1,0:T(8,128)(2,1)S(1)} %maximum_select_fusion.8), channel_id=1, source_target_pairs={{0,1},{1,0},{2,3},{3,2},{4,5},{5,4},{6,7},{7,6},{8,9},{9,8},{10,11... | collective-permute-start | bytes 3145736 | tf_op jit(solution)/shard_map/ppermute | solution.py:303
  107.8 26.0 %collective-permute-start.8 = (bf16[2,256,1024]{2,1,0:T(8,128)(2,1)S(1)}, bf16[2,256,1024]{2,1,0:T(8,128)(2,1)S(1)}, u32[]{:S(2)}, u32[]{:S(2)}) collective-permute-start(bf16[2,256,1024]{2,1,0:T(8,128)(2,1)S(1)} %maximum_select_fusion.10), channel_id=1, source_target_pairs={{0,2},{1,3},{2,0},{3,1},{4,6},{5,7},{6,4},{7,5},{8,10},{9,11},{10,... | collective-permute-start | bytes 3145736 | tf_op jit(solution)/shard_map/ppermute | solution.py:303
  116.2 37.1 %collective-permute-start.4 = (bf16[1024,2048]{1,0:T(8,128)(2,1)}, bf16[1024,2048]{1,0:T(8,128)(2,1)}, u32[]{:S(2)}, u32[]{:S(2)}) collective-permute-start(bf16[1024,2048]{1,0:T(8,128)(2,1)} %pad_maximum_fusion.own_ref), channel_id=1, source_target_pairs={{0,4},{4,0},{8,12},{12,8},{16,20},{20,16},{24,28},{28,24},{1,5},{5... | collective-permute-start | bytes 12582920 | tf_op jit(solution)/shard_map/ppermute | solution.py:306
  136.6 27.9 %collective-permute-start.9 = (bf16[1024,2048]{1,0:T(8,128)(2,1)}, bf16[1024,2048]{1,0:T(8,128)(2,1)}, u32[]{:S(2)}, u32[]{:S(2)}) collective-permute-start(bf16[1024,2048]{1,0:T(8,128)(2,1)} %pad_maximum_fusion.1.own_ref), channel_id=1, source_target_pairs={{0,4},{4,0},{8,12},{12,8},{16,20},{20,16},{24,28},{28,24},{1,5},{5... | collective-permute-start | bytes 12582920 | tf_op jit(solution)/shard_map/ppermute | solution.py:306
  138.5 12.1 %all-to-all-start = ((f32[32,1,896]{2,1,0:T(1,128)}), f32[32,1,896]{2,1,0:T(1,128)S(1)}, u32[]{:S(2)}, u32[]{:S(2)}) async-start(f32[32,1,896]{2,1,0:T(1,128)} %broadcast_in_dim.101), calls=%async_computation | async-start | bytes 229376 | tf_op jit(solution)/shard_map/all_to_all | solution.py:440
  142.5 186.6 %all-gather.11.cloned.1.call-start = ((), (), s32[]{:S(2)}) async-start(), calls=%async_computation.14 | async-start | bytes 5242880 | tf_op jit(solution)/shard_map/all_gather | solution.py:357
  197.2 224.3 %reduce-scatter.7.cloned.1.call-start = ((), (), s32[]{:S(2)}) async-start(), calls=%async_computation.16 | async-start | bytes 5242880 | tf_op jit(solution)/shard_map/reduce_scatter | solution.py:360
  233.6 205.6 %reduce-scatter.5.cloned.1.call-start = ((), (), s32[]{:S(2)}) async-start(), calls=%async_computation.15 | async-start | bytes 5242880 | tf_op jit(solution)/shard_map/reduce_scatter | solution.py:360
  262.7 22.4 %copy-start.2 = (f32[1024,128]{1,0:T(8,128)S(1)}, f32[1024,128]{1,0:T(8,128)}, u32[]{:S(2)}) copy-start(f32[1024,128]{1,0:T(8,128)} %get-tuple-element.79.sin_ref) | copy-start | bytes 1572868
  262.7 22.4 %copy-start.3 = (f32[1024,128]{1,0:T(8,128)S(1)}, f32[1024,128]{1,0:T(8,128)}, u32[]{:S(2)}) copy-start(f32[1024,128]{1,0:T(8,128)} %get-tuple-element.81.cos_ref) | copy-start | bytes 1572868
  262.7 44.8 %slice-start = ((s8[8388608]{0:T(1024)(128)(4,1)}), s8[4194304]{0:T(1024)(128)(4,1)S(1)}, s32[]{:S(2)}) async-start(s8[8388608]{0:T(1024)(128)(4,1)} %bitcast.224), calls=%async_computation.19 | async-start | bytes 8388608
  285.0 22.5 %slice-start.1 = ((s8[8388608]{0:T(1024)(128)(4,1)}), s8[4194304]{0:T(1024)(128)(4,1)S(1)}, s32[]{:S(2)}) async-start(s8[8388608]{0:T(1024)(128)(4,1)} %bitcast.224), calls=%async_computation.20 | async-start | bytes 8388608
  329.0 170.0 %reduce-scatter.11.cloned.1.call-start = ((), (), s32[]{:S(2)}) async-start(), calls=%async_computation.18 | async-start | bytes 2621440 | tf_op jit(solution)/shard_map/reduce_scatter | solution.py:360
  334.6 17.8 %slice-start.2 = ((s8[8388608]{0:T(1024)(128)(4,1)}), s8[4194304]{0:T(1024)(128)(4,1)S(1)}, s32[]{:S(2)}) async-start(s8[8388608]{0:T(1024)(128)(4,1)} %bitcast.226), calls=%async_computation.21 | async-start | bytes 8388608
  336.6 15.8 %slice-start.3 = ((s8[8388608]{0:T(1024)(128)(4,1)}), s8[4194304]{0:T(1024)(128)(4,1)S(1)}, s32[]{:S(2)}) async-start(s8[8388608]{0:T(1024)(128)(4,1)} %bitcast.226), calls=%async_computation.22 | async-start | bytes 8388608
  351.1 16.8 %copy-start.16 = (bf16[2048,512]{1,0:T(8,128)(2,1)}, bf16[2048,512]{1,0:T(8,128)(2,1)S(1)}, u32[]{:S(2)}) copy-start(bf16[2048,512]{1,0:T(8,128)(2,1)S(1)} %get-tuple-element.50.refs_2_) | copy-start | bytes 6291460
  358.2 193.2 %reduce-scatter.9.cloned.1.call-start = ((), (), s32[]{:S(2)}) async-start(), calls=%async_computation.17 | async-start | bytes 2621440 | tf_op jit(solution)/shard_map/reduce_scatter | solution.py:360
  370.0 13.1 %copy-start.22 = (bf16[1,256,2048]{2,1,0:T(8,128)(2,1)S(1)}, bf16[1,256,2048]{2,1,0:T(8,128)(2,1)}, u32[]{:S(2)}) copy-start(bf16[1,256,2048]{2,1,0:T(8,128)(2,1)} %param.13) | copy-start | bytes 3145732
  370.0 13.3 %copy-start.9 = (bf16[2048,512]{1,0:T(8,128)(2,1)S(1)}, bf16[2048,512]{1,0:T(8,128)(2,1)}, u32[]{:S(2)}) copy-start(bf16[2048,512]{1,0:T(8,128)(2,1)} %copy-done.8) | copy-start | bytes 6291460
  382.9 58.6 %collective-permute-start.15 = (bf16[1024,2048]{1,0:T(8,128)(2,1)}, bf16[1024,2048]{1,0:T(8,128)(2,1)}, u32[]{:S(2)}, u32[]{:S(2)}) collective-permute-start(bf16[1024,2048]{1,0:T(8,128)(2,1)} %shard_map.179), channel_id=1, source_target_pairs={{0,4},{4,0},{8,12},{12,8},{16,20},{20,16},{24,28},{28,24},{1,5},{5... | collective-permute-start | bytes 12582920 | tf_op jit(solution)/shard_map/ppermute | solution.py:306
  393.7 58.9 %collective-permute-start.10 = (bf16[1024,2048]{1,0:T(8,128)(2,1)}, bf16[1024,2048]{1,0:T(8,128)(2,1)}, u32[]{:S(2)}, u32[]{:S(2)}) collective-permute-start(bf16[1024,2048]{1,0:T(8,128)(2,1)} %shard_map.177), channel_id=1, source_target_pairs={{0,4},{4,0},{8,12},{12,8},{16,20},{20,16},{24,28},{28,24},{1,5},{5... | collective-permute-start | bytes 12582920 | tf_op jit(solution)/shard_map/ppermute | solution.py:306
  424.8 33.9 %all-to-all-start.5 = ((bf16[8,64,512]{2,1,0:T(8,128)(2,1)}), bf16[8,64,512]{2,1,0:T(8,128)(2,1)S(1)}, u32[]{:S(2)}, u32[]{:S(2)}) async-start(bf16[8,64,512]{2,1,0:T(8,128)(2,1)} %bitcast.101), calls=%async_computation.7 | async-start | bytes 1048576 | tf_op jit(solution)/shard_map/all_to_all | solution.py:354
  448.6 52.5 %collective-permute-start.18 = (bf16[2,256,1024]{2,1,0:T(8,128)(2,1)}, bf16[2,256,1024]{2,1,0:T(8,128)(2,1)}, u32[]{:S(2)}, u32[]{:S(2)}) collective-permute-start(bf16[2,256,1024]{2,1,0:T(8,128)(2,1)} %dynamic-slice_bitcast_fusion), channel_id=1, source_target_pairs={{0,2},{1,3},{2,0},{3,1},{4,6},{5,7},{6,4},{7,5},{8,10},{9,11},{10,... | collective-permute-start | bytes 3145736 | tf_op jit(solution)/shard_map/ppermute | solution.py:303
  451.2 52.7 %collective-permute-start.16 = (bf16[2,256,1024]{2,1,0:T(8,128)(2,1)}, bf16[2,256,1024]{2,1,0:T(8,128)(2,1)}, u32[]{:S(2)}, u32[]{:S(2)}) collective-permute-start(bf16[2,256,1024]{2,1,0:T(8,128)(2,1)} %dynamic-slice_bitcast_fusion.1), channel_id=1, source_target_pairs={{0,1},{1,0},{2,3},{3,2},{4,5},{5,4},{6,7},{7,6},{8,9},{9,8},{10,11... | collective-permute-start | bytes 3145736 | tf_op jit(solution)/shard_map/ppermute | solution.py:303
  458.8 26.6 %all-to-all-start.4 = ((bf16[8,64,768]{2,1,0:T(8,128)(2,1)}), bf16[8,64,768]{2,1,0:T(8,128)(2,1)}, u32[]{:S(2)}, u32[]{:S(2)}) async-start(bf16[8,64,768]{2,1,0:T(8,128)(2,1)} %bitcast.97), calls=%async_computation.5 | async-start | bytes 1572864 | tf_op jit(solution)/shard_map/all_to_all | solution.py:354
  468.3 38.1 %collective-permute-start.13 = (bf16[2,256,1024]{2,1,0:T(8,128)(2,1)}, bf16[2,256,1024]{2,1,0:T(8,128)(2,1)}, u32[]{:S(2)}, u32[]{:S(2)}) collective-permute-start(bf16[2,256,1024]{2,1,0:T(8,128)(2,1)} %dynamic-slice_bitcast_fusion.2), channel_id=1, source_target_pairs={{0,2},{1,3},{2,0},{3,1},{4,6},{5,7},{6,4},{7,5},{8,10},{9,11},{10,... | collective-permute-start | bytes 3145736 | tf_op jit(solution)/shard_map/ppermute | solution.py:303
  497.5 26.3 %collective-permute-start.11 = (bf16[2,256,1024]{2,1,0:T(8,128)(2,1)}, bf16[2,256,1024]{2,1,0:T(8,128)(2,1)}, u32[]{:S(2)}, u32[]{:S(2)}) collective-permute-start(bf16[2,256,1024]{2,1,0:T(8,128)(2,1)} %dynamic-slice_bitcast_fusion.3), channel_id=1, source_target_pairs={{0,1},{1,0},{2,3},{3,2},{4,5},{5,4},{6,7},{7,6},{8,9},{9,8},{10,11... | collective-permute-start | bytes 3145736 | tf_op jit(solution)/shard_map/ppermute | solution.py:303
  503.3 31.7 %collective-permute-start.19 = (bf16[256,1024]{1,0:T(8,128)(2,1)S(1)}, bf16[256,1024]{1,0:T(8,128)(2,1)S(1)}, u32[]{:S(2)}, u32[]{:S(2)}) collective-permute-start(bf16[256,1024]{1,0:T(8,128)(2,1)S(1)} %dynamic-slice_bitcast_fusion.4), channel_id=1, source_target_pairs={{0,1},{1,0},{2,3},{3,2},{4,5},{5,4},{6,7},{7,6},{8,9},{9,8},{10,11... | collective-permute-start | bytes 1572872 | tf_op jit(solution)/shard_map/ppermute | solution.py:303
  505.6 29.5 %collective-permute-start.17 = (bf16[256,1024]{1,0:T(8,128)(2,1)S(1)}, bf16[256,1024]{1,0:T(8,128)(2,1)S(1)}, u32[]{:S(2)}, u32[]{:S(2)}) collective-permute-start(bf16[256,1024]{1,0:T(8,128)(2,1)S(1)} %dynamic-slice_bitcast_fusion.5), channel_id=1, source_target_pairs={{0,2},{1,3},{2,0},{3,1},{4,6},{5,7},{6,4},{7,5},{8,10},{9,11},{10,... | collective-permute-start | bytes 1572872 | tf_op jit(solution)/shard_map/ppermute | solution.py:303
  508.0 17.4 %copy-start.32 = (bf16[2,256,1024]{2,1,0:T(8,128)(2,1)}, bf16[2,256,1024]{2,1,0:T(8,128)(2,1)S(1)}, u32[]{:S(2)}) copy-start(bf16[2,256,1024]{2,1,0:T(8,128)(2,1)S(1)} %fusion.15) | copy-start | bytes 3145732
  509.0 36.5 %collective-permute-start.14 = (bf16[256,1024]{1,0:T(8,128)(2,1)}, bf16[256,1024]{1,0:T(8,128)(2,1)}, u32[]{:S(2)}, u32[]{:S(2)}) collective-permute-start(bf16[256,1024]{1,0:T(8,128)(2,1)} %dynamic-slice_bitcast_fusion.6), channel_id=1, source_target_pairs={{0,1},{1,0},{2,3},{3,2},{4,5},{5,4},{6,7},{7,6},{8,9},{9,8},{10,11... | collective-permute-start | bytes 1572872 | tf_op jit(solution)/shard_map/ppermute | solution.py:303
  526.4 20.4 %collective-permute-start.12 = (bf16[256,1024]{1,0:T(8,128)(2,1)}, bf16[256,1024]{1,0:T(8,128)(2,1)}, u32[]{:S(2)}, u32[]{:S(2)}) collective-permute-start(bf16[256,1024]{1,0:T(8,128)(2,1)} %dynamic-slice_bitcast_fusion.7), channel_id=1, source_target_pairs={{0,2},{1,3},{2,0},{3,1},{4,6},{5,7},{6,4},{7,5},{8,10},{9,11},{10,... | collective-permute-start | bytes 1572872 | tf_op jit(solution)/shard_map/ppermute | solution.py:303
  537.5 13.8 %all-to-all-start.3 = ((f32[32,1,640]{2,1,0:T(1,128)}), f32[32,1,640]{2,1,0:T(1,128)S(1)}, u32[]{:S(2)}, u32[]{:S(2)}) async-start(f32[32,1,640]{2,1,0:T(1,128)} %all_to_all.31), calls=%async_computation.4 | async-start | bytes 163840 | tf_op jit(solution)/shard_map/all_to_all | solution.py:594
  551.3 12.9 %all-to-all-start.6 = ((bf16[8,64,512]{2,1,0:T(8,128)(2,1)}), bf16[8,64,512]{2,1,0:T(8,128)(2,1)S(1)}, u32[]{:S(2)}, u32[]{:S(2)}) async-start(bf16[8,64,512]{2,1,0:T(8,128)(2,1)} %bitcast.285), calls=%async_computation.9 | async-start | bytes 1048576 | tf_op jit(solution)/shard_map/all_to_all | solution.py:354
  (53 other events, 258.7 us)
Sparse Core Ops, SparseCore 0:
  9.6 30.6 all-gather.4
  42.4 80.2 all-gather.6
  137.8 62.8 all-gather.8
  202.7 79.4 all-gather.10
  284.3 75.2 reduce-scatter.6
  361.9 77.2 reduce-scatter.4
  441.5 44.3 reduce-scatter.10
  488.3 43.1 reduce-scatter.8

commit v3 on v2

--- a/solution.py
+++ b/solution.py
@@ -201,7 +201,7 @@
 def hidden_layer(normed, grad, up, down, bias):
     tokens, width = normed.shape
     units = up.shape[1]
-    block = min(256, tokens)
+    block = min(512, tokens)
     rows = pl.BlockSpec((block, width), lambda i: (i, 0))
     part = pl.BlockSpec((block, units), lambda i: (i, 0))
 
@@ -233,7 +233,7 @@
 def heads_layer(normed, grad, weight, proj, bias):
     tokens, width = normed.shape
     columns, inner = weight.shape[1], proj.shape[0]
-    block = min(256, tokens)
+    block = min(512, tokens)
     rows = pl.BlockSpec((block, width), lambda i: (i, 0))
 
     def whole(shape):
@@ -265,7 +265,7 @@
 def joined_product(lefts, rights, dims, first, tokens):
     count = len(lefts)
     columns = rights[0].shape[1 if dims is NN else 0]
-    block = min(256, tokens)
+    block = min(512, tokens)
     steps = tokens // block
     rights_specs = [pl.BlockSpec(x.shape, lambda i, first: (0, 0)) for x in rights]
     return pl.pallas_call(
@@ -286,6 +286,32 @@
     )(first[None], *lefts, *rights)
 
 
+def pack_kernel(main_ref, extra_ref, out_ref):
+    main, few = main_ref.shape[2], extra_ref.shape[1]
+    columns = out_ref.shape[2] - main
+    out_ref[0, :, :main] = main_ref[0]
+    for i in range(extra_ref.shape[2] // columns):
+        out_ref[0, i * few : (i + 1) * few, main:] = extra_ref[0, :, i * columns : (i + 1) * columns]
+
+
+def pack(main, extra):
+    lead, rows, columns = main.shape
+    total = columns + extra.shape[1] * extra.shape[2] // rows
+
+    def block(x):
+        return pl.BlockSpec((1,) + x[1:], lambda i: (i, 0, 0))
+
+    return pl.pallas_call(
+        pack_kernel,
+        grid=(lead,),
+        in_specs=[block(main.shape), block(extra.shape)],
+        out_specs=block((lead, rows, total)),
+        out_shape=jax.ShapeDtypeStruct((lead, rows, total), bf16),
+        compiler_params=params(),
+        cost_estimate=pl.CostEstimate(flops=0, bytes_accessed=4 * lead * rows * total, transcendentals=0),
+    )(main, extra)
+
+
 def after(x, *others):
     if not others:
         return x
@@ -311,7 +337,7 @@
     def two(flag, mine, theirs, axis):
         return jnp.where(flag == 0, jnp.stack([mine, theirs], axis), jnp.stack([theirs, mine], axis))
 
-    def gather_plane(x, core, seq):
+    def gather_plane(x, core, seq, *others):
         if n_seq != 4:
             whole = lax.all_gather(x, BOTH, axis_index_groups=plane_groups, axis=0, tiled=True)
             whole = whole.reshape((CORES, n_seq * x.shape[0]) + x.shape[1:])
@@ -322,6 +348,7 @@
         left = two(bit_y, left, seq_permute(left, 2), 0)
         right = two(bit_x, right, seq_permute(right, 1), 0)
         early = left
+        left = after(left, *others)
         left = two(bit_x, left, seq_permute(left, 1), 1)
         right = two(bit_y, right, seq_permute(right, 2), 0)
         own = jnp.concatenate([left, right], axis=3).reshape(4 * x.shape[0], x.shape[1])
@@ -330,9 +357,10 @@
     def scatter_plane(product, tokens, core, seq):
         if n_seq != 4:
             both = [product(core ^ i) for i in range(CORES)]
-            return lax.psum_scatter(
+            x = lax.psum_scatter(
                 jnp.concatenate(both), BOTH, axis_index_groups=plane_groups, scatter_dimension=0, tiled=True
             ).astype(f32)
+            return x, (x, x, x)
         other = core_permute(product(jnp.int32(1)))
         x = product(jnp.int32(0)).astype(f32) + other.astype(f32)
         x = x.astype(bf16).reshape(2, 2, tokens // n_seq, x.shape[1])
@@ -346,9 +374,10 @@
         right = (take(right, bit_y).astype(f32) + from_y.astype(f32)).astype(bf16)
         from_y = seq_permute(take(left, 1 - bit_y), 2)
         from_x = seq_permute(take(right, 1 - bit_x), 1)
+        stages = (x, left, right)
         left = take(left, bit_y).astype(f32) + from_y.astype(f32)
         right = take(right, bit_x).astype(f32) + from_x.astype(f32)
-        return jnp.concatenate([left, right], axis=1)
+        return jnp.concatenate([left, right], axis=1), stages
 
     def swap_plane(x):
         return lax.all_to_all(x, BOTH, 0, 0, axis_index_groups=plane_groups, tiled=True)
@@ -426,14 +455,12 @@
         def swap_columns(x):
             return swap_plane(x).reshape(ranks * in_rows, x.shape[2])
 
-        hidden_send = [swap_columns(split_hidden(in_weight[:, 3 * width :], 0))]
-        later = [split_heads(in_weight[:, : 3 * width])]
-        later += [split_hidden(in_weight[:, 3 * width :], c) for c in range(1, chunks)]
-        later = swap_columns(after(jnp.concatenate(later, axis=2), hidden_send[0]))
-        heads_send = later[:, : 3 * mine_cols]
-        for c in range(1, chunks):
-            at = 3 * mine_cols + (c - 1) * planes * part
-            hidden_send.append(later[:, at : at + planes * part])
+        units = planes * part
+        first_send = swap_columns(
+            jnp.concatenate(
+                [split_hidden(in_weight[:, 3 * width :], 0), split_heads(in_weight[:, : 3 * width])], axis=2
+            )
+        )
         token_halves = gather_plane(tokens[0], core, seq)
         grad_halves = gather_plane(after(cotangent[0], token_halves[2]), core, seq)
         small = jnp.concatenate([x.astype(f32) for x in (in_bias, ln_gain, ln_bias, out_bias, positions[0])])
@@ -462,12 +489,6 @@
             return swap_plane(x.reshape(ranks, in_rows, x.shape[1]))
 
         own_parts = []
-        def pack(main, extra):
-            lead, few = extra.shape[:2]
-            columns = few * width // main.shape[1]
-            extra = extra.reshape(lead, few, width // columns, columns)
-            return jnp.concatenate([main, jnp.swapaxes(extra, 1, 2).reshape(lead, -1, columns)], axis=2)
-
         def unpack(x, few):
             lead, packed, total = x.shape
             columns = few * width // packed
@@ -486,12 +507,11 @@
 
         normed = over_both(norm_kernel, *token_halves[:2], gain_all, shift_all)
         grad_all = over_both(join_kernel, *grad_halves[:2])
-        def gather_hidden(c, *others):
-            x = pack(hidden_send[c][None], down_weight[None, c * part : (c + 1) * part])[0]
-            x = gather_line(after(x, *others)).reshape(planes, ranks * in_rows, -1)
-            x, y = unpack(x, part)
-            w_hidden[c], down[c] = x.reshape(width, -1), y.reshape(-1, width)
-            return w_hidden[c]
+        def gather_packed(main, c, *others):
+            x = pack(main[None], down_weight[None, c * part : (c + 1) * part])[0]
+            x = gather_line(after(x, *others))
+            down[c] = unpack(x.reshape(planes, ranks * in_rows, -1), part)[1].reshape(-1, width)
+            return x
 
         if whole_heads:
             proj = gather_line(proj_weight)
@@ -499,8 +519,11 @@
             proj = lax.dynamic_slice_in_dim(
                 lax.all_gather(proj_weight, BOTH, axis=0, tiled=True), rank * mine_cols, mine_cols, 0
             )
-        gather_hidden(0, proj)
-        w_heads = gather_line(after(heads_send, proj))
+        x = gather_packed(first_send, 0, proj)
+        w_hidden[0], w_heads = x[:, :units], x[:, units : units + 3 * mine_cols]
+        for c in range(1, chunks):
+            more = split_hidden(in_weight[:, 3 * width :], c)
+            w_hidden[c] = gather_packed(swap_columns(after(more, token_halves[0])), c, x, normed, grad_all)[:, :units]
         by_plane = (planes, width // planes, -1)
 
         def scatter_packed(main, extra, few):
@@ -509,25 +532,14 @@
             return x[0], y[0].astype(f32)
 
         to_hidden, to_down = hidden_part(0)
-        for c in range(1, chunks):
-            gather_hidden(c, w_hidden[0], activated[0])
         first, second = scatter_packed(to_hidden, to_down, part)
-        grad_hidden.append(first)
+        grad_hidden.append(own_columns(first))
         grad_down.append(second)
-        hop = ()
-        mixed, grad_attended = heads_layer(normed, after(grad_all, to_hidden, to_down, *hidden_send), w_heads, proj, bias_heads[0])
+        mixed, grad_attended = heads_layer(normed, after(grad_all, to_hidden, to_down), w_heads, proj, bias_heads[0])
         cosine, sine = rotary_wide(place)
         start = (jnp.arange(place.shape[0], dtype=jnp.int32) % length - place)[:, None]
-        attended, grad_mixed = [], []
-        for i in range(CORES):
-            rows_of = slice(i * length, (i + 1) * length)
-            a, m = attention(
-                mixed[rows_of], after(grad_attended[rows_of], *hop), cosine[rows_of], sine[rows_of], start[rows_of], length
-            )
-            attended.append(a)
-            grad_mixed.append(m)
-        attended, grad_mixed = jnp.concatenate(attended), jnp.concatenate(grad_mixed)
-        to_proj = dot(attended, after(grad_all, *hop), TN).astype(bf16)
+        attended, grad_mixed = attention(mixed, grad_attended, cosine, sine, start, length)
+        to_proj = dot(attended, grad_all, TN).astype(bf16)
         to_heads = dot(normed, grad_mixed, TN).astype(bf16)
         if whole_heads:
             grad_heads, grad_proj = scatter_packed(to_heads, to_proj, proj_rows)
@@ -542,20 +554,21 @@
 
         last = []
         for c in range(1, chunks):
-            to_hidden, to_down = hidden_part(c, to_heads, to_proj)
-            last += [to_hidden, to_down]
-            grad_hidden.append(scatter_line(to_hidden))
-            grad_down.append(scatter_line(to_down).astype(f32))
+            last += hidden_part(c, to_heads, to_proj)
         bias_heads_sum = jnp.sum(grad_mixed.astype(f32), axis=0)
-        attended, grad_mixed = after(attended, *last), after(grad_mixed, *last)
-        out = scatter_plane(
+        grad_mixed = after(grad_mixed, *last)
+        grad_normed, stages = scatter_plane(
+            lambda i: joined_product([grad_mixed] + grad_u, [w_heads] + w_hidden, NT, i, length), length, core, seq
+        )
+        attended = after(attended, *last, stages[0], grad_hidden[0])
+        out, more = scatter_plane(
             lambda i: joined_product([attended] + activated, [proj] + down, NN, i, length), length, core, seq
         )
-        grad_normed = scatter_plane(
-            lambda i: joined_product([grad_mixed] + grad_u, [w_heads] + w_hidden, NT, i, length), length, core, seq
-        )
-
-        grad_normed = after(grad_normed, grad_proj, grad_heads)
+        for c in range(1, chunks):
+            to_hidden, to_down = last[2 * c - 2 : 2 * c]
+            grad_hidden.append(scatter_line(after(to_hidden, stages[0])))
+            grad_down.append(scatter_line(after(to_down, *stages, grad_hidden[c])).astype(f32))
+
         own = tokens[0].astype(f32)
         own_grad = cotangent[0].astype(f32)
         result = own + out + out_bias_all
@@ -594,7 +607,7 @@
         sums = jnp.sum(lax.all_to_all(sums, BOTH, 0, 0, tiled=True), axis=0)
 
         grad_in = jnp.concatenate(
-            [join_heads(own_columns(grad_heads)), join_hidden([own_columns(x) for x in grad_hidden])], axis=1
+            [join_heads(own_columns(grad_heads)), join_hidden(grad_hidden[:1] + [own_columns(x) for x in grad_hidden[1:]])], axis=1
         ).astype(f32)
         return (
             result.astype(bf16)[None],

time: 587 us -> 568 us (0.968)
  local copies, waits for them, and re-layouts: 117 us -> 88.8 us
  waiting for transfers between devices: 119 us -> 140 us
  other arithmetic: 70.1 us -> 59.7 us
  starting transfers between devices: 55.4 us -> 49 us
    all_to_all x5, waiting for transfers between devices: 14.3 us -> 32.2 us  [swap_plane(): lax.all_to_all(x, BOTH, 0, 0, axis_index_groups=plane_groups, tiled=True)]
    another operation x5 -> x0, local copies, waits for them, and re-layouts: 12.7 us -> none  [pack(): extra = extra.reshape(lead, few, width // columns, columns)]
    all_gather x4 -> x3, waiting for transfers between devices: 11 us -> 0.02 us  [gather_line(): lax.all_gather(x, 'batch', axis_index_groups=line_groups, axis=0, tiled=T...]
    ppermute x16, waiting for transfers between devices: 74.8 us -> 84.3 us  [seq_permute(): return lax.ppermute(x, 'seq', [(s, s ^ bit) for s in range(n_seq)])]
    ppermute x16, starting transfers between devices: 25.6 us -> 16.9 us  [seq_permute(): return lax.ppermute(x, 'seq', [(s, s ^ bit) for s in range(n_seq)])]
    pallas_call x0 -> x4, Pallas kernels: none -> 7.59 us  [pack(): pl.pallas_call(pack_kernel, grid=(lead,), in_specs=[block(main.shape), bl...]
    concatenate x4 -> x1, local copies, waits for them, and re-layouts: 6.99 us -> 0.36 us  [shards(): place = jnp.concatenate([take(place, core), take(place, 1 - core)])]
    unnamed x137 -> x101, local copies, waits for them, and re-layouts: 23.2 us -> 18.3 us
  transfers between devices with their start and end apart: 35 -> 34, of which waited for: 12 -> 16; matrix products, arithmetic and copies ran while one was open for 37% -> 32% of each run, Pallas kernels for 27% -> 28%
where the time goes in v3:
time: 568 us; the launch traced here: 558 us
  Pallas kernels  159 us (28%)
  waiting for transfers between devices  140 us (25%)
  local copies, waits for them, and re-layouts  88.8 us (16%)
  other arithmetic  59.7 us (11%)
  starting transfers between devices  49 us (9%)
  matrix products  45.9 us (8%)
  between operations  15.5 us (3%)
    ppermute x16, waiting for transfers between devices, seq_permute(): return lax.ppermute(x, 'seq', [(s, s ^ bit) for s in range(n_seq)])  84.3 us
    dot_general x6, matrix products, dot(): lax.dot_general(left, right, (dims, ((), ())), preferred_element_type=f32)  45.9 us
    pallas_call x4, Pallas kernels, joined_product(): pl.pallas_call(functools.partial(joined_kernel, count, dims), grid_spec=p...  45.3 us
    pallas_call x1, Pallas kernels, attention(): pl.pallas_call(functools.partial(attention_kernel, min(256, length)), gri...  43.3 us
    all_to_all x5, waiting for transfers between devices, swap_plane(): lax.all_to_all(x, BOTH, 0, 0, axis_index_groups=plane_groups, tiled=True)  32.2 us
    pallas_call x2, Pallas kernels, hidden_layer(): pl.pallas_call(hidden_kernel, grid=(tokens // block,), in_specs=[rows, ro...  27 us
    all_to_all x5, starting transfers between devices, swap_plane(): lax.all_to_all(x, BOTH, 0, 0, axis_index_groups=plane_groups, tiled=True)  21.1 us
    pallas_call x2, Pallas kernels, over_both(): pl.pallas_call(functools.partial(kernel, steps), grid=(2 * steps,), in_sp...  20.9 us
  transfers between devices with their start and end apart: 34, of which 16 were waited for; matrix products, arithmetic and copies ran while one was open for 32% of the time, Pallas kernels for 28%

profile of v3, /device:TPU:0, one launch (start us, length us, event | category | flops | bytes accessed | tf_op | source)
XLA Modules:
  0.0 557.8 jit_solution(12874026448577737064)
XLA Ops:
  20.9 5.3 all-to-all-start.1
  26.4 17.5 %all-to-all-done.1 = bf16[8,64,1280]{2,1,0:T(8,128)(2,1)S(1)} async-done(((bf16[8,64,1280]{2,1,0:T(8,128)(2,1)}), bf16[8,64,1280]{2,1,0:T(8,128)(2,1)S(1)}, u32[]{:S(2)}, u32[]{:S(2)}) %all-to-all-start.1) | async-done | bytes 1310752 | tf_op jit(solution)/shard_map/all_to_all | solution.py:383
  48.9 12.7 %collective-permute-done = bf16[256,1024]{1,0:T(8,128)(2,1)S(1)} collective-permute-done((bf16[256,1024]{1,0:T(8,128)(2,1)}, bf16[256,1024]{1,0:T(8,128)(2,1)S(1)}, u32[]{:S(2)}, u32[]{:S(2)}) %collective-permute-start) | collective-permute-done | bytes 524320 | tf_op jit(solution)/shard_map/ppermute | solution.py:329
  73.0 7.9 %collective-permute-done.5 = bf16[256,1024]{1,0:T(8,128)(2,1)S(1)} collective-permute-done((bf16[256,1024]{1,0:T(8,128)(2,1)}, bf16[256,1024]{1,0:T(8,128)(2,1)S(1)}, u32[]{:S(2)}, u32[]{:S(2)}) %collective-permute-start.5) | collective-permute-done | bytes 524320 | tf_op jit(solution)/shard_map/ppermute | solution.py:329
  81.9 21.8 %collective-permute-done.7 = bf16[256,1024]{1,0:T(8,128)(2,1)S(1)} collective-permute-done((bf16[256,1024]{1,0:T(8,128)(2,1)}, bf16[256,1024]{1,0:T(8,128)(2,1)S(1)}, u32[]{:S(2)}, u32[]{:S(2)}) %collective-permute-start.7) | collective-permute-done | bytes 524320 | tf_op jit(solution)/shard_map/ppermute | solution.py:329
  108.4 2.5 pad_maximum_fusion.own_ref
  110.9 13.5 %collective-permute-done.6 = bf16[2,256,1024]{2,1,0:T(8,128)(2,1)S(1)} collective-permute-done((bf16[2,256,1024]{2,1,0:T(8,128)(2,1)S(1)}, bf16[2,256,1024]{2,1,0:T(8,128)(2,1)S(1)}, u32[]{:S(2)}, u32[]{:S(2)}) %collective-permute-start.6) | collective-permute-done | bytes 1048608 | tf_op jit(solution)/shard_map/ppermute | solution.py:329
  126.1 2.4 pad_maximum_fusion.1.own_ref
  129.4 5.3 all-to-all-start
  135.9 12.1 %all-to-all-done = f32[32,1,896]{2,1,0:T(1,128)S(1)} async-done(((f32[32,1,896]{2,1,0:T(1,128)}), f32[32,1,896]{2,1,0:T(1,128)S(1)}, u32[]{:S(2)}, u32[]{:S(2)}) %all-to-all-start) | async-done | bytes 114720 | tf_op jit(solution)/shard_map/all_to_all | solution.py:467
  148.0 3.5 all-to-all-start.2
  152.6 8.1 %all-to-all-done.2 = bf16[8,64,512]{2,1,0:T(8,128)(2,1)S(1)} async-done(((bf16[8,64,512]{2,1,0:T(8,128)(2,1)}), bf16[8,64,512]{2,1,0:T(8,128)(2,1)S(1)}, u32[]{:S(2)}, u32[]{:S(2)}) %all-to-all-start.2) | async-done | bytes 524320 | tf_op jit(solution)/shard_map/all_to_all | solution.py:383
  161.8 11.3 %shard_map.169.normed_ref = bf16[2048,2048]{1,0:T(8,128)(2,1)} custom-call(bf16[1024,2048]{1,0:T(8,128)(2,1)} %pad_maximum_fusion.own_ref, bf16[1024,2048]{1,0:T(8,128)(2,1)} %collective-permute-done.4.other_ref, f32[1,2048]{1,0:T(1,128)S(1)} %broadcast_in_dim_reshape.14.gain_ref, f32[1,2048]{1,0:T(1,128)S(1)} %broadcast_in_dim_reshape.15.shift_ref), custom_call_target="tpu_custom_call" | custom-call | flops 33554432 | bytes 16777216 | tf_op jit(solution)/shard_map/pallas_call | solution.py:171
  173.1 9.6 %shard_map.170.grad_ref = bf16[2048,2048]{1,0:T(8,128)(2,1)} custom-call(bf16[1024,2048]{1,0:T(8,128)(2,1)} %pad_maximum_fusion.1.own_ref, bf16[1024,2048]{1,0:T(8,128)(2,1)} %collective-permute-done.9.other_ref), custom_call_target="tpu_custom_call" | custom-call | flops 33554432 | bytes 16777216 | tf_op jit(solution)/shard_map/pallas_call | solution.py:171
  188.3 3.2 slice.151.up_ref.refs_4_
  191.4 13.2 %shard_map.172 = (bf16[2048,512]{1,0:T(8,128)(2,1)S(1)}, bf16[2048,512]{1,0:T(8,128)(2,1)S(1)}, f32[1,512]{1,0:T(1,128)S(1)}) custom-call(bf16[2048,2048]{1,0:T(8,128)(2,1)} %shard_map.169.normed_ref, bf16[2048,2048]{1,0:T(8,128)(2,1)} %shard_map.170.grad_ref, bf16[2048,512]{1,0:T(8,128)(2,1)} %slice.151.up_ref.refs_4_, bf16[512,2048]{1,0:T(8,128)(2,1)} %bitcast.259, ...), custom_call_target="tpu_custom_call" | custom-call | flops 8589934592 | bytes 16777216 | tf_op jit(solution)/shard_map/pallas_call | solution.py:211
  204.7 9.7 %convolution_convert_fusion.3 = bf16[512,2048]{1,0:T(8,128)(2,1)S(1)} fusion(bf16[2048,512]{1,0:T(8,128)(2,1)S(1)} %get-tuple-element.36.refs_1_, bf16[2048,2048]{1,0:T(8,128)(2,1)} %shard_map.170.grad_ref), kind=kOutput, calls=%fused_computation.11 | convolution fusion | flops 4296015872 | bytes 12582912 | tf_op jit(solution)/shard_map/dot_general | solution.py:24
  214.4 8.5 %convolution_convert_fusion.4 = bf16[2048,512]{1,0:T(8,128)(2,1)S(1)} fusion(bf16[2048,2048]{1,0:T(8,128)(2,1)} %shard_map.169.normed_ref, bf16[2048,512]{1,0:T(8,128)(2,1)S(1)} %get-tuple-element.35.refs_1_), kind=kOutput, calls=%fused_computation.12 | convolution fusion | flops 4296015872 | bytes 12582912 | tf_op jit(solution)/shard_map/dot_general | solution.py:24
  222.9 2.6 shard_map.179
  226.9 3.8 fusion.26
  232.9 14.6 %shard_map.173 = (f32[2048,768]{1,0:T(8,128)}, bf16[2048,256]{1,0:T(8,128)(2,1)S(1)}) custom-call(bf16[2048,2048]{1,0:T(8,128)(2,1)} %shard_map.169.normed_ref, bf16[2048,2048]{1,0:T(8,128)(2,1)} %shard_map.170.grad_ref, bf16[2048,768]{1,0:T(8,128)(2,1)S(1)} %slice.156.in_ref.refs_3_, bf16[256,2048]{1,0:T(8,128)(2,1)S(1)} %copy-done.1, ...), custom_call_target="tpu_custom_call" | custom-call | flops 8589934592 | bytes 16777216 | tf_op jit(solution)/shard_map/pallas_call | solution.py:242
  247.6 43.3 %shard_map.174 = (bf16[2048,256]{1,0:T(8,128)(2,1)S(1)}, bf16[2048,768]{1,0:T(8,128)(2,1)}) custom-call(f32[2048,768]{1,0:T(8,128)} %get-tuple-element.38.mixed_ref, bf16[2048,256]{1,0:T(8,128)(2,1)S(1)} %get-tuple-element.39.grad_ref, f32[2048,128]{1,0:T(8,128)S(1)} %get-tuple-element.91.cos_ref, f32[2048,128]{1,0:T(8,128)S(1)} %get-tuple-element.90.sin_ref, ...), custom_call_target="tpu_custom_call" | custom-call | flops 21474836480 | bytes 8388608 | tf_op jit(solution)/shard_map/pallas_call | solution.py:101
  293.2 9.4 %convolution_convert_fusion = bf16[2048,768]{1,0:T(8,128)(2,1)S(1)} fusion(bf16[2048,2048]{1,0:T(8,128)(2,1)} %shard_map.169.normed_ref, bf16[2048,768]{1,0:T(8,128)(2,1)S(1)} %copy-done.26), kind=kOutput, calls=%fused_computation.5 | convolution fusion | flops 6444023808 | bytes 14680064 | tf_op jit(solution)/shard_map/dot_general | solution.py:24
  302.7 2.6 shard_map.182
  313.2 13.8 %shard_map.176 = (bf16[2048,512]{1,0:T(8,128)(2,1)S(1)}, bf16[2048,512]{1,0:T(8,128)(2,1)S(1)}, f32[1,512]{1,0:T(1,128)S(1)}) custom-call(bf16[2048,2048]{1,0:T(8,128)(2,1)} %shard_map.169.normed_ref, bf16[2048,2048]{1,0:T(8,128)(2,1)} %shard_map.170.grad_ref, bf16[2048,512]{1,0:T(8,128)(2,1)} %slice.160.up_ref.refs_5_, bf16[512,2048]{1,0:T(8,128)(2,1)} %bitcast.262, ...), custom_call_target="tpu_custom_call" | custom-call | flops 8589934592 | bytes 16777216 | tf_op jit(solution)/shard_map/pallas_call | solution.py:211
  328.3 5.9 %convolution_convert_fusion.2 = bf16[2048,512]{1,0:T(8,128)(2,1)} fusion(bf16[2048,2048]{1,0:T(8,128)(2,1)S(1)} %bitcast.233, bf16[2048,512]{1,0:T(8,128)(2,1)S(1)} %get-tuple-element.45.refs_2_), kind=kOutput, calls=%fused_computation.10 | convolution fusion | flops 4296015872 | bytes 12582912 | tf_op jit(solution)/shard_map/dot_general | solution.py:24
  335.6 10.0 %convolution_convert_fusion.1 = bf16[512,2048]{1,0:T(8,128)(2,1)} fusion(bf16[2048,512]{1,0:T(8,128)(2,1)} %copy-done.6, bf16[2048,2048]{1,0:T(8,128)(2,1)} %shard_map.170.grad_ref), kind=kOutput, calls=%fused_computation.9 | convolution fusion | flops 4296015872 | bytes 12582912 | tf_op jit(solution)/shard_map/dot_general | solution.py:24
  349.2 12.8 %shard_map.178 = bf16[1024,2048]{1,0:T(8,128)(2,1)} custom-call(s32[1]{0:T(128)} %constant.211.clone.1.first_ref, bf16[2048,768]{1,0:T(8,128)(2,1)} %get-tuple-element.47.refs_0_, bf16[2048,512]{1,0:T(8,128)(2,1)S(1)} %copy-done.8, bf16[2048,512]{1,0:T(8,128)(2,1)S(1)} %copy-done.10, bf16[2048,768]{1,0:T(8,128)(2,1)} %copy-done, ...), custom_call_target="tpu_custom_call" | custom-call | flops 7516192768 | bytes 8388608 | tf_op jit(solution)/shard_map/pallas_call | solution.py:271
  362.5 12.9 %shard_map.177 = bf16[1024,2048]{1,0:T(8,128)(2,1)} custom-call(s32[1]{0:T(128)} %constant.187.clone.1.first_ref, bf16[2048,768]{1,0:T(8,128)(2,1)} %get-tuple-element.47.refs_0_, bf16[2048,512]{1,0:T(8,128)(2,1)S(1)} %copy-done.8, bf16[2048,512]{1,0:T(8,128)(2,1)S(1)} %copy-done.10, bf16[2048,768]{1,0:T(8,128)(2,1)} %copy-done, ...), custom_call_target="tpu_custom_call" | custom-call | flops 7516192768 | bytes 8388608 | tf_op jit(solution)/shard_map/pallas_call | solution.py:271
  377.6 3.9 all-to-all-start.3
  381.5 8.0 %add_convert_fusion.1 = bf16[1024,2048]{1,0:T(8,128)(2,1)} fusion(bf16[1024,2048]{1,0:T(8,128)(2,1)} %collective-permute-done.10, bf16[1024,2048]{1,0:T(8,128)(2,1)} %shard_map.177), kind=kLoop, calls=%fused_computation.1 | loop fusion | flops 8388608 | bytes 12582912 | tf_op jit(solution)/shard_map/convert_element_type | solution.py:366
  393.1 9.8 %shard_map.181 = bf16[1024,2048]{1,0:T(8,128)(2,1)} custom-call(s32[1]{0:T(128)} %constant.211.clone.1.first_ref, bf16[2048,256]{1,0:T(8,128)(2,1)S(1)} %get-tuple-element.48.refs_0_, bf16[2048,512]{1,0:T(8,128)(2,1)S(1)} %copy-done.4, bf16[2048,512]{1,0:T(8,128)(2,1)} %copy-done.6, bf16[256,2048]{1,0:T(8,128)(2,1)S(1)} %copy-done.2, ...), custom_call_target="tpu_custom_call" | custom-call | flops 5368709120 | bytes 8388608 | tf_op jit(solution)/shard_map/pallas_call | solution.py:271
  405.4 2.4 convert_reduce_fusion
  408.1 10.3 %reduce-scatter.7.cloned.1.call-done = bf16[512,1024]{1,0:T(8,128)(2,1)} async-done(((bf16[2048,1024]{1,0:T(8,128)(2,1)}), bf16[512,1024]{1,0:T(8,128)(2,1)}) %reduce-scatter.7.cloned.1.call-update) | async-done | bytes 1048592 | tf_op jit(solution)/shard_map/reduce_scatter | solution.py:389
  420.4 4.2 all-to-all-start.5
  424.7 4.0 fusion.43
  442.5 3.6 reshape.757
  446.2 4.4 copy.75
  450.6 3.2 reshape.758
  455.4 9.9 %shard_map.180 = bf16[1024,2048]{1,0:T(8,128)(2,1)} custom-call(s32[1]{0:T(128)} %constant.187.clone.1.first_ref, bf16[2048,256]{1,0:T(8,128)(2,1)S(1)} %get-tuple-element.48.refs_0_, bf16[2048,512]{1,0:T(8,128)(2,1)S(1)} %copy-done.5, bf16[2048,512]{1,0:T(8,128)(2,1)} %copy-done.6, bf16[256,2048]{1,0:T(8,128)(2,1)S(1)} %copy-done.2, ...), custom_call_target="tpu_custom_call" | custom-call | flops 5368709120 | bytes 8388608 | tf_op jit(solution)/shard_map/pallas_call | solution.py:271
  470.0 4.1 add_convert_fusion
  477.6 3.0 collective-permute-done.19
  486.7 4.0 all-to-all-start.4
  491.4 14.6 %collective-permute-done.14 = bf16[2,256,1024]{2,1,0:T(8,128)(2,1)} collective-permute-done((bf16[2,256,1024]{2,1,0:T(8,128)(2,1)}, bf16[2,256,1024]{2,1,0:T(8,128)(2,1)}, u32[]{:S(2)}, u32[]{:S(2)}) %collective-permute-start.14) | collective-permute-done | bytes 1048608 | tf_op jit(solution)/shard_map/ppermute | solution.py:329
  515.0 6.3 %collective-permute-done.15 = bf16[256,1024]{1,0:T(8,128)(2,1)} collective-permute-done((bf16[256,1024]{1,0:T(8,128)(2,1)}, bf16[256,1024]{1,0:T(8,128)(2,1)}, u32[]{:S(2)}, u32[]{:S(2)}) %collective-permute-start.15) | collective-permute-done | bytes 524320 | tf_op jit(solution)/shard_map/ppermute | solution.py:329
  527.4 4.1 all-to-all-start.6
  531.6 3.8 fusion.17
  535.4 5.4 all-to-all-done.6
  (282 shorter events, 133.4 us)
Async XLA Ops:
  7.2 38.1 %all-gather.4.cloned.1.call-start = ((), (), s32[]{:S(2)}) async-start(), calls=%async_computation.11 | async-start | bytes 1310720 | tf_op jit(solution)/shard_map/all_gather | solution.py:386
  20.9 23.0 %all-to-all-start.1 = ((bf16[8,64,1280]{2,1,0:T(8,128)(2,1)}), bf16[8,64,1280]{2,1,0:T(8,128)(2,1)S(1)}, u32[]{:S(2)}, u32[]{:S(2)}) async-start(bf16[8,64,1280]{2,1,0:T(8,128)(2,1)} %pad_maximum_fusion.4), calls=%async_computation.1 | async-start | bytes 2621440 | tf_op jit(solution)/shard_map/all_to_all | solution.py:383
  26.2 156.5 %all-gather.6.cloned.1.call-start = ((), (), s32[]{:S(2)}) async-start(), calls=%async_computation.12 | async-start | bytes 9175040 | tf_op jit(solution)/shard_map/all_gather | solution.py:386
  47.3 16.7 %copy-start.13 = (bf16[1,256,2048]{2,1,0:T(8,128)(2,1)S(1)}, bf16[1,256,2048]{2,1,0:T(8,128)(2,1)}, u32[]{:S(2)}) copy-start(bf16[1,256,2048]{2,1,0:T(8,128)(2,1)} %param.13) | copy-start | bytes 3145732
  47.3 14.3 %collective-permute-start = (bf16[256,1024]{1,0:T(8,128)(2,1)}, bf16[256,1024]{1,0:T(8,128)(2,1)S(1)}, u32[]{:S(2)}, u32[]{:S(2)}) collective-permute-start(bf16[256,1024]{1,0:T(8,128)(2,1)} %get-tuple-element.84), channel_id=1, source_target_pairs={{0,2},{1,3},{2,0},{3,1},{4,6},{5,7},{6,4},{7,5},{8,10},{9,11},{10,... | collective-permute-start | bytes 1572872 | tf_op jit(solution)/shard_map/ppermute | solution.py:329
  48.3 19.9 %collective-permute-start.2 = (bf16[256,1024]{1,0:T(8,128)(2,1)}, bf16[256,1024]{1,0:T(8,128)(2,1)S(1)}, u32[]{:S(2)}, u32[]{:S(2)}) collective-permute-start(bf16[256,1024]{1,0:T(8,128)(2,1)} %get-tuple-element.83), channel_id=1, source_target_pairs={{0,1},{1,0},{2,3},{3,2},{4,5},{5,4},{6,7},{7,6},{8,9},{9,8},{10,11... | collective-permute-start | bytes 1572872 | tf_op jit(solution)/shard_map/ppermute | solution.py:329
  65.8 15.1 %collective-permute-start.5 = (bf16[256,1024]{1,0:T(8,128)(2,1)}, bf16[256,1024]{1,0:T(8,128)(2,1)S(1)}, u32[]{:S(2)}, u32[]{:S(2)}) collective-permute-start(bf16[256,1024]{1,0:T(8,128)(2,1)} %get-tuple-element.78), channel_id=1, source_target_pairs={{0,2},{1,3},{2,0},{3,1},{4,6},{5,7},{6,4},{7,5},{8,10},{9,11},{10,... | collective-permute-start | bytes 1572872 | tf_op jit(solution)/shard_map/ppermute | solution.py:329
  66.2 39.8 %collective-permute-start.1 = (bf16[2,256,1024]{2,1,0:T(8,128)(2,1)}, bf16[2,256,1024]{2,1,0:T(8,128)(2,1)}, u32[]{:S(2)}, u32[]{:S(2)}) collective-permute-start(bf16[2,256,1024]{2,1,0:T(8,128)(2,1)} %maximum_select_fusion.5), channel_id=1, source_target_pairs={{0,1},{1,0},{2,3},{3,2},{4,5},{5,4},{6,7},{7,6},{8,9},{9,8},{10,11... | collective-permute-start | bytes 3145736 | tf_op jit(solution)/shard_map/ppermute | solution.py:329
  67.0 36.8 %collective-permute-start.7 = (bf16[256,1024]{1,0:T(8,128)(2,1)}, bf16[256,1024]{1,0:T(8,128)(2,1)S(1)}, u32[]{:S(2)}, u32[]{:S(2)}) collective-permute-start(bf16[256,1024]{1,0:T(8,128)(2,1)} %get-tuple-element.77), channel_id=1, source_target_pairs={{0,1},{1,0},{2,3},{3,2},{4,5},{5,4},{6,7},{7,6},{8,9},{9,8},{10,11... | collective-permute-start | bytes 1572872 | tf_op jit(solution)/shard_map/ppermute | solution.py:329
  69.6 38.4 %collective-permute-start.3 = (bf16[2,256,1024]{2,1,0:T(8,128)(2,1)S(1)}, bf16[2,256,1024]{2,1,0:T(8,128)(2,1)S(1)}, u32[]{:S(2)}, u32[]{:S(2)}) collective-permute-start(bf16[2,256,1024]{2,1,0:T(8,128)(2,1)S(1)} %maximum_select_fusion.7), channel_id=1, source_target_pairs={{0,2},{1,3},{2,0},{3,1},{4,6},{5,7},{6,4},{7,5},{8,10},{9,11},{10,... | collective-permute-start | bytes 3145736 | tf_op jit(solution)/shard_map/ppermute | solution.py:329
  72.8 30.9 %copy-start.33 = (bf16[1,256,1024]{2,1,0:T(8,128)(2,1)S(1)}, bf16[1,256,1024]{2,1,0:T(8,128)(2,1)}, u32[]{:S(2)}) copy-start(bf16[1,256,1024]{2,1,0:T(8,128)(2,1)} %get-tuple-element.76) | copy-start | bytes 1572868
  80.9 24.8 %copy-start.32 = (bf16[1,1,256,1024]{3,2,1,0:T(8,128)(2,1)S(1)}, bf16[1,1,256,1024]{3,2,1,0:T(8,128)(2,1)}, u32[]{:S(2)}) copy-start(bf16[1,1,256,1024]{3,2,1,0:T(8,128)(2,1)} %get-tuple-element.75) | copy-start | bytes 1572868
  81.0 43.3 %collective-permute-start.6 = (bf16[2,256,1024]{2,1,0:T(8,128)(2,1)S(1)}, bf16[2,256,1024]{2,1,0:T(8,128)(2,1)S(1)}, u32[]{:S(2)}, u32[]{:S(2)}) collective-permute-start(bf16[2,256,1024]{2,1,0:T(8,128)(2,1)S(1)} %maximum_select_fusion.8), channel_id=1, source_target_pairs={{0,1},{1,0},{2,3},{3,2},{4,5},{5,4},{6,7},{7,6},{8,9},{9,8},{10,11... | collective-permute-start | bytes 3145736 | tf_op jit(solution)/shard_map/ppermute | solution.py:329
  103.9 21.8 %collective-permute-start.8 = (bf16[2,256,1024]{2,1,0:T(8,128)(2,1)S(1)}, bf16[2,256,1024]{2,1,0:T(8,128)(2,1)S(1)}, u32[]{:S(2)}, u32[]{:S(2)}) collective-permute-start(bf16[2,256,1024]{2,1,0:T(8,128)(2,1)S(1)} %maximum_select_fusion.10), channel_id=1, source_target_pairs={{0,2},{1,3},{2,0},{3,1},{4,6},{5,7},{6,4},{7,5},{8,10},{9,11},{10,... | collective-permute-start | bytes 3145736 | tf_op jit(solution)/shard_map/ppermute | solution.py:329
  110.9 50.9 %collective-permute-start.4 = (bf16[1024,2048]{1,0:T(8,128)(2,1)}, bf16[1024,2048]{1,0:T(8,128)(2,1)}, u32[]{:S(2)}, u32[]{:S(2)}) collective-permute-start(bf16[1024,2048]{1,0:T(8,128)(2,1)} %pad_maximum_fusion.own_ref), channel_id=1, source_target_pairs={{0,4},{4,0},{8,12},{12,8},{16,20},{20,16},{24,28},{28,24},{1,5},{5... | collective-permute-start | bytes 12582920 | tf_op jit(solution)/shard_map/ppermute | solution.py:332
  128.6 44.5 %collective-permute-start.9 = (bf16[1024,2048]{1,0:T(8,128)(2,1)}, bf16[1024,2048]{1,0:T(8,128)(2,1)}, u32[]{:S(2)}, u32[]{:S(2)}) collective-permute-start(bf16[1024,2048]{1,0:T(8,128)(2,1)} %pad_maximum_fusion.1.own_ref), channel_id=1, source_target_pairs={{0,4},{4,0},{8,12},{12,8},{16,20},{20,16},{24,28},{28,24},{1,5},{5... | collective-permute-start | bytes 12582920 | tf_op jit(solution)/shard_map/ppermute | solution.py:332
  129.4 18.6 %all-to-all-start = ((f32[32,1,896]{2,1,0:T(1,128)}), f32[32,1,896]{2,1,0:T(1,128)S(1)}, u32[]{:S(2)}, u32[]{:S(2)}) async-start(f32[32,1,896]{2,1,0:T(1,128)} %broadcast_in_dim.102), calls=%async_computation | async-start | bytes 229376 | tf_op jit(solution)/shard_map/all_to_all | solution.py:467
  148.0 12.7 %all-to-all-start.2 = ((bf16[8,64,512]{2,1,0:T(8,128)(2,1)}), bf16[8,64,512]{2,1,0:T(8,128)(2,1)S(1)}, u32[]{:S(2)}, u32[]{:S(2)}) async-start(bf16[8,64,512]{2,1,0:T(8,128)(2,1)} %reshape.739), calls=%async_computation.2 | async-start | bytes 1048576 | tf_op jit(solution)/shard_map/all_to_all | solution.py:383
  151.5 153.8 %all-gather.8.cloned.1.call-start = ((), (), s32[]{:S(2)}) async-start(), calls=%async_computation.13 | async-start | bytes 5242880 | tf_op jit(solution)/shard_map/all_gather | solution.py:386
  152.5 20.6 %copy-start.36 = (f32[32,64]{1,0:T(8,128)}, f32[32,64]{1,0:T(8,128)S(1)}, u32[]{:S(2)}) copy-start(f32[32,64]{1,0:T(8,128)S(1)} %get-tuple-element.87) | copy-start | bytes 24580
  182.7 192.7 %reduce-scatter.5.cloned.1.call-start = ((), (), s32[]{:S(2)}) async-start(), calls=%async_computation.14 | async-start | bytes 5242880 | tf_op jit(solution)/shard_map/reduce_scatter | solution.py:389
  225.5 192.8 %reduce-scatter.7.cloned.1.call-start = ((), (), s32[]{:S(2)}) async-start(), calls=%async_computation.15 | async-start | bytes 5242880 | tf_op jit(solution)/shard_map/reduce_scatter | solution.py:389
  232.9 14.6 %copy-start = (bf16[2048,768]{1,0:T(8,128)(2,1)}, bf16[2048,768]{1,0:T(8,128)(2,1)S(1)}, u32[]{:S(2)}) copy-start(bf16[2048,768]{1,0:T(8,128)(2,1)S(1)} %slice.156.in_ref.refs_3_) | copy-start | bytes 9437188
  232.9 57.9 %slice-start = ((s8[8388608]{0:T(1024)(128)(4,1)}), s8[4194304]{0:T(1024)(128)(4,1)S(1)}, s32[]{:S(2)}) async-start(s8[8388608]{0:T(1024)(128)(4,1)} %bitcast.222), calls=%async_computation.18 | async-start | bytes 8388608
  247.6 43.3 %slice-start.1 = ((s8[8388608]{0:T(1024)(128)(4,1)}), s8[4194304]{0:T(1024)(128)(4,1)S(1)}, s32[]{:S(2)}) async-start(s8[8388608]{0:T(1024)(128)(4,1)} %bitcast.222), calls=%async_computation.19 | async-start | bytes 8388608
  311.6 16.7 %slice-start.2 = ((s8[8388608]{0:T(1024)(128)(4,1)}), s8[4194304]{0:T(1024)(128)(4,1)S(1)}, s32[]{:S(2)}) async-start(s8[8388608]{0:T(1024)(128)(4,1)} %bitcast.232), calls=%async_computation.20 | async-start | bytes 8388608
  313.2 15.1 %slice-start.3 = ((s8[8388608]{0:T(1024)(128)(4,1)}), s8[4194304]{0:T(1024)(128)(4,1)S(1)}, s32[]{:S(2)}) async-start(s8[8388608]{0:T(1024)(128)(4,1)} %bitcast.232), calls=%async_computation.21 | async-start | bytes 8388608
  362.0 19.5 %collective-permute-start.10 = (bf16[1024,2048]{1,0:T(8,128)(2,1)}, bf16[1024,2048]{1,0:T(8,128)(2,1)}, u32[]{:S(2)}, u32[]{:S(2)}) collective-permute-start(bf16[1024,2048]{1,0:T(8,128)(2,1)} %shard_map.178), channel_id=1, source_target_pairs={{0,4},{4,0},{8,12},{12,8},{16,20},{20,16},{24,28},{28,24},{1,5},{5... | collective-permute-start | bytes 12582920 | tf_op jit(solution)/shard_map/ppermute | solution.py:332
  377.6 13.1 %all-to-all-start.3 = ((bf16[8,64,512]{2,1,0:T(8,128)(2,1)}), bf16[8,64,512]{2,1,0:T(8,128)(2,1)S(1)}, u32[]{:S(2)}, u32[]{:S(2)}) async-start(bf16[8,64,512]{2,1,0:T(8,128)(2,1)} %bitcast.64), calls=%async_computation.4 | async-start | bytes 1048576 | tf_op jit(solution)/shard_map/all_to_all | solution.py:383
  381.5 10.0 %copy-start.2 = (bf16[256,2048]{1,0:T(8,128)(2,1)S(1)}, bf16[256,2048]{1,0:T(8,128)(2,1)}, u32[]{:S(2)}) copy-start(bf16[256,2048]{1,0:T(8,128)(2,1)} %all-gather.4.cloned.1.call-done.proj_ref.refs_3_) | copy-start | bytes 3145732
  393.1 11.5 %copy-start.12 = (bf16[1,256,2048]{2,1,0:T(8,128)(2,1)S(1)}, bf16[1,256,2048]{2,1,0:T(8,128)(2,1)}, u32[]{:S(2)}) copy-start(bf16[1,256,2048]{2,1,0:T(8,128)(2,1)} %param.11) | copy-start | bytes 3145732
  402.8 67.2 %collective-permute-start.11 = (bf16[1024,2048]{1,0:T(8,128)(2,1)}, bf16[1024,2048]{1,0:T(8,128)(2,1)}, u32[]{:S(2)}, u32[]{:S(2)}) collective-permute-start(bf16[1024,2048]{1,0:T(8,128)(2,1)} %shard_map.181), channel_id=1, source_target_pairs={{0,4},{4,0},{8,12},{12,8},{16,20},{20,16},{24,28},{28,24},{1,5},{5... | collective-permute-start | bytes 12582920 | tf_op jit(solution)/shard_map/ppermute | solution.py:332
  420.4 22.1 %all-to-all-start.5 = ((bf16[8,64,768]{2,1,0:T(8,128)(2,1)}), bf16[8,64,768]{2,1,0:T(8,128)(2,1)}, u32[]{:S(2)}, u32[]{:S(2)}) async-start(bf16[8,64,768]{2,1,0:T(8,128)(2,1)} %bitcast.250), calls=%async_computation.7 | async-start | bytes 1572864 | tf_op jit(solution)/shard_map/all_to_all | solution.py:383
  424.6 66.3 %reduce-scatter.9.cloned.1.call-start = ((), (), s32[]{:S(2)}) async-start(), calls=%async_computation.16 | async-start | bytes 2621440 | tf_op jit(solution)/shard_map/reduce_scatter | solution.py:389
  429.8 35.4 %collective-permute-start.18 = (bf16[2,256,1024]{2,1,0:T(8,128)(2,1)}, bf16[2,256,1024]{2,1,0:T(8,128)(2,1)}, u32[]{:S(2)}, u32[]{:S(2)}) collective-permute-start(bf16[2,256,1024]{2,1,0:T(8,128)(2,1)} %dynamic-slice_bitcast_fusion), channel_id=1, source_target_pairs={{0,2},{1,3},{2,0},{3,1},{4,6},{5,7},{6,4},{7,5},{8,10},{9,11},{10,... | collective-permute-start | bytes 3145736 | tf_op jit(solution)/shard_map/ppermute | solution.py:329
  438.2 29.5 %collective-permute-start.16 = (bf16[2,256,1024]{2,1,0:T(8,128)(2,1)}, bf16[2,256,1024]{2,1,0:T(8,128)(2,1)}, u32[]{:S(2)}, u32[]{:S(2)}) collective-permute-start(bf16[2,256,1024]{2,1,0:T(8,128)(2,1)} %dynamic-slice_bitcast_fusion.1), channel_id=1, source_target_pairs={{0,1},{1,0},{2,3},{3,2},{4,5},{5,4},{6,7},{7,6},{8,9},{9,8},{10,11... | collective-permute-start | bytes 3145736 | tf_op jit(solution)/shard_map/ppermute | solution.py:329
  455.4 9.9 %copy-start.18 = (bf16[2,2,256,1024]{3,2,1,0:T(8,128)(2,1)S(1)}, bf16[2,2,256,1024]{3,2,1,0:T(8,128)(2,1)}, u32[]{:S(2)}) copy-start(bf16[2,2,256,1024]{3,2,1,0:T(8,128)(2,1)} %copy-done.17) | copy-start | bytes 6291460
  467.1 13.5 %collective-permute-start.19 = (bf16[256,1024]{1,0:T(8,128)(2,1)S(1)}, bf16[256,1024]{1,0:T(8,128)(2,1)S(1)}, u32[]{:S(2)}, u32[]{:S(2)}) collective-permute-start(bf16[256,1024]{1,0:T(8,128)(2,1)S(1)} %dynamic-slice_bitcast_fusion.4), channel_id=1, source_target_pairs={{0,1},{1,0},{2,3},{3,2},{4,5},{5,4},{6,7},{7,6},{8,9},{9,8},{10,11... | collective-permute-start | bytes 1572872 | tf_op jit(solution)/shard_map/ppermute | solution.py:329
  469.6 14.9 %collective-permute-start.17 = (bf16[256,1024]{1,0:T(8,128)(2,1)S(1)}, bf16[256,1024]{1,0:T(8,128)(2,1)S(1)}, u32[]{:S(2)}, u32[]{:S(2)}) collective-permute-start(bf16[256,1024]{1,0:T(8,128)(2,1)S(1)} %dynamic-slice_bitcast_fusion.5), channel_id=1, source_target_pairs={{0,2},{1,3},{2,0},{3,1},{4,6},{5,7},{6,4},{7,5},{8,10},{9,11},{10,... | collective-permute-start | bytes 1572872 | tf_op jit(solution)/shard_map/ppermute | solution.py:329
  475.9 30.1 %collective-permute-start.14 = (bf16[2,256,1024]{2,1,0:T(8,128)(2,1)}, bf16[2,256,1024]{2,1,0:T(8,128)(2,1)}, u32[]{:S(2)}, u32[]{:S(2)}) collective-permute-start(bf16[2,256,1024]{2,1,0:T(8,128)(2,1)} %dynamic-slice_bitcast_fusion.2), channel_id=1, source_target_pairs={{0,2},{1,3},{2,0},{3,1},{4,6},{5,7},{6,4},{7,5},{8,10},{9,11},{10,... | collective-permute-start | bytes 3145736 | tf_op jit(solution)/shard_map/ppermute | solution.py:329
  481.8 28.5 %collective-permute-start.12 = (bf16[2,256,1024]{2,1,0:T(8,128)(2,1)}, bf16[2,256,1024]{2,1,0:T(8,128)(2,1)}, u32[]{:S(2)}, u32[]{:S(2)}) collective-permute-start(bf16[2,256,1024]{2,1,0:T(8,128)(2,1)} %dynamic-slice_bitcast_fusion.3), channel_id=1, source_target_pairs={{0,1},{1,0},{2,3},{3,2},{4,5},{5,4},{6,7},{7,6},{8,9},{9,8},{10,11... | collective-permute-start | bytes 3145736 | tf_op jit(solution)/shard_map/ppermute | solution.py:329
  486.7 27.1 %all-to-all-start.4 = ((f32[32,1,640]{2,1,0:T(1,128)}), f32[32,1,640]{2,1,0:T(1,128)S(1)}, u32[]{:S(2)}, u32[]{:S(2)}) async-start(f32[32,1,640]{2,1,0:T(1,128)} %all_to_all.32), calls=%async_computation.5 | async-start | bytes 163840 | tf_op jit(solution)/shard_map/all_to_all | solution.py:607
  490.7 57.2 %reduce-scatter.11.cloned.1.call-start = ((), (), s32[]{:S(2)}) async-start(), calls=%async_computation.17 | async-start | bytes 2621440 | tf_op jit(solution)/shard_map/reduce_scatter | solution.py:389
  491.4 18.9 %copy-start.16 = (bf16[2,2,256,1024]{3,2,1,0:T(8,128)(2,1)S(1)}, bf16[2,2,256,1024]{3,2,1,0:T(8,128)(2,1)}, u32[]{:S(2)}) copy-start(bf16[2,2,256,1024]{3,2,1,0:T(8,128)(2,1)} %copy-done.15) | copy-start | bytes 6291460
  508.9 12.3 %collective-permute-start.15 = (bf16[256,1024]{1,0:T(8,128)(2,1)}, bf16[256,1024]{1,0:T(8,128)(2,1)}, u32[]{:S(2)}, u32[]{:S(2)}) collective-permute-start(bf16[256,1024]{1,0:T(8,128)(2,1)} %dynamic-slice_bitcast_fusion.6), channel_id=1, source_target_pairs={{0,1},{1,0},{2,3},{3,2},{4,5},{5,4},{6,7},{7,6},{8,9},{9,8},{10,11... | collective-permute-start | bytes 1572872 | tf_op jit(solution)/shard_map/ppermute | solution.py:329
  513.1 12.1 %collective-permute-start.13 = (bf16[256,1024]{1,0:T(8,128)(2,1)}, bf16[256,1024]{1,0:T(8,128)(2,1)}, u32[]{:S(2)}, u32[]{:S(2)}) collective-permute-start(bf16[256,1024]{1,0:T(8,128)(2,1)} %dynamic-slice_bitcast_fusion.7), channel_id=1, source_target_pairs={{0,2},{1,3},{2,0},{3,1},{4,6},{5,7},{6,4},{7,5},{8,10},{9,11},{10,... | collective-permute-start | bytes 1572872 | tf_op jit(solution)/shard_map/ppermute | solution.py:329
  513.8 11.4 %copy-start.24 = (bf16[2,256,1024]{2,1,0:T(8,128)(2,1)S(1)}, bf16[2,256,1024]{2,1,0:T(8,128)(2,1)}, u32[]{:S(2)}) copy-start(bf16[2,256,1024]{2,1,0:T(8,128)(2,1)} %copy-done.23) | copy-start | bytes 3145732
  527.4 13.4 %all-to-all-start.6 = ((bf16[8,64,512]{2,1,0:T(8,128)(2,1)}), bf16[8,64,512]{2,1,0:T(8,128)(2,1)}, u32[]{:S(2)}, u32[]{:S(2)}) async-start(bf16[8,64,512]{2,1,0:T(8,128)(2,1)} %bitcast.277), calls=%async_computation.9 | async-start | bytes 1048576 | tf_op jit(solution)/shard_map/all_to_all | solution.py:383
  (35 other events, 115.1 us)
Sparse Core Ops, SparseCore 0:
  9.6 30.6 all-gather.3
  45.4 134.7 all-gather.5
  182.8 78.4 all-gather.7
  263.5 75.2 reduce-scatter.4
  341.0 77.2 reduce-scatter.6
  436.0 43.4 reduce-scatter.8
  493.9 45.0 reduce-scatter.10

commit v4 on v3

--- a/solution.py
+++ b/solution.py
@@ -35,72 +35,75 @@
 def attention_kernel(
     block, mixed_ref, grad_ref, cos_ref, sin_ref, start_ref, out_ref, dmixed_ref, q_s, k_s, v_s, o_s, dq_s, dk_s, dv_s
 ):
-    head = pl.program_id(1)
     length, width = grad_ref.shape
+    heads = width // HD
     scale = HD**-0.5
 
     def wide(ref):
         table = ref[...]
         return jnp.concatenate([table] * (width // table.shape[1]), axis=1)
 
-    @pl.when(head == 0)
-    def _():
-        cosine, sine = wide(cos_ref), wide(sin_ref)
-        q = mixed_ref[:, 0:width]
-        q_s[...] = ((q * cosine + swap_halves(q) * sine).astype(bf16) * scale).astype(bf16)
-        k = mixed_ref[:, width : 2 * width]
-        k_s[...] = (k * cosine + swap_halves(k) * sine).astype(bf16)
-        v_s[...] = mixed_ref[:, 2 * width : 3 * width].astype(bf16)
-        o_s[...] = jnp.zeros_like(o_s)
-        dq_s[...] = jnp.zeros_like(dq_s)
-        dk_s[...] = jnp.zeros_like(dk_s)
-        dv_s[...] = jnp.zeros_like(dv_s)
-
-    mine = lax.broadcasted_iota(jnp.int32, (1, width), 1) // HD == head
+    cosine, sine = wide(cos_ref), wide(sin_ref)
+    q = mixed_ref[:, 0:width]
+    q_s[...] = ((q * cosine + swap_halves(q) * sine).astype(bf16) * scale).astype(bf16)
+    k = mixed_ref[:, width : 2 * width]
+    k_s[...] = (k * cosine + swap_halves(k) * sine).astype(bf16)
+    v_s[...] = mixed_ref[:, 2 * width : 3 * width].astype(bf16)
+    dk_s[...] = jnp.zeros_like(dk_s)
+    dv_s[...] = jnp.zeros_like(dv_s)
+    lane_head = lax.broadcasted_iota(jnp.int32, (1, width), 1) // HD
     zero = jnp.zeros((), bf16)
+
+    def stack(x):
+        return jnp.concatenate([jnp.where(lane_head == h, x, zero) for h in range(heads)])
+
+    def unstack(x):
+        total = jnp.where(lane_head == 0, x[:block], 0.0)
+        for h in range(1, heads):
+            total = jnp.where(lane_head == h, x[h * block : (h + 1) * block], total)
+        return total
+
     for i in range(length // block):
         rows = pl.ds(i * block, block)
         reach = (i + 1) * block
-        q = jnp.where(mine, q_s[rows, :], zero)
-        grad = jnp.where(mine, grad_ref[rows, :], zero)
+        q = stack(q_s[rows, :])
+        grad = stack(grad_ref[rows, :])
         k = k_s[0:reach, :]
         v = v_s[0:reach, :]
         scores = dot(q, k, NT)
         key_at = lax.broadcasted_iota(jnp.int32, (block, reach), 1)
         query_at = i * block + lax.broadcasted_iota(jnp.int32, (block, reach), 0)
         allowed = (key_at <= query_at) & (key_at >= start_ref[rows, :])
-        scores = jnp.where(allowed, scores, NEG_LARGE)
+        shift = jnp.where(allowed, 0.0, NEG_LARGE)
+        scores = (scores.reshape(heads, block, reach) + shift[None]).reshape(heads * block, reach)
         probs = jnp.exp(scores - jnp.max(scores, axis=1, keepdims=True))
         probs = probs * (1.0 / jnp.sum(probs, axis=1, keepdims=True))
         low = probs.astype(bf16)
-        o_s[rows, :] = jnp.where(mine, dot(low, v, NN), o_s[rows, :])
+        o_s[rows, :] = unstack(dot(low, v, NN))
         dprobs = dot(grad, v, NT)
         delta = jnp.sum(probs * dprobs, axis=1, keepdims=True)
         dscores = (probs * (dprobs - delta)).astype(bf16)
-        dq_s[rows, :] = jnp.where(mine, dot(dscores, k, NN), dq_s[rows, :])
+        dq_s[rows, :] = unstack(dot(dscores, k, NN))
         dk_s[0:reach, :] += dot(dscores, q, TN)
         dv_s[0:reach, :] += dot(low, grad, TN)
 
-    @pl.when(head == pl.num_programs(1) - 1)
-    def _():
-        cosine, sine = wide(cos_ref), wide(sin_ref)
-        out_ref[...] = o_s[...].astype(bf16)
-        dq = dq_s[...] * scale
-        dmixed_ref[:, 0:width] = (dq * cosine - swap_halves(dq) * sine).astype(bf16)
-        dk = dk_s[...]
-        dmixed_ref[:, width : 2 * width] = (dk * cosine - swap_halves(dk) * sine).astype(bf16)
-        dmixed_ref[:, 2 * width : 3 * width] = dv_s[...].astype(bf16)
+    out_ref[...] = o_s[...].astype(bf16)
+    dq = dq_s[...] * scale
+    dmixed_ref[:, 0:width] = (dq * cosine - swap_halves(dq) * sine).astype(bf16)
+    dk = dk_s[...]
+    dmixed_ref[:, width : 2 * width] = (dk * cosine - swap_halves(dk) * sine).astype(bf16)
+    dmixed_ref[:, 2 * width : 3 * width] = dv_s[...].astype(bf16)
 
 
 def attention(mixed, grad, cosine, sine, start, length):
     tokens, width = grad.shape
 
     def rows(columns):
-        return pl.BlockSpec((length, columns), lambda s, h: (s, 0))
+        return pl.BlockSpec((length, columns), lambda s: (s, 0))
 
     return pl.pallas_call(
         functools.partial(attention_kernel, min(256, length)),
-        grid=(tokens // length, width // HD),
+        grid=(tokens // length,),
         in_specs=[rows(3 * width), rows(width), rows(cosine.shape[1]), rows(cosine.shape[1]), rows(1)],
         out_specs=[rows(width), rows(3 * width)],
         out_shape=[
@@ -108,7 +111,7 @@
             jax.ShapeDtypeStruct((tokens, 3 * width), bf16),
         ],
         scratch_shapes=[pltpu.VMEM((length, width), bf16)] * 3 + [pltpu.VMEM((length, width), f32)] * 4,
-        compiler_params=pltpu.CompilerParams(vmem_limit_bytes=48 * 1024 * 1024),
+        compiler_params=pltpu.CompilerParams(vmem_limit_bytes=56 * 1024 * 1024),
         cost_estimate=pl.CostEstimate(
             flops=40 * tokens * length * width, bytes_accessed=16 * tokens * width, transcendentals=0
         ),
@@ -564,6 +567,7 @@
         out, more = scatter_plane(
             lambda i: joined_product([attended] + activated, [proj] + down, NN, i, length), length, core, seq
         )
+        grad_heads = after(grad_heads, more[0])
         for c in range(1, chunks):
             to_hidden, to_down = last[2 * c - 2 : 2 * c]
             grad_hidden.append(scatter_line(after(to_hidden, stages[0])))

time: 568 us -> 572 us (level)
  Pallas kernels: 159 us -> 146 us
  waiting for transfers between devices: 140 us -> 146 us
    pallas_call x1, Pallas kernels: 43.3 us -> 30 us  [attention(): pl.pallas_call(functools.partial(attention_kernel, min(256, length)), gri...]
    all_to_all x5, waiting for transfers between devices: 32.2 us -> 38.7 us  [swap_plane(): lax.all_to_all(x, BOTH, 0, 0, axis_index_groups=plane_groups, tiled=True)]
    unnamed x101 -> x105, local copies, waits for them, and re-layouts: 18.3 us -> 22.1 us
  transfers between devices with their start and end apart: 34 -> 34, of which waited for: 16 -> 17; matrix products, arithmetic and copies ran while one was open for 32% -> 33% of each run, Pallas kernels for 28% -> 26%
where the time goes in v4:
time: 572 us; the launch traced here: 562 us
  waiting for transfers between devices  146 us (26%)
  Pallas kernels  146 us (26%)
  local copies, waits for them, and re-layouts  91.3 us (16%)
  other arithmetic  62.4 us (11%)
  starting transfers between devices  51.8 us (9%)
  matrix products  48.9 us (9%)
  between operations  15.5 us (3%)
    ppermute x16, waiting for transfers between devices, seq_permute(): return lax.ppermute(x, 'seq', [(s, s ^ bit) for s in range(n_seq)])  80.5 us
    dot_general x6, matrix products, dot(): lax.dot_general(left, right, (dims, ((), ())), preferred_element_type=f32)  48.9 us
    pallas_call x4, Pallas kernels, joined_product(): pl.pallas_call(functools.partial(joined_kernel, count, dims), grid_spec=p...  45.9 us
    all_to_all x5, waiting for transfers between devices, swap_plane(): lax.all_to_all(x, BOTH, 0, 0, axis_index_groups=plane_groups, tiled=True)  38.7 us
    pallas_call x1, Pallas kernels, attention(): pl.pallas_call(functools.partial(attention_kernel, min(256, length)), gri...  30 us
    pallas_call x2, Pallas kernels, hidden_layer(): pl.pallas_call(hidden_kernel, grid=(tokens // block,), in_specs=[rows, ro...  27 us
    unnamed x105, local copies, waits for them, and re-layouts  22.1 us
    pallas_call x2, Pallas kernels, over_both(): pl.pallas_call(functools.partial(kernel, steps), grid=(2 * steps,), in_sp...  20.9 us
  transfers between devices with their start and end apart: 34, of which 17 were waited for; matrix products, arithmetic and copies ran while one was open for 33% of the time, Pallas kernels for 26%

profile of v4, /device:TPU:0, one launch (start us, length us, event | category | flops | bytes accessed | tf_op | source)
XLA Modules:
  0.0 561.8 jit_solution(1051239375770389691)
XLA Ops:
  20.9 5.3 all-to-all-start.1
  26.4 17.5 %all-to-all-done.1 = bf16[8,64,1280]{2,1,0:T(8,128)(2,1)S(1)} async-done(((bf16[8,64,1280]{2,1,0:T(8,128)(2,1)}), bf16[8,64,1280]{2,1,0:T(8,128)(2,1)S(1)}, u32[]{:S(2)}, u32[]{:S(2)}) %all-to-all-start.1) | async-done | bytes 1310752 | tf_op jit(solution)/shard_map/all_to_all | solution.py:386
  48.9 12.7 %collective-permute-done = bf16[256,1024]{1,0:T(8,128)(2,1)S(1)} collective-permute-done((bf16[256,1024]{1,0:T(8,128)(2,1)}, bf16[256,1024]{1,0:T(8,128)(2,1)S(1)}, u32[]{:S(2)}, u32[]{:S(2)}) %collective-permute-start) | collective-permute-done | bytes 524320 | tf_op jit(solution)/shard_map/ppermute | solution.py:332
  73.0 7.9 %collective-permute-done.5 = bf16[256,1024]{1,0:T(8,128)(2,1)S(1)} collective-permute-done((bf16[256,1024]{1,0:T(8,128)(2,1)}, bf16[256,1024]{1,0:T(8,128)(2,1)S(1)}, u32[]{:S(2)}, u32[]{:S(2)}) %collective-permute-start.5) | collective-permute-done | bytes 524320 | tf_op jit(solution)/shard_map/ppermute | solution.py:332
  81.9 21.8 %collective-permute-done.7 = bf16[256,1024]{1,0:T(8,128)(2,1)S(1)} collective-permute-done((bf16[256,1024]{1,0:T(8,128)(2,1)}, bf16[256,1024]{1,0:T(8,128)(2,1)S(1)}, u32[]{:S(2)}, u32[]{:S(2)}) %collective-permute-start.7) | collective-permute-done | bytes 524320 | tf_op jit(solution)/shard_map/ppermute | solution.py:332
  108.4 2.5 pad_maximum_fusion.own_ref
  110.9 13.5 %collective-permute-done.6 = bf16[2,256,1024]{2,1,0:T(8,128)(2,1)S(1)} collective-permute-done((bf16[2,256,1024]{2,1,0:T(8,128)(2,1)S(1)}, bf16[2,256,1024]{2,1,0:T(8,128)(2,1)S(1)}, u32[]{:S(2)}, u32[]{:S(2)}) %collective-permute-start.6) | collective-permute-done | bytes 1048608 | tf_op jit(solution)/shard_map/ppermute | solution.py:332
  129.4 5.3 all-to-all-start
  135.9 12.1 %all-to-all-done = f32[32,1,896]{2,1,0:T(1,128)S(1)} async-done(((f32[32,1,896]{2,1,0:T(1,128)}), f32[32,1,896]{2,1,0:T(1,128)S(1)}, u32[]{:S(2)}, u32[]{:S(2)}) %all-to-all-start) | async-done | bytes 114720 | tf_op jit(solution)/shard_map/all_to_all | solution.py:470
  148.0 3.5 all-to-all-start.2
  152.6 8.1 %all-to-all-done.2 = bf16[8,64,512]{2,1,0:T(8,128)(2,1)S(1)} async-done(((bf16[8,64,512]{2,1,0:T(8,128)(2,1)}), bf16[8,64,512]{2,1,0:T(8,128)(2,1)S(1)}, u32[]{:S(2)}, u32[]{:S(2)}) %all-to-all-start.2) | async-done | bytes 524320 | tf_op jit(solution)/shard_map/all_to_all | solution.py:386
  161.9 11.3 %shard_map.169.normed_ref = bf16[2048,2048]{1,0:T(8,128)(2,1)} custom-call(bf16[1024,2048]{1,0:T(8,128)(2,1)} %pad_maximum_fusion.own_ref, bf16[1024,2048]{1,0:T(8,128)(2,1)} %collective-permute-done.4.other_ref, f32[1,2048]{1,0:T(1,128)S(1)} %broadcast_in_dim_reshape.14.gain_ref, f32[1,2048]{1,0:T(1,128)S(1)} %broadcast_in_dim_reshape.15.shift_ref), custom_call_target="tpu_custom_call" | custom-call | flops 33554432 | bytes 16777216 | tf_op jit(solution)/shard_map/pallas_call | solution.py:174
  173.2 9.6 %shard_map.170.grad_ref = bf16[2048,2048]{1,0:T(8,128)(2,1)} custom-call(bf16[1024,2048]{1,0:T(8,128)(2,1)} %pad_maximum_fusion.1.own_ref, bf16[1024,2048]{1,0:T(8,128)(2,1)} %collective-permute-done.9.other_ref), custom_call_target="tpu_custom_call" | custom-call | flops 33554432 | bytes 16777216 | tf_op jit(solution)/shard_map/pallas_call | solution.py:174
  188.3 3.2 slice.151.up_ref.refs_4_
  191.5 13.2 %shard_map.172 = (bf16[2048,512]{1,0:T(8,128)(2,1)S(1)}, bf16[2048,512]{1,0:T(8,128)(2,1)S(1)}, f32[1,512]{1,0:T(1,128)S(1)}) custom-call(bf16[2048,2048]{1,0:T(8,128)(2,1)} %shard_map.169.normed_ref, bf16[2048,2048]{1,0:T(8,128)(2,1)} %shard_map.170.grad_ref, bf16[2048,512]{1,0:T(8,128)(2,1)} %slice.151.up_ref.refs_4_, bf16[512,2048]{1,0:T(8,128)(2,1)} %bitcast.259, ...), custom_call_target="tpu_custom_call" | custom-call | flops 8589934592 | bytes 16777216 | tf_op jit(solution)/shard_map/pallas_call | solution.py:214
  204.8 9.7 %convolution_convert_fusion.3 = bf16[512,2048]{1,0:T(8,128)(2,1)S(1)} fusion(bf16[2048,512]{1,0:T(8,128)(2,1)S(1)} %get-tuple-element.37.refs_1_, bf16[2048,2048]{1,0:T(8,128)(2,1)} %shard_map.170.grad_ref), kind=kOutput, calls=%fused_computation.11 | convolution fusion | flops 4296015872 | bytes 12582912 | tf_op jit(solution)/shard_map/dot_general | solution.py:24
  214.5 8.5 %convolution_convert_fusion.4 = bf16[2048,512]{1,0:T(8,128)(2,1)S(1)} fusion(bf16[2048,2048]{1,0:T(8,128)(2,1)} %shard_map.169.normed_ref, bf16[2048,512]{1,0:T(8,128)(2,1)S(1)} %get-tuple-element.36.refs_1_), kind=kOutput, calls=%fused_computation.12 | convolution fusion | flops 4296015872 | bytes 12582912 | tf_op jit(solution)/shard_map/dot_general | solution.py:24
  223.0 2.6 shard_map.179
  227.5 5.6 fusion.26
  235.3 14.5 %shard_map.173 = (f32[2048,768]{1,0:T(8,128)}, bf16[2048,256]{1,0:T(8,128)(2,1)S(1)}) custom-call(bf16[2048,2048]{1,0:T(8,128)(2,1)} %shard_map.169.normed_ref, bf16[2048,2048]{1,0:T(8,128)(2,1)} %shard_map.170.grad_ref, bf16[2048,768]{1,0:T(8,128)(2,1)S(1)} %slice.156.in_ref.refs_3_, bf16[256,2048]{1,0:T(8,128)(2,1)S(1)} %copy-done.2, ...), custom_call_target="tpu_custom_call" | custom-call | flops 8589934592 | bytes 16777216 | tf_op jit(solution)/shard_map/pallas_call | solution.py:245
  250.8 30.0 %shard_map.174 = (bf16[2048,256]{1,0:T(8,128)(2,1)}, bf16[2048,768]{1,0:T(8,128)(2,1)}) custom-call(f32[2048,768]{1,0:T(8,128)} %get-tuple-element.39.mixed_ref, bf16[2048,256]{1,0:T(8,128)(2,1)} %copy-done.14, f32[2048,128]{1,0:T(8,128)} %get-tuple-element.93.cos_ref, f32[2048,128]{1,0:T(8,128)} %get-tuple-element.92.sin_ref, s32[2048,1]{1,0:T(8,128)} %fusion.28.start_ref), custom_call_target="tpu_custom_call" | custom-call | flops 21474836480 | bytes 8388608 | tf_op jit(solution)/shard_map/pallas_call | solution.py:104
  280.8 6.3 %convolution_convert_fusion.5 = bf16[256,2048]{1,0:T(8,128)(2,1)S(1)} fusion(bf16[2048,256]{1,0:T(8,128)(2,1)} %get-tuple-element.49.refs_0_, bf16[2048,2048]{1,0:T(8,128)(2,1)} %shard_map.170.grad_ref), kind=kOutput, calls=%fused_computation.17 | convolution fusion | flops 2148007936 | bytes 10485760 | tf_op jit(solution)/shard_map/dot_general | solution.py:24
  287.1 9.4 %convolution_convert_fusion = bf16[2048,768]{1,0:T(8,128)(2,1)S(1)} fusion(bf16[2048,2048]{1,0:T(8,128)(2,1)} %shard_map.169.normed_ref, bf16[2048,768]{1,0:T(8,128)(2,1)S(1)} %copy-done.29), kind=kOutput, calls=%fused_computation.5 | convolution fusion | flops 6444023808 | bytes 14680064 | tf_op jit(solution)/shard_map/dot_general | solution.py:24
  296.5 2.6 shard_map.182
  307.0 13.8 %shard_map.176 = (bf16[2048,512]{1,0:T(8,128)(2,1)S(1)}, bf16[2048,512]{1,0:T(8,128)(2,1)S(1)}, f32[1,512]{1,0:T(1,128)S(1)}) custom-call(bf16[2048,2048]{1,0:T(8,128)(2,1)} %shard_map.169.normed_ref, bf16[2048,2048]{1,0:T(8,128)(2,1)} %shard_map.170.grad_ref, bf16[2048,512]{1,0:T(8,128)(2,1)} %slice.160.up_ref.refs_5_, bf16[512,2048]{1,0:T(8,128)(2,1)} %bitcast.262, ...), custom_call_target="tpu_custom_call" | custom-call | flops 8589934592 | bytes 16777216 | tf_op jit(solution)/shard_map/pallas_call | solution.py:214
  320.8 5.8 %convolution_convert_fusion.2 = bf16[2048,512]{1,0:T(8,128)(2,1)} fusion(bf16[2048,2048]{1,0:T(8,128)(2,1)S(1)} %bitcast.233, bf16[2048,512]{1,0:T(8,128)(2,1)S(1)} %get-tuple-element.46.refs_2_), kind=kOutput, calls=%fused_computation.10 | convolution fusion | flops 4296015872 | bytes 12582912 | tf_op jit(solution)/shard_map/dot_general | solution.py:24
  327.9 9.3 %convolution_convert_fusion.1 = bf16[512,2048]{1,0:T(8,128)(2,1)} fusion(bf16[2048,512]{1,0:T(8,128)(2,1)S(1)} %get-tuple-element.47.refs_2_, bf16[2048,2048]{1,0:T(8,128)(2,1)} %shard_map.170.grad_ref), kind=kOutput, calls=%fused_computation.9 | convolution fusion | flops 4296015872 | bytes 12582912 | tf_op jit(solution)/shard_map/dot_general | solution.py:24
  340.4 12.9 %shard_map.178 = bf16[1024,2048]{1,0:T(8,128)(2,1)} custom-call(s32[1]{0:T(128)} %constant.211.clone.1.first_ref, bf16[2048,768]{1,0:T(8,128)(2,1)} %get-tuple-element.48.refs_0_, bf16[2048,512]{1,0:T(8,128)(2,1)S(1)} %copy-done.9, bf16[2048,512]{1,0:T(8,128)(2,1)S(1)} %copy-done.12, bf16[2048,768]{1,0:T(8,128)(2,1)} %copy-done, ...), custom_call_target="tpu_custom_call" | custom-call | flops 7516192768 | bytes 8388608 | tf_op jit(solution)/shard_map/pallas_call | solution.py:274
  357.1 12.9 %shard_map.177 = bf16[1024,2048]{1,0:T(8,128)(2,1)} custom-call(s32[1]{0:T(128)} %constant.187.clone.1.first_ref, bf16[2048,768]{1,0:T(8,128)(2,1)} %get-tuple-element.48.refs_0_, bf16[2048,512]{1,0:T(8,128)(2,1)S(1)} %copy-done.10, bf16[2048,512]{1,0:T(8,128)(2,1)S(1)} %copy-done.13, bf16[2048,768]{1,0:T(8,128)(2,1)} %copy-done, ...), custom_call_target="tpu_custom_call" | custom-call | flops 7516192768 | bytes 8388608 | tf_op jit(solution)/shard_map/pallas_call | solution.py:274
  372.2 3.5 all-to-all-start.3
  375.8 8.0 %add_convert_fusion.1 = bf16[1024,2048]{1,0:T(8,128)(2,1)} fusion(bf16[1024,2048]{1,0:T(8,128)(2,1)} %collective-permute-done.10, bf16[1024,2048]{1,0:T(8,128)(2,1)} %shard_map.177), kind=kLoop, calls=%fused_computation.1 | loop fusion | flops 8388608 | bytes 12582912 | tf_op jit(solution)/shard_map/convert_element_type | solution.py:369
  387.3 10.1 %shard_map.181 = bf16[1024,2048]{1,0:T(8,128)(2,1)} custom-call(s32[1]{0:T(128)} %constant.211.clone.1.first_ref, bf16[2048,256]{1,0:T(8,128)(2,1)S(1)} %copy-done.1, bf16[2048,512]{1,0:T(8,128)(2,1)S(1)} %copy-done.5, bf16[2048,512]{1,0:T(8,128)(2,1)} %copy-done.7, bf16[256,2048]{1,0:T(8,128)(2,1)S(1)} %copy-done.3, bf16[512,2048]{1,0:T(8,128)(2,1)} %bitcast.260, ...), custom_call_target="tpu_custom_call" | custom-call | flops 5368709120 | bytes 8388608 | tf_op jit(solution)/shard_map/pallas_call | solution.py:274
  404.7 13.2 %reduce-scatter.7.cloned.1.call-done = bf16[512,1024]{1,0:T(8,128)(2,1)} async-done(((bf16[2048,1024]{1,0:T(8,128)(2,1)}), bf16[512,1024]{1,0:T(8,128)(2,1)}) %reduce-scatter.7.cloned.1.call-update) | async-done | bytes 1048592 | tf_op jit(solution)/shard_map/reduce_scatter | solution.py:392
  418.9 4.0 fusion.43
  436.1 10.0 %shard_map.180 = bf16[1024,2048]{1,0:T(8,128)(2,1)} custom-call(s32[1]{0:T(128)} %constant.187.clone.1.first_ref, bf16[2048,256]{1,0:T(8,128)(2,1)S(1)} %copy-done.1, bf16[2048,512]{1,0:T(8,128)(2,1)S(1)} %copy-done.6, bf16[2048,512]{1,0:T(8,128)(2,1)} %copy-done.7, bf16[256,2048]{1,0:T(8,128)(2,1)S(1)} %copy-done.3, bf16[512,2048]{1,0:T(8,128)(2,1)} %bitcast.261, ...), custom_call_target="tpu_custom_call" | custom-call | flops 5368709120 | bytes 8388608 | tf_op jit(solution)/shard_map/pallas_call | solution.py:274
  446.1 4.4 collective-permute-done.18
  457.7 4.1 add_convert_fusion
  468.8 3.7 collective-permute-done.17
  474.6 4.2 all-to-all-start.4
  479.6 13.0 %collective-permute-done.14 = bf16[2,256,1024]{2,1,0:T(8,128)(2,1)} collective-permute-done((bf16[2,256,1024]{2,1,0:T(8,128)(2,1)}, bf16[2,256,1024]{2,1,0:T(8,128)(2,1)}, u32[]{:S(2)}, u32[]{:S(2)}) %collective-permute-start.14) | collective-permute-done | bytes 1048608 | tf_op jit(solution)/shard_map/ppermute | solution.py:332
  497.9 4.2 all-to-all-start.5
  509.0 6.5 %all-to-all-done.5 = bf16[8,64,768]{2,1,0:T(8,128)(2,1)} async-done(((bf16[8,64,768]{2,1,0:T(8,128)(2,1)}), bf16[8,64,768]{2,1,0:T(8,128)(2,1)}, u32[]{:S(2)}, u32[]{:S(2)}) %all-to-all-start.5) | async-done | bytes 786464 | tf_op jit(solution)/shard_map/all_to_all | solution.py:386
  515.6 3.5 reshape.761
  519.1 4.4 copy.75
  523.4 3.1 reshape.762
  531.3 4.4 all-to-all-start.6
  535.6 3.8 fusion.17
  539.4 5.4 all-to-all-done.6
  (285 shorter events, 141.6 us)
Async XLA Ops:
  7.2 38.1 %all-gather.4.cloned.1.call-start = ((), (), s32[]{:S(2)}) async-start(), calls=%async_computation.11 | async-start | bytes 1310720 | tf_op jit(solution)/shard_map/all_gather | solution.py:389
  20.9 23.0 %all-to-all-start.1 = ((bf16[8,64,1280]{2,1,0:T(8,128)(2,1)}), bf16[8,64,1280]{2,1,0:T(8,128)(2,1)S(1)}, u32[]{:S(2)}, u32[]{:S(2)}) async-start(bf16[8,64,1280]{2,1,0:T(8,128)(2,1)} %pad_maximum_fusion.4), calls=%async_computation.1 | async-start | bytes 2621440 | tf_op jit(solution)/shard_map/all_to_all | solution.py:386
  26.2 156.6 %all-gather.6.cloned.1.call-start = ((), (), s32[]{:S(2)}) async-start(), calls=%async_computation.12 | async-start | bytes 9175040 | tf_op jit(solution)/shard_map/all_gather | solution.py:389
  47.3 16.7 %copy-start.17 = (bf16[1,256,2048]{2,1,0:T(8,128)(2,1)S(1)}, bf16[1,256,2048]{2,1,0:T(8,128)(2,1)}, u32[]{:S(2)}) copy-start(bf16[1,256,2048]{2,1,0:T(8,128)(2,1)} %param.13) | copy-start | bytes 3145732
  47.3 14.3 %collective-permute-start = (bf16[256,1024]{1,0:T(8,128)(2,1)}, bf16[256,1024]{1,0:T(8,128)(2,1)S(1)}, u32[]{:S(2)}, u32[]{:S(2)}) collective-permute-start(bf16[256,1024]{1,0:T(8,128)(2,1)} %get-tuple-element.86), channel_id=1, source_target_pairs={{0,2},{1,3},{2,0},{3,1},{4,6},{5,7},{6,4},{7,5},{8,10},{9,11},{10,... | collective-permute-start | bytes 1572872 | tf_op jit(solution)/shard_map/ppermute | solution.py:332
  48.3 19.9 %collective-permute-start.2 = (bf16[256,1024]{1,0:T(8,128)(2,1)}, bf16[256,1024]{1,0:T(8,128)(2,1)S(1)}, u32[]{:S(2)}, u32[]{:S(2)}) collective-permute-start(bf16[256,1024]{1,0:T(8,128)(2,1)} %get-tuple-element.85), channel_id=1, source_target_pairs={{0,1},{1,0},{2,3},{3,2},{4,5},{5,4},{6,7},{7,6},{8,9},{9,8},{10,11... | collective-permute-start | bytes 1572872 | tf_op jit(solution)/shard_map/ppermute | solution.py:332
  65.8 15.1 %collective-permute-start.5 = (bf16[256,1024]{1,0:T(8,128)(2,1)}, bf16[256,1024]{1,0:T(8,128)(2,1)S(1)}, u32[]{:S(2)}, u32[]{:S(2)}) collective-permute-start(bf16[256,1024]{1,0:T(8,128)(2,1)} %get-tuple-element.80), channel_id=1, source_target_pairs={{0,2},{1,3},{2,0},{3,1},{4,6},{5,7},{6,4},{7,5},{8,10},{9,11},{10,... | collective-permute-start | bytes 1572872 | tf_op jit(solution)/shard_map/ppermute | solution.py:332
  66.2 39.8 %collective-permute-start.1 = (bf16[2,256,1024]{2,1,0:T(8,128)(2,1)}, bf16[2,256,1024]{2,1,0:T(8,128)(2,1)}, u32[]{:S(2)}, u32[]{:S(2)}) collective-permute-start(bf16[2,256,1024]{2,1,0:T(8,128)(2,1)} %maximum_select_fusion.5), channel_id=1, source_target_pairs={{0,1},{1,0},{2,3},{3,2},{4,5},{5,4},{6,7},{7,6},{8,9},{9,8},{10,11... | collective-permute-start | bytes 3145736 | tf_op jit(solution)/shard_map/ppermute | solution.py:332
  67.0 36.8 %collective-permute-start.7 = (bf16[256,1024]{1,0:T(8,128)(2,1)}, bf16[256,1024]{1,0:T(8,128)(2,1)S(1)}, u32[]{:S(2)}, u32[]{:S(2)}) collective-permute-start(bf16[256,1024]{1,0:T(8,128)(2,1)} %get-tuple-element.79), channel_id=1, source_target_pairs={{0,1},{1,0},{2,3},{3,2},{4,5},{5,4},{6,7},{7,6},{8,9},{9,8},{10,11... | collective-permute-start | bytes 1572872 | tf_op jit(solution)/shard_map/ppermute | solution.py:332
  69.6 38.4 %collective-permute-start.3 = (bf16[2,256,1024]{2,1,0:T(8,128)(2,1)S(1)}, bf16[2,256,1024]{2,1,0:T(8,128)(2,1)S(1)}, u32[]{:S(2)}, u32[]{:S(2)}) collective-permute-start(bf16[2,256,1024]{2,1,0:T(8,128)(2,1)S(1)} %maximum_select_fusion.7), channel_id=1, source_target_pairs={{0,2},{1,3},{2,0},{3,1},{4,6},{5,7},{6,4},{7,5},{8,10},{9,11},{10,... | collective-permute-start | bytes 3145736 | tf_op jit(solution)/shard_map/ppermute | solution.py:332
  72.8 30.9 %copy-start.36 = (bf16[1,256,1024]{2,1,0:T(8,128)(2,1)S(1)}, bf16[1,256,1024]{2,1,0:T(8,128)(2,1)}, u32[]{:S(2)}) copy-start(bf16[1,256,1024]{2,1,0:T(8,128)(2,1)} %get-tuple-element.78) | copy-start | bytes 1572868
  80.9 24.8 %copy-start.35 = (bf16[1,1,256,1024]{3,2,1,0:T(8,128)(2,1)S(1)}, bf16[1,1,256,1024]{3,2,1,0:T(8,128)(2,1)}, u32[]{:S(2)}) copy-start(bf16[1,1,256,1024]{3,2,1,0:T(8,128)(2,1)} %get-tuple-element.77) | copy-start | bytes 1572868
  81.0 43.3 %collective-permute-start.6 = (bf16[2,256,1024]{2,1,0:T(8,128)(2,1)S(1)}, bf16[2,256,1024]{2,1,0:T(8,128)(2,1)S(1)}, u32[]{:S(2)}, u32[]{:S(2)}) collective-permute-start(bf16[2,256,1024]{2,1,0:T(8,128)(2,1)S(1)} %maximum_select_fusion.8), channel_id=1, source_target_pairs={{0,1},{1,0},{2,3},{3,2},{4,5},{5,4},{6,7},{7,6},{8,9},{9,8},{10,11... | collective-permute-start | bytes 3145736 | tf_op jit(solution)/shard_map/ppermute | solution.py:332
  103.9 21.8 %collective-permute-start.8 = (bf16[2,256,1024]{2,1,0:T(8,128)(2,1)S(1)}, bf16[2,256,1024]{2,1,0:T(8,128)(2,1)S(1)}, u32[]{:S(2)}, u32[]{:S(2)}) collective-permute-start(bf16[2,256,1024]{2,1,0:T(8,128)(2,1)S(1)} %maximum_select_fusion.10), channel_id=1, source_target_pairs={{0,2},{1,3},{2,0},{3,1},{4,6},{5,7},{6,4},{7,5},{8,10},{9,11},{10,... | collective-permute-start | bytes 3145736 | tf_op jit(solution)/shard_map/ppermute | solution.py:332
  110.9 51.0 %collective-permute-start.4 = (bf16[1024,2048]{1,0:T(8,128)(2,1)}, bf16[1024,2048]{1,0:T(8,128)(2,1)}, u32[]{:S(2)}, u32[]{:S(2)}) collective-permute-start(bf16[1024,2048]{1,0:T(8,128)(2,1)} %pad_maximum_fusion.own_ref), channel_id=1, source_target_pairs={{0,4},{4,0},{8,12},{12,8},{16,20},{20,16},{24,28},{28,24},{1,5},{5... | collective-permute-start | bytes 12582920 | tf_op jit(solution)/shard_map/ppermute | solution.py:335
  128.6 44.6 %collective-permute-start.9 = (bf16[1024,2048]{1,0:T(8,128)(2,1)}, bf16[1024,2048]{1,0:T(8,128)(2,1)}, u32[]{:S(2)}, u32[]{:S(2)}) collective-permute-start(bf16[1024,2048]{1,0:T(8,128)(2,1)} %pad_maximum_fusion.1.own_ref), channel_id=1, source_target_pairs={{0,4},{4,0},{8,12},{12,8},{16,20},{20,16},{24,28},{28,24},{1,5},{5... | collective-permute-start | bytes 12582920 | tf_op jit(solution)/shard_map/ppermute | solution.py:335
  129.4 18.6 %all-to-all-start = ((f32[32,1,896]{2,1,0:T(1,128)}), f32[32,1,896]{2,1,0:T(1,128)S(1)}, u32[]{:S(2)}, u32[]{:S(2)}) async-start(f32[32,1,896]{2,1,0:T(1,128)} %broadcast_in_dim.102), calls=%async_computation | async-start | bytes 229376 | tf_op jit(solution)/shard_map/all_to_all | solution.py:470
  148.0 12.7 %all-to-all-start.2 = ((bf16[8,64,512]{2,1,0:T(8,128)(2,1)}), bf16[8,64,512]{2,1,0:T(8,128)(2,1)S(1)}, u32[]{:S(2)}, u32[]{:S(2)}) async-start(bf16[8,64,512]{2,1,0:T(8,128)(2,1)} %reshape.742), calls=%async_computation.2 | async-start | bytes 1048576 | tf_op jit(solution)/shard_map/all_to_all | solution.py:386
  151.5 147.6 %all-gather.8.cloned.1.call-start = ((), (), s32[]{:S(2)}) async-start(), calls=%async_computation.13 | async-start | bytes 5242880 | tf_op jit(solution)/shard_map/all_gather | solution.py:389
  152.5 20.7 %copy-start.40 = (f32[32,64]{1,0:T(8,128)}, f32[32,64]{1,0:T(8,128)S(1)}, u32[]{:S(2)}) copy-start(f32[32,64]{1,0:T(8,128)S(1)} %get-tuple-element.89) | copy-start | bytes 24580
  182.8 187.2 %reduce-scatter.5.cloned.1.call-start = ((), (), s32[]{:S(2)}) async-start(), calls=%async_computation.14 | async-start | bytes 5242880 | tf_op jit(solution)/shard_map/reduce_scatter | solution.py:392
  204.7 9.7 %copy-start.4 = (bf16[2048,512]{1,0:T(8,128)(2,1)}, bf16[2048,512]{1,0:T(8,128)(2,1)S(1)}, u32[]{:S(2)}) copy-start(bf16[2048,512]{1,0:T(8,128)(2,1)S(1)} %get-tuple-element.37.refs_1_) | copy-start | bytes 6291460
  225.6 192.3 %reduce-scatter.7.cloned.1.call-start = ((), (), s32[]{:S(2)}) async-start(), calls=%async_computation.15 | async-start | bytes 5242880 | tf_op jit(solution)/shard_map/reduce_scatter | solution.py:392
  235.3 14.5 %copy-start = (bf16[2048,768]{1,0:T(8,128)(2,1)}, bf16[2048,768]{1,0:T(8,128)(2,1)S(1)}, u32[]{:S(2)}) copy-start(bf16[2048,768]{1,0:T(8,128)(2,1)S(1)} %slice.156.in_ref.refs_3_) | copy-start | bytes 9437188
  305.4 15.4 %slice-start = ((s8[8388608]{0:T(1024)(128)(4,1)}), s8[4194304]{0:T(1024)(128)(4,1)S(1)}, s32[]{:S(2)}) async-start(s8[8388608]{0:T(1024)(128)(4,1)} %bitcast.232), calls=%async_computation.18 | async-start | bytes 8388608
  307.0 13.8 %slice-start.1 = ((s8[8388608]{0:T(1024)(128)(4,1)}), s8[4194304]{0:T(1024)(128)(4,1)S(1)}, s32[]{:S(2)}) async-start(s8[8388608]{0:T(1024)(128)(4,1)} %bitcast.232), calls=%async_computation.19 | async-start | bytes 8388608
  340.4 15.0 %copy-start.10 = (bf16[2048,512]{1,0:T(8,128)(2,1)S(1)}, bf16[2048,512]{1,0:T(8,128)(2,1)}, u32[]{:S(2)}) copy-start(bf16[2048,512]{1,0:T(8,128)(2,1)} %copy-done.8) | copy-start | bytes 6291460
  353.4 22.4 %collective-permute-start.10 = (bf16[1024,2048]{1,0:T(8,128)(2,1)}, bf16[1024,2048]{1,0:T(8,128)(2,1)}, u32[]{:S(2)}, u32[]{:S(2)}) collective-permute-start(bf16[1024,2048]{1,0:T(8,128)(2,1)} %shard_map.178), channel_id=1, source_target_pairs={{0,4},{4,0},{8,12},{12,8},{16,20},{20,16},{24,28},{28,24},{1,5},{5... | collective-permute-start | bytes 12582920 | tf_op jit(solution)/shard_map/ppermute | solution.py:335
  372.2 12.7 %all-to-all-start.3 = ((bf16[8,64,512]{2,1,0:T(8,128)(2,1)}), bf16[8,64,512]{2,1,0:T(8,128)(2,1)S(1)}, u32[]{:S(2)}, u32[]{:S(2)}) async-start(bf16[8,64,512]{2,1,0:T(8,128)(2,1)} %bitcast.64), calls=%async_computation.4 | async-start | bytes 1048576 | tf_op jit(solution)/shard_map/all_to_all | solution.py:386
  375.7 10.0 %copy-start.1 = (bf16[2048,256]{1,0:T(8,128)(2,1)S(1)}, bf16[2048,256]{1,0:T(8,128)(2,1)}, u32[]{:S(2)}) copy-start(bf16[2048,256]{1,0:T(8,128)(2,1)} %get-tuple-element.49.refs_0_) | copy-start | bytes 3145732
  375.7 10.0 %copy-start.3 = (bf16[256,2048]{1,0:T(8,128)(2,1)S(1)}, bf16[256,2048]{1,0:T(8,128)(2,1)}, u32[]{:S(2)}) copy-start(bf16[256,2048]{1,0:T(8,128)(2,1)} %all-gather.4.cloned.1.call-done.proj_ref.refs_3_) | copy-start | bytes 3145732
  375.7 103.3 %reduce-scatter.9.cloned.1.call-start = ((), (), s32[]{:S(2)}) async-start(), calls=%async_computation.16 | async-start | bytes 2621440 | tf_op jit(solution)/shard_map/reduce_scatter | solution.py:392
  387.3 10.8 %copy-start.16 = (bf16[1,256,2048]{2,1,0:T(8,128)(2,1)S(1)}, bf16[1,256,2048]{2,1,0:T(8,128)(2,1)}, u32[]{:S(2)}) copy-start(bf16[1,256,2048]{2,1,0:T(8,128)(2,1)} %param.11) | copy-start | bytes 3145732
  397.4 60.3 %collective-permute-start.11 = (bf16[1024,2048]{1,0:T(8,128)(2,1)}, bf16[1024,2048]{1,0:T(8,128)(2,1)}, u32[]{:S(2)}, u32[]{:S(2)}) collective-permute-start(bf16[1024,2048]{1,0:T(8,128)(2,1)} %shard_map.181), channel_id=1, source_target_pairs={{0,4},{4,0},{8,12},{12,8},{16,20},{20,16},{24,28},{28,24},{1,5},{5... | collective-permute-start | bytes 12582920 | tf_op jit(solution)/shard_map/ppermute | solution.py:335
  425.2 25.3 %collective-permute-start.18 = (bf16[2,256,1024]{2,1,0:T(8,128)(2,1)}, bf16[2,256,1024]{2,1,0:T(8,128)(2,1)}, u32[]{:S(2)}, u32[]{:S(2)}) collective-permute-start(bf16[2,256,1024]{2,1,0:T(8,128)(2,1)} %dynamic-slice_bitcast_fusion), channel_id=1, source_target_pairs={{0,2},{1,3},{2,0},{3,1},{4,6},{5,7},{6,4},{7,5},{8,10},{9,11},{10,... | collective-permute-start | bytes 3145736 | tf_op jit(solution)/shard_map/ppermute | solution.py:332
  429.9 25.9 %collective-permute-start.16 = (bf16[2,256,1024]{2,1,0:T(8,128)(2,1)}, bf16[2,256,1024]{2,1,0:T(8,128)(2,1)}, u32[]{:S(2)}, u32[]{:S(2)}) collective-permute-start(bf16[2,256,1024]{2,1,0:T(8,128)(2,1)} %dynamic-slice_bitcast_fusion.1), channel_id=1, source_target_pairs={{0,1},{1,0},{2,3},{3,2},{4,5},{5,4},{6,7},{7,6},{8,9},{9,8},{10,11... | collective-permute-start | bytes 3145736 | tf_op jit(solution)/shard_map/ppermute | solution.py:332
  436.1 14.4 %copy-start.22 = (bf16[2,2,256,1024]{3,2,1,0:T(8,128)(2,1)S(1)}, bf16[2,2,256,1024]{3,2,1,0:T(8,128)(2,1)}, u32[]{:S(2)}) copy-start(bf16[2,2,256,1024]{3,2,1,0:T(8,128)(2,1)} %copy-done.21) | copy-start | bytes 6291460
  446.1 9.8 %copy-start.19 = (bf16[2,2,256,1024]{3,2,1,0:T(8,128)(2,1)S(1)}, bf16[2,2,256,1024]{3,2,1,0:T(8,128)(2,1)}, u32[]{:S(2)}) copy-start(bf16[2,2,256,1024]{3,2,1,0:T(8,128)(2,1)} %get-tuple-element.61) | copy-start | bytes 6291460
  452.2 13.9 %collective-permute-start.19 = (bf16[256,1024]{1,0:T(8,128)(2,1)S(1)}, bf16[256,1024]{1,0:T(8,128)(2,1)S(1)}, u32[]{:S(2)}, u32[]{:S(2)}) collective-permute-start(bf16[256,1024]{1,0:T(8,128)(2,1)S(1)} %dynamic-slice_bitcast_fusion.4), channel_id=1, source_target_pairs={{0,1},{1,0},{2,3},{3,2},{4,5},{5,4},{6,7},{7,6},{8,9},{9,8},{10,11... | collective-permute-start | bytes 1572872 | tf_op jit(solution)/shard_map/ppermute | solution.py:332
  457.6 14.9 %collective-permute-start.17 = (bf16[256,1024]{1,0:T(8,128)(2,1)S(1)}, bf16[256,1024]{1,0:T(8,128)(2,1)S(1)}, u32[]{:S(2)}, u32[]{:S(2)}) collective-permute-start(bf16[256,1024]{1,0:T(8,128)(2,1)S(1)} %dynamic-slice_bitcast_fusion.5), channel_id=1, source_target_pairs={{0,2},{1,3},{2,0},{3,1},{4,6},{5,7},{6,4},{7,5},{8,10},{9,11},{10,... | collective-permute-start | bytes 1572872 | tf_op jit(solution)/shard_map/ppermute | solution.py:332
  463.5 29.1 %collective-permute-start.14 = (bf16[2,256,1024]{2,1,0:T(8,128)(2,1)}, bf16[2,256,1024]{2,1,0:T(8,128)(2,1)}, u32[]{:S(2)}, u32[]{:S(2)}) collective-permute-start(bf16[2,256,1024]{2,1,0:T(8,128)(2,1)} %dynamic-slice_bitcast_fusion.2), channel_id=1, source_target_pairs={{0,2},{1,3},{2,0},{3,1},{4,6},{5,7},{6,4},{7,5},{8,10},{9,11},{10,... | collective-permute-start | bytes 3145736 | tf_op jit(solution)/shard_map/ppermute | solution.py:332
  467.3 34.8 %collective-permute-start.12 = (bf16[2,256,1024]{2,1,0:T(8,128)(2,1)}, bf16[2,256,1024]{2,1,0:T(8,128)(2,1)}, u32[]{:S(2)}, u32[]{:S(2)}) collective-permute-start(bf16[2,256,1024]{2,1,0:T(8,128)(2,1)} %dynamic-slice_bitcast_fusion.3), channel_id=1, source_target_pairs={{0,1},{1,0},{2,3},{3,2},{4,5},{5,4},{6,7},{7,6},{8,9},{9,8},{10,11... | collective-permute-start | bytes 3145736 | tf_op jit(solution)/shard_map/ppermute | solution.py:332
  474.6 23.3 %all-to-all-start.4 = ((f32[32,1,640]{2,1,0:T(1,128)}), f32[32,1,640]{2,1,0:T(1,128)S(1)}, u32[]{:S(2)}, u32[]{:S(2)}) async-start(f32[32,1,640]{2,1,0:T(1,128)} %all_to_all.32), calls=%async_computation.5 | async-start | bytes 163840 | tf_op jit(solution)/shard_map/all_to_all | solution.py:611
  478.9 73.0 %reduce-scatter.11.cloned.1.call-start = ((), (), s32[]{:S(2)}) async-start(), calls=%async_computation.17 | async-start | bytes 2621440 | tf_op jit(solution)/shard_map/reduce_scatter | solution.py:392
  496.4 30.2 %collective-permute-start.15 = (bf16[256,1024]{1,0:T(8,128)(2,1)}, bf16[256,1024]{1,0:T(8,128)(2,1)}, u32[]{:S(2)}, u32[]{:S(2)}) collective-permute-start(bf16[256,1024]{1,0:T(8,128)(2,1)} %dynamic-slice_bitcast_fusion.6), channel_id=1, source_target_pairs={{0,1},{1,0},{2,3},{3,2},{4,5},{5,4},{6,7},{7,6},{8,9},{9,8},{10,11... | collective-permute-start | bytes 1572872 | tf_op jit(solution)/shard_map/ppermute | solution.py:332
  497.9 17.7 %all-to-all-start.5 = ((bf16[8,64,768]{2,1,0:T(8,128)(2,1)}), bf16[8,64,768]{2,1,0:T(8,128)(2,1)}, u32[]{:S(2)}, u32[]{:S(2)}) async-start(bf16[8,64,768]{2,1,0:T(8,128)(2,1)} %bitcast.250), calls=%async_computation.7 | async-start | bytes 1572864 | tf_op jit(solution)/shard_map/all_to_all | solution.py:386
  505.9 23.2 %collective-permute-start.13 = (bf16[256,1024]{1,0:T(8,128)(2,1)}, bf16[256,1024]{1,0:T(8,128)(2,1)}, u32[]{:S(2)}, u32[]{:S(2)}) collective-permute-start(bf16[256,1024]{1,0:T(8,128)(2,1)} %dynamic-slice_bitcast_fusion.7), channel_id=1, source_target_pairs={{0,2},{1,3},{2,0},{3,1},{4,6},{5,7},{6,4},{7,5},{8,10},{9,11},{10,... | collective-permute-start | bytes 1572872 | tf_op jit(solution)/shard_map/ppermute | solution.py:332
  531.3 13.6 %all-to-all-start.6 = ((bf16[8,64,512]{2,1,0:T(8,128)(2,1)}), bf16[8,64,512]{2,1,0:T(8,128)(2,1)}, u32[]{:S(2)}, u32[]{:S(2)}) async-start(bf16[8,64,512]{2,1,0:T(8,128)(2,1)} %bitcast.277), calls=%async_computation.9 | async-start | bytes 1048576 | tf_op jit(solution)/shard_map/all_to_all | solution.py:386
  (37 other events, 112.6 us)
Sparse Core Ops, SparseCore 0:
  9.6 30.6 all-gather.3
  45.4 134.7 all-gather.5
  182.9 77.8 all-gather.7
  263.0 75.2 reduce-scatter.4
  340.6 77.2 reduce-scatter.6
  427.7 43.4 reduce-scatter.8
  482.1 45.0 reduce-scatter.10
